TPU v7x, 256 devices: a whole 4x4x8 slice. The times are simulated.
256 devices in a mesh: wide: 64 (over y, z, core), narrow: 4 (over x).
Axes of the slice: x: 4, y: 4, z: 8, core: 2. Of those that a mesh axis runs over, the one named last changes fastest.
Arguments:
- acts: bfloat16 [1024, 8192], P(None, 'wide'), may hold values from -6 to 6
- grads: bfloat16 [1024, 28672], P('wide', 'narrow'), may hold values from -6 to 6
- act_basis: bfloat16 [8192, 8192], P('wide', 'narrow'), may hold values from -0.0625 to 0.0625
- grad_basis: bfloat16 [28672, 28672], P('narrow', 'wide'), may hold values from -0.03125 to 0.03125
Outputs:
- eigenvalues: float32 [28672, 8192], P('wide', 'narrow')
All inputs are finite; a program needn't handle non-finite values.
Results may differ from a plain program's by a relative error of at most 0.0027.
Values may be sent and summed in bfloat16 or wider, within the bound.
No kernel may reach another device: no remote copies, remote signals or barrier semaphores. Data moves between devices by JAX's collectives and lax.ppermute only.
A program may use at most 128 MiB of HBM per device.

v0:
```python
import jax
import jax.numpy as jnp
from jax import lax
from jax.sharding import PartitionSpec as P

EXAMPLES = 8
T_EX = 128


def body(acts, grads, act_basis, grad_basis):
    partial_grads = jnp.dot(
        lax.all_gather(grads, "wide", axis=0, tiled=True),
        grad_basis,
        preferred_element_type=jnp.float32,
    )
    rot_grads = lax.psum(partial_grads, "narrow").astype(jnp.bfloat16)
    act_terms = jnp.dot(acts, act_basis, preferred_element_type=jnp.float32)
    rot_acts = lax.psum(act_terms, "wide").astype(jnp.bfloat16)
    grads_ex = rot_grads.reshape(EXAMPLES, T_EX, rot_grads.shape[1])
    acts_ex = rot_acts.reshape(EXAMPLES, T_EX, rot_acts.shape[1])

    def accumulate(total, pair):
        rotated = jnp.dot(pair[0].T, pair[1], preferred_element_type=jnp.float32)
        return (total + rotated * rotated, None)

    start = jnp.zeros((rot_grads.shape[1], rot_acts.shape[1]), jnp.float32)
    total, unused = lax.scan(accumulate, start, (grads_ex, acts_ex))
    return total / (EXAMPLES * T_EX)


def solution(mesh):
    return jax.shard_map(
        body,
        mesh=mesh,
        in_specs=(P(None, "wide"), P("wide", "narrow"), P("wide", "narrow"), P("narrow", "wide")),
        out_specs=P("wide", "narrow"),
        check_vma=False,
    )
```

profile of v0, /device:TPU:2, one launch (start us, length us, event | category | flops | bytes accessed | tf_op | source)
XLA Modules:
  0.0 422.3 jit_solution(16768911146070813406)
XLA Ops:
  6.5 0.0 copy-start
  6.5 0.0 all-gather.2.cloned.1.call-start
  6.5 0.7 all-gather.2.cloned.1.call-update
  7.3 0.3 copy-done
  7.6 5.5 %fusion.6 = f32[1024,2048]{1,0:T(8,128)} fusion(bf16[1024,128]{1,0:T(8,128)(2,1)} %param.6, bf16[128,2048]{1,0:T(8,128)(2,1)S(1)} %copy-done), kind=kOutput, calls=%fused_computation.8 | convolution fusion | flops 536870912 | bytes 9175040 | tf_op jit(solution)/shard_map/dot_general | solution.py:17
  13.1 313.1 %all-reduce.3 = bf16[1024,2048]{1,0:T(8,128)(2,1)} all-reduce(f32[1024,2048]{1,0:T(8,128)} %fusion.6), channel_id=1, replica_groups=mesh['wide'=64,'narrow'=4] {'wide'}, use_global_device_ids=true, to_apply=%region_1.0 | all-reduce | flops 2097152 | bytes 12582912 | tf_op jit(solution)/shard_map/psum | solution.py:18
  326.1 0.0 all-gather.2.cloned.1.call-done
  326.1 11.9 %fusion.5 = f32[1024,448]{0,1:T(8,128)S(1)} fusion(bf16[1024,7168]{1,0:T(8,128)(2,1)} %all-gather.2.cloned.1.call-done, bf16[7168,448]{0,1:T(8,128)(2,1)} %param.9), kind=kOutput, calls=%fused_computation.7 | convolution fusion | flops 6576668672 | bytes 22937600 | tf_op jit(solution)/shard_map/dot_general | solution.py:11
  338.1 36.0 %all-reduce.2 = bf16[1024,448]{0,1:T(8,128)(2,1)S(1)} all-reduce(f32[1024,448]{0,1:T(8,128)S(1)} %fusion.5), channel_id=1, replica_groups=mesh['wide'=64,'narrow'=4] {'narrow'}, use_global_device_ids=true, to_apply=%region_0.0 | all-reduce | flops 458752 | bytes 2752512 | tf_op jit(solution)/shard_map/psum | solution.py:16
  374.1 0.5 copy.6
  374.6 36.5 %while.11 = (s32[]{:T(128)}, f32[448,2048]{1,0:T(8,128)}, bf16[8,128,448]{2,1,0:T(8,128)(2,1)S(1)}, bf16[8,128,2048]{2,1,0:T(8,128)(2,1)}, s32[]{:T(128)}, /*index=5*/s32[]{:T(128)}) while((s32[]{:T(128)}, f32[448,2048]{1,0:T(8,128)}, bf16[8,128,448]{2,1,0:T(8,128)(2,1)S(1)}, bf16[8,128,2048]{2,1,0:T(8,128)(2,1)}, s32[]{:T(128)}, ...), condition=%wide.region_3.4_spmd.clone, body=%wide.region_2.3_spmd.clone.sunk | while | flops 237633536 | bytes 7997014 | solution.py:27
  374.7 3.6 select_add_fusion.2
  378.2 4.7 %select_add_fusion.2 = f32[448,2048]{1,0:T(8,128)} fusion(f32[448,2048]{1,0:T(8,128)} %get-tuple-element.87, pred[]{:T(512)S(6)} %compare.3, bf16[8,128,2048]{2,1,0:T(8,128)(2,1)} %get-tuple-element.95, s32[]{:T(128)S(6)} %copy.11, bf16[8,128,448]{2,1,0:T(8,128)(2,1)S(1)} %get-tuple-element.94), kind=kOutput, calls=%fused_computation.clone.1 | convolution fusion | flops 237633536 | bytes 7996928 | tf_op jit(solution)/shard_map/while/body/eval_jaxpr/dot_general | solution.py:23
  382.9 4.7 %select_add_fusion.2 = f32[448,2048]{1,0:T(8,128)} fusion(f32[448,2048]{1,0:T(8,128)} %get-tuple-element.87, pred[]{:T(512)S(6)} %compare.3, bf16[8,128,2048]{2,1,0:T(8,128)(2,1)} %get-tuple-element.95, s32[]{:T(128)S(6)} %copy.11, bf16[8,128,448]{2,1,0:T(8,128)(2,1)S(1)} %get-tuple-element.94), kind=kOutput, calls=%fused_computation.clone.1 | convolution fusion | flops 237633536 | bytes 7996928 | tf_op jit(solution)/shard_map/while/body/eval_jaxpr/dot_general | solution.py:23
  387.6 4.7 %select_add_fusion.2 = f32[448,2048]{1,0:T(8,128)} fusion(f32[448,2048]{1,0:T(8,128)} %get-tuple-element.87, pred[]{:T(512)S(6)} %compare.3, bf16[8,128,2048]{2,1,0:T(8,128)(2,1)} %get-tuple-element.95, s32[]{:T(128)S(6)} %copy.11, bf16[8,128,448]{2,1,0:T(8,128)(2,1)S(1)} %get-tuple-element.94), kind=kOutput, calls=%fused_computation.clone.1 | convolution fusion | flops 237633536 | bytes 7996928 | tf_op jit(solution)/shard_map/while/body/eval_jaxpr/dot_general | solution.py:23
  392.3 4.7 %select_add_fusion.2 = f32[448,2048]{1,0:T(8,128)} fusion(f32[448,2048]{1,0:T(8,128)} %get-tuple-element.87, pred[]{:T(512)S(6)} %compare.3, bf16[8,128,2048]{2,1,0:T(8,128)(2,1)} %get-tuple-element.95, s32[]{:T(128)S(6)} %copy.11, bf16[8,128,448]{2,1,0:T(8,128)(2,1)S(1)} %get-tuple-element.94), kind=kOutput, calls=%fused_computation.clone.1 | convolution fusion | flops 237633536 | bytes 7996928 | tf_op jit(solution)/shard_map/while/body/eval_jaxpr/dot_general | solution.py:23
  397.0 4.7 %select_add_fusion.2 = f32[448,2048]{1,0:T(8,128)} fusion(f32[448,2048]{1,0:T(8,128)} %get-tuple-element.87, pred[]{:T(512)S(6)} %compare.3, bf16[8,128,2048]{2,1,0:T(8,128)(2,1)} %get-tuple-element.95, s32[]{:T(128)S(6)} %copy.11, bf16[8,128,448]{2,1,0:T(8,128)(2,1)S(1)} %get-tuple-element.94), kind=kOutput, calls=%fused_computation.clone.1 | convolution fusion | flops 237633536 | bytes 7996928 | tf_op jit(solution)/shard_map/while/body/eval_jaxpr/dot_general | solution.py:23
  401.8 4.7 %select_add_fusion.2 = f32[448,2048]{1,0:T(8,128)} fusion(f32[448,2048]{1,0:T(8,128)} %get-tuple-element.87, pred[]{:T(512)S(6)} %compare.3, bf16[8,128,2048]{2,1,0:T(8,128)(2,1)} %get-tuple-element.95, s32[]{:T(128)S(6)} %copy.11, bf16[8,128,448]{2,1,0:T(8,128)(2,1)S(1)} %get-tuple-element.94), kind=kOutput, calls=%fused_computation.clone.1 | convolution fusion | flops 237633536 | bytes 7996928 | tf_op jit(solution)/shard_map/while/body/eval_jaxpr/dot_general | solution.py:23
  406.5 4.7 %select_add_fusion.2 = f32[448,2048]{1,0:T(8,128)} fusion(f32[448,2048]{1,0:T(8,128)} %get-tuple-element.87, pred[]{:T(512)S(6)} %compare.3, bf16[8,128,2048]{2,1,0:T(8,128)(2,1)} %get-tuple-element.95, s32[]{:T(128)S(6)} %copy.11, bf16[8,128,448]{2,1,0:T(8,128)(2,1)S(1)} %get-tuple-element.94), kind=kOutput, calls=%fused_computation.clone.1 | convolution fusion | flops 237633536 | bytes 7996928 | tf_op jit(solution)/shard_map/while/body/eval_jaxpr/dot_general | solution.py:23
  411.2 4.3 %broadcast_multiply_fusion = f32[448,2048]{1,0:T(8,128)} fusion(f32[448,2048]{1,0:T(8,128)} %get-tuple-element.27), kind=kLoop, calls=%fused_computation.6 | loop fusion | flops 917504 | bytes 7340032 | tf_op jit(solution)/shard_map/div | solution.py:28
  (1 shorter events, 0.0 us)
Async XLA Ops:
  6.5 1.0 copy-start
  6.5 319.6 %all-gather.2.cloned.1.call-start = ((), (), s32[]{:S(2)}) async-start(), calls=%async_computation | async-start | bytes 14909440 | tf_op jit(solution)/shard_map/all_gather | solution.py:12
Sparse Core Ops, SparseCore 0:
  10.1 110.4 all-gather.1
where the time goes:
time: 423 us; the launch traced here: 422 us
  blocking collectives  349 us (83%)
  matrix products  53.9 us (13%)
  between operations  13.4 us (3%)
  other arithmetic  4.33 us (1%)
    psum x1, blocking collectives, body(): rot_acts = lax.psum(act_terms, 'wide').astype(jnp.bfloat16)  313 us
    dot_general x8, matrix products, accumulate(): rotated = jnp.dot(pair[0].T, pair[1], preferred_element_type=jnp.float32)  36.5 us
    psum x1, blocking collectives, body(): rot_grads = lax.psum(partial_grads, 'narrow').astype(jnp.bfloat16)  36 us
    dot_general x1, matrix products, body(): jnp.dot(lax.all_gather(grads, 'wide', axis=0, tiled=True), grad_basis, pr...  11.9 us
  transfers between devices with their start and end apart: 1, of which 0 were waited for; matrix products, arithmetic and copies ran while one was open for 1% of the time, Pallas kernels for 0%

commit v1 on v0

v1 whole, which is shorter than its diff:
```python
import jax
import jax.numpy as jnp
from jax import lax
from jax.experimental import pallas as pl
from jax.experimental.pallas import tpu as pltpu
from jax.sharding import Mesh, PartitionSpec as P

EXAMPLES = 8
T_EX = 128
NY, NZ, NC, NX = 4, 8, 2, 4
ROWS = 16
Y_STEPS = (0, -1, 1, 2)
BLOCKS = NY * NZ * NC
BF16, F32 = jnp.bfloat16, jnp.float32
SIZES = {"y": NY, "z": NZ, "core": NC, "x": NX}


def shift(v, axis, d):
    n = SIZES[axis]
    return lax.ppermute(v, axis, [(i, (i + d) % n) for i in range(n)])


def ring_z(v):
    up, down = [v], [v]
    for _ in range(4):
        up.append(shift(up[-1], "z", 1))
    for _ in range(3):
        down.append(shift(down[-1], "z", -1))
    return up + down[:0:-1]


def product_kernel(x_ref, b_ref, b_other_ref, o_ref, o_other_ref):
    k = pl.program_id(0)
    for b, o in ((b_ref, o_ref), (b_other_ref, o_other_ref)):
        r = lax.dot_general(x_ref[...], b[...], (((1,), (1,)), ((), ())), preferred_element_type=F32)

        @pl.when(k == 0)
        def _():
            o[...] = r

        @pl.when(k > 0)
        def _():
            o[...] += r


def product(x, b, b_other):
    rows, depth = x.shape
    cols = b.shape[0]
    step = depth // 7
    spec_b = pl.BlockSpec((cols, step), lambda k: (0, k))
    spec_o = pl.BlockSpec((rows, cols), lambda k: (0, 0))
    return pl.pallas_call(
        product_kernel,
        grid=(7,),
        in_specs=[pl.BlockSpec((rows, step), lambda k: (0, k)), spec_b, spec_b],
        out_specs=[spec_o, spec_o],
        out_shape=[jax.ShapeDtypeStruct((rows, cols), F32)] * 2,
        compiler_params=pltpu.CompilerParams(vmem_limit_bytes=24 * 2**20),
        cost_estimate=pl.CostEstimate(
            flops=4 * rows * cols * depth, bytes_accessed=2 * depth * (rows + 2 * cols) + 8 * rows * cols, transcendentals=0
        ),
    )(x, b, b_other)


def finish_kernel(table, g_ref, own_ref, other_ref, o_ref, rows, turned):
    @pl.when(pl.program_id(0) == 0)
    def _():
        for i in range(BLOCKS):
            at = pl.multiple_of(table[i] * ROWS, ROWS)
            rows[pl.ds(at, ROWS), :] = g_ref[i * ROWS : (i + 1) * ROWS, :]
        for e in range(EXAMPLES):
            turned[e] = rows[e * T_EX : (e + 1) * T_EX, :].T

    for i in range(EXAMPLES):
        ref = own_ref if i < NY else other_ref
        r = jnp.dot(turned[table[BLOCKS + i]], ref[i % NY, 0], preferred_element_type=F32)
        r = r * r
        if i > 0:
            r = r + o_ref[...]
        if i == EXAMPLES - 1:
            r = r * (1.0 / (EXAMPLES * T_EX))
        o_ref[...] = r


def finish(table, g_all, own, other):
    tokens, cols = g_all.shape
    n_blk = own.shape[3]
    spec_a = pl.BlockSpec((NY, 1, T_EX, n_blk), lambda j, t: (0, j, 0, 0))
    return pl.pallas_call(
        finish_kernel,
        grid_spec=pltpu.PrefetchScalarGridSpec(
            num_scalar_prefetch=1,
            grid=(NZ,),
            in_specs=[pl.BlockSpec((tokens, cols), lambda j, t: (0, 0)), spec_a, spec_a],
            out_specs=pl.BlockSpec((cols, n_blk), lambda j, t: (0, j)),
            scratch_shapes=[pltpu.VMEM((tokens, cols), BF16), pltpu.VMEM((EXAMPLES, cols, T_EX), BF16)],
        ),
        out_shape=jax.ShapeDtypeStruct((cols, NZ * n_blk), F32),
        compiler_params=pltpu.CompilerParams(vmem_limit_bytes=24 * 2**20),
        cost_estimate=pl.CostEstimate(
            flops=2 * tokens * cols * NZ * n_blk, bytes_accessed=4 * cols * NZ * n_blk + 4 * tokens * n_blk * NZ, transcendentals=0
        ),
    )(table, g_all, own, other)


def places(y, z, c, x):
    steps = jnp.array(Y_STEPS, jnp.int32)

    def place(block, core):
        return (((y + steps[block // NZ]) % NY) * NZ + (z - block % NZ) % NZ) * NC + core

    near = jnp.arange(3 * NZ, dtype=jnp.int32)
    near = jnp.concatenate([place(near, c), place(near, 1 - c)]).reshape(NX, -1)
    far = 3 * NZ + jnp.arange(NZ, dtype=jnp.int32)
    y_all = jnp.arange(NY, dtype=jnp.int32) * NC
    slots = (x - jnp.arange(NX, dtype=jnp.int32)) % NX
    return jnp.concatenate([near[slots].reshape(-1), place(far, c), place(far, 1 - c), y_all + c, y_all + 1 - c]).astype(jnp.int32)


def rotate_acts(acts, act_basis):
    gathered = lax.all_gather(acts, "z", axis=1, tiled=True)
    basis = lax.all_to_all(act_basis, "z", 1, 0, tiled=True)
    partial = jnp.dot(gathered, basis, preferred_element_type=F32)
    terms = lax.all_to_all(partial, ("y", "core"), 0, 0, tiled=True)
    piece = terms.reshape(NY * NC, T_EX, -1).sum(0).astype(BF16)
    own = lax.all_gather(piece, ("y", "z"), axis=0).reshape(NY, NZ, T_EX, -1)
    return own, shift(own, "core", 1)


def rotate_grads(grads, grad_basis, x):
    basis = grad_basis.T
    basis_other = shift(basis, "core", 1)
    load = jnp.concatenate(ring_z(grads), axis=0)
    h = load.shape[0] // 2
    below, above = shift(load, "y", 1), shift(load, "y", -1)
    far = jnp.concatenate([shift(below[:h], "y", 1), shift(above[h:], "y", -1)], axis=0)

    mine, theirs = product(jnp.concatenate([load, below, above], axis=0), basis, basis_other)
    partial = jnp.concatenate([mine, shift(theirs, "core", 1)], axis=0)
    partial = partial.reshape(NX, -1, partial.shape[1])
    total = lax.dynamic_index_in_dim(partial, x, 0, False)
    for d in (1, 2, -1):
        total = total + shift(lax.dynamic_index_in_dim(partial, (x + d) % NX, 0, False), "x", d)
    total = total.astype(BF16)
    out = [total, shift(total, "x", 1), shift(total, "x", 2), shift(total, "x", -1)]

    mine, theirs = product(far, basis, basis_other)
    partial = jnp.concatenate([mine, shift(theirs, "core", 1)], axis=0)
    out.append(lax.psum(partial, "x").astype(BF16))
    return jnp.concatenate(out, axis=0)


def body(acts, grads, act_basis, grad_basis):
    y, z, c, x = (lax.axis_index(a) for a in ("y", "z", "core", "x"))
    own, other = rotate_acts(acts, act_basis)
    g_all = rotate_grads(grads, grad_basis, x)
    return finish(places(y, z, c, x), g_all, own, other)


def solution(mesh):
    wide = ("y", "z", "core")
    return jax.shard_map(
        body,
        mesh=Mesh(mesh.devices.reshape(NY, NZ, NC, NX), wide + ("x",)),
        in_specs=(P(None, wide), P(wide, "x"), P(wide, "x"), P("x", wide)),
        out_specs=P(wide, "x"),
        check_vma=False,
    )
```

time: 423 us -> 270 us (0.64)
  blocking collectives: 349 us -> 24.7 us
  waiting for transfers between devices: 0.71 us -> 124 us
  matrix products: 53.9 us -> 3.29 us
  starting transfers between devices: 0.01 us -> 36.9 us
  Pallas kernels: 0 us -> 29.4 us
  local copies, waits for them, and re-layouts: 0.84 us -> 28.4 us
    psum x2 -> x1, blocking collectives: 349 us -> 24.7 us  [rotate_grads(): out.append(lax.psum(partial, 'x').astype(BF16))]
    ppermute x0 -> x21, waiting for transfers between devices: none -> 98.3 us  [shift(): return lax.ppermute(v, axis, [(i, (i + d) % n) for i in range(n)])]
    dot_general x10 -> x1, matrix products: 53.9 us -> 3.29 us  [rotate_acts(): partial = jnp.dot(gathered, basis, preferred_element_type=F32)]
    pallas_call x0 -> x3, Pallas kernels: none -> 29.4 us  [the longest x2 20 us: product(): pl.pallas_call(product_kernel, grid=(7,), in_specs=[pl.BlockSpec((rows, s...]
    ppermute x0 -> x21, starting transfers between devices: none -> 27 us  [shift(): return lax.ppermute(v, axis, [(i, (i + d) % n) for i in range(n)])]
    unnamed x3 -> x39, local copies, waits for them, and re-layouts: 0.84 us -> 16.5 us
    all_gather x1 -> x2, waiting for transfers between devices: 0.01 us -> 13.7 us  [the longest x1 6.89 us: rotate_acts(): gathered = lax.all_gather(acts, 'z', axis=1, tiled=True)]
    all_to_all x0 -> x2, waiting for transfers between devices: none -> 11.6 us  [the longest x1 11.6 us: rotate_acts(): terms = lax.all_to_all(partial, ('y', 'core'), 0, 0, tiled=True)]
  transfers between devices with their start and end apart: 1 -> 25, of which waited for: 0 -> 13; matrix products, arithmetic and copies ran while one was open for 1% -> 13% of each run, Pallas kernels for 0% -> 7%
where the time goes in v1:
time: 270 us; the launch traced here: 268 us
  waiting for transfers between devices  124 us (46%)
  starting transfers between devices  36.9 us (14%)
  Pallas kernels  29.4 us (11%)
  local copies, waits for them, and re-layouts  28.4 us (11%)
  blocking collectives  24.7 us (9%)
  between operations  13.7 us (5%)
  other arithmetic  7.51 us (3%)
  matrix products  3.29 us (1%)
    ppermute x21, waiting for transfers between devices, shift(): return lax.ppermute(v, axis, [(i, (i + d) % n) for i in range(n)])  98.3 us
    ppermute x21, starting transfers between devices, shift(): return lax.ppermute(v, axis, [(i, (i + d) % n) for i in range(n)])  27 us
    psum x1, blocking collectives, rotate_grads(): out.append(lax.psum(partial, 'x').astype(BF16))  24.7 us
    pallas_call x2, Pallas kernels, product(): pl.pallas_call(product_kernel, grid=(7,), in_specs=[pl.BlockSpec((rows, s...  20 us
    unnamed x39, local copies, waits for them, and re-layouts  16.5 us
    all_to_all x1, waiting for transfers between devices, rotate_acts(): terms = lax.all_to_all(partial, ('y', 'core'), 0, 0, tiled=True)  11.6 us
    pallas_call x1, Pallas kernels, finish(): pl.pallas_call(finish_kernel, grid_spec=pltpu.PrefetchScalarGridSpec(num_...  9.35 us
    all_gather x1, waiting for transfers between devices, rotate_acts(): gathered = lax.all_gather(acts, 'z', axis=1, tiled=True)  6.89 us
  transfers between devices with their start and end apart: 25, of which 13 were waited for; matrix products, arithmetic and copies ran while one was open for 13% of the time, Pallas kernels for 7%

profile of v1, /device:TPU:2, one launch (start us, length us, event | category | flops | bytes accessed | tf_op | source)
XLA Modules:
  0.0 267.6 jit_solution(7895927817093946654)
XLA Ops:
  6.5 1.9 collective-permute-start
  8.5 3.9 %collective-permute-start.4 = (bf16[16,7168]{1,0:T(8,128)(2,1)}, bf16[16,7168]{1,0:T(8,128)(2,1)S(1)}, u32[]{:S(2)}, u32[]{:S(2)}) collective-permute-start(bf16[16,7168]{1,0:T(8,128)(2,1)} %param.6), channel_id=1, source_target_pairs={{0,56},{8,0},{16,8},{24,16},{32,24},{40,32},{48,40},{56,48},{1,57}... | collective-permute-start | bytes 688136 | tf_op jit(solution)/shard_map/ppermute | solution.py:20
  12.4 1.9 copy.13
  14.3 5.8 %all-to-all-start = ((bf16[128,8,256]{2,0,1:T(8,128)(2,1)}), bf16[128,8,256]{2,0,1:T(8,128)(2,1)S(1)}, u32[]{:S(2)}, u32[]{:S(2)}) async-start(bf16[128,8,256]{2,0,1:T(8,128)(2,1)} %bitcast.33), calls=%async_computation | async-start | bytes 1048576 | tf_op jit(solution)/shard_map/all_to_all | solution.py:122
  20.9 2.0 collective-permute-start.1
  22.9 1.3 collective-permute-start.5
  24.9 21.2 %collective-permute-done.1 = bf16[16,7168]{1,0:T(8,128)(2,1)S(1)} collective-permute-done((bf16[16,7168]{1,0:T(8,128)(2,1)S(1)}, bf16[16,7168]{1,0:T(8,128)(2,1)S(1)}, u32[]{:S(2)}, u32[]{:S(2)}) %collective-permute-start.1) | collective-permute-done | bytes 229408 | tf_op jit(solution)/shard_map/ppermute | solution.py:20
  46.2 3.2 %collective-permute-start.6 = (bf16[16,7168]{1,0:T(8,128)(2,1)S(1)}, bf16[16,7168]{1,0:T(8,128)(2,1)S(1)}, u32[]{:S(2)}, u32[]{:S(2)}) collective-permute-start(bf16[16,7168]{1,0:T(8,128)(2,1)S(1)} %collective-permute-done.5), channel_id=1, source_target_pairs={{0,56},{8,0},{16,8},{24,16},{32,24},{40,32},{48,40},{56,48},{1,57}... | collective-permute-start | bytes 688136 | tf_op jit(solution)/shard_map/ppermute | solution.py:20
  50.1 7.9 %collective-permute-done.2 = bf16[16,7168]{1,0:T(8,128)(2,1)S(1)} collective-permute-done((bf16[16,7168]{1,0:T(8,128)(2,1)S(1)}, bf16[16,7168]{1,0:T(8,128)(2,1)S(1)}, u32[]{:S(2)}, u32[]{:S(2)}) %collective-permute-start.2) | collective-permute-done | bytes 229408 | tf_op jit(solution)/shard_map/ppermute | solution.py:20
  58.7 9.3 %collective-permute-done.3 = bf16[16,7168]{1,0:T(8,128)(2,1)S(1)} collective-permute-done((bf16[16,7168]{1,0:T(8,128)(2,1)S(1)}, bf16[16,7168]{1,0:T(8,128)(2,1)S(1)}, u32[]{:S(2)}, u32[]{:S(2)}) %collective-permute-start.3) | collective-permute-done | bytes 229408 | tf_op jit(solution)/shard_map/ppermute | solution.py:20
  68.0 0.8 constant_dynamic-update-slice_fusion.3
  68.8 6.9 %all-gather.4.cloned.1.call-done = bf16[1024,1024]{1,0:T(8,128)(2,1)} async-done(((bf16[1024,128]{1,0:T(8,128)(2,1)}), bf16[1024,1024]{1,0:T(8,128)(2,1)}) %all-gather.4.cloned.1.call-update) | async-done | bytes 2097168 | tf_op jit(solution)/shard_map/all_gather | solution.py:121
  75.6 3.3 %fusion.26 = f32[8,128,256]{2,1,0:T(8,128)} fusion(bf16[8,128,1024]{2,1,0:T(8,128)(2,1)} %bitcast.43, bf16[1024,256,1]{1,0,2:T(8,128)(2,1)S(1)} %bitcast.44), kind=kOutput, calls=%fused_computation.100 | convolution fusion | flops 536870912 | bytes 3670016 | tf_op jit(solution)/shard_map/dot_general | solution.py:123
  78.9 4.0 %all-to-all-start.1 = ((f32[8,128,256]{2,1,0:T(8,128)}), f32[8,128,256]{2,1,0:T(8,128)S(1)}, u32[]{:S(2)}, u32[]{:S(2)}) async-start(f32[8,128,256]{2,1,0:T(8,128)} %fusion.26), calls=%async_computation.1 | async-start | bytes 2097152 | tf_op jit(solution)/shard_map/all_to_all | solution.py:124
  83.6 1.9 constant_dynamic-update-slice_fusion.2
  85.5 1.7 constant_dynamic-update-slice_fusion.1
  87.3 11.6 %all-to-all-done.1 = f32[8,128,256]{2,1,0:T(8,128)S(1)} async-done(((f32[8,128,256]{2,1,0:T(8,128)}), f32[8,128,256]{2,1,0:T(8,128)S(1)}, u32[]{:S(2)}, u32[]{:S(2)}) %all-to-all-start.1) | async-done | bytes 1048608 | tf_op jit(solution)/shard_map/all_to_all | solution.py:124
  99.6 0.8 constant_dynamic-update-slice_fusion
  100.4 1.2 collective-permute-start.8
  101.6 0.9 collective-permute-start.7
  105.0 38.3 %collective-permute-done.8 = bf16[128,7168]{1,0:T(8,128)(2,1)} collective-permute-done((bf16[128,7168]{1,0:T(8,128)(2,1)}, bf16[128,7168]{1,0:T(8,128)(2,1)}, u32[]{:S(2)}, u32[]{:S(2)}) %collective-permute-start.8) | collective-permute-done | bytes 1835040 | tf_op jit(solution)/shard_map/ppermute | solution.py:20
  143.3 2.2 slice.18
  145.5 2.4 collective-permute-start.18
  147.9 2.2 slice.17
  150.0 2.9 %constant_dynamic-update-slice_fusion.9 = bf16[384,7168]{1,0:T(8,128)(2,1)} fusion(bf16[384,7168]{1,0:T(8,128)(2,1)} %get-tuple-element.23, bf16[128,7168]{1,0:T(8,128)(2,1)} %collective-permute-done.7), kind=kLoop, calls=%fused_computation.23 | loop fusion | bytes 3670016
  152.9 2.9 %constant_dynamic-update-slice_fusion.8.x_ref = bf16[384,7168]{1,0:T(8,128)(2,1)} fusion(bf16[384,7168]{1,0:T(8,128)(2,1)} %constant_dynamic-update-slice_fusion.9, bf16[128,7168]{1,0:T(8,128)(2,1)} %collective-permute-done.8), kind=kLoop, calls=%fused_computation.22 | loop fusion | bytes 3670016 | tf_op jit(solution)/shard_map/concatenate | solution.py:138
  155.8 11.2 %shard_map.55 = (f32[384,448]{1,0:T(8,128)S(1)}, f32[384,448]{1,0:T(8,128)S(1)}) custom-call(bf16[384,7168]{1,0:T(8,128)(2,1)} %constant_dynamic-update-slice_fusion.8.x_ref, bf16[448,7168]{1,0:T(8,128)(2,1)S(1)} %bitcast.37, bf16[448,7168]{1,0:T(8,128)(2,1)} %collective-permute-done.9.b_other_ref), custom_call_target="tpu_custom_call" | custom-call | flops 4932501504 | bytes 19726336 | tf_op jit(solution)/shard_map/pallas_call | solution.py:52
  167.1 0.9 copy-done.2
  168.3 6.8 %all-gather.6.cloned.1.call-done = bf16[4096,256]{1,0:T(8,128)(2,1)} async-done(((bf16[128,256]{1,0:T(8,128)(2,1)}), bf16[4096,256]{1,0:T(8,128)(2,1)}) %all-gather.6.cloned.1.call-update) | async-done | bytes 2097168 | tf_op jit(solution)/shard_map/all_gather | solution.py:126
  175.2 2.7 collective-permute-done.17
  177.9 1.6 pad_maximum_fusion.x_ref
  179.5 2.8 %copy-done = bf16[7168,448]{0,1:T(8,128)(2,1)S(1)} copy-done((bf16[7168,448]{0,1:T(8,128)(2,1)S(1)}, bf16[7168,448]{0,1:T(8,128)(2,1)}, u32[]{:S(2)}) %copy-start) | copy-done | bytes 6422552
  182.3 8.8 %shard_map.56 = (f32[128,448]{1,0:T(8,128)S(1)}, f32[128,448]{1,0:T(8,128)S(1)}) custom-call(bf16[128,7168]{1,0:T(8,128)(2,1)S(1)} %pad_maximum_fusion.x_ref, bf16[448,7168]{1,0:T(8,128)(2,1)S(1)} %bitcast.38, bf16[448,7168]{1,0:T(8,128)(2,1)} %collective-permute-done.9.b_other_ref), custom_call_target="tpu_custom_call" | custom-call | flops 1644167168 | bytes 15138816 | tf_op jit(solution)/shard_map/pallas_call | solution.py:52
  191.8 0.8 collective-permute-start.13
  192.6 2.2 collective-permute-start.12
  194.8 1.8 collective-permute-start.11
  196.7 1.8 pad_maximum_fusion.2
  198.5 5.0 %collective-permute-done.13 = f32[192,448]{1,0:T(8,128)} collective-permute-done((f32[192,448]{1,0:T(8,128)S(1)}, f32[192,448]{1,0:T(8,128)}, u32[]{:S(2)}, u32[]{:S(2)}) %collective-permute-start.13) | collective-permute-done | bytes 344096 | tf_op jit(solution)/shard_map/ppermute | solution.py:20
  203.4 9.4 %collective-permute-done.12 = f32[192,448]{1,0:T(8,128)} collective-permute-done((f32[192,448]{1,0:T(8,128)S(1)}, f32[192,448]{1,0:T(8,128)}, u32[]{:S(2)}, u32[]{:S(2)}) %collective-permute-start.12) | collective-permute-done | bytes 344096 | tf_op jit(solution)/shard_map/ppermute | solution.py:20
  212.8 0.9 collective-permute-done.11
  213.7 2.2 constant_dynamic-update-slice_fusion.21
  215.9 1.4 collective-permute-start.14
  217.3 3.3 %collective-permute-start.15 = (bf16[192,448]{1,0:T(8,128)(2,1)}, bf16[192,448]{1,0:T(8,128)(2,1)}, u32[]{:S(2)}, u32[]{:S(2)}) collective-permute-start(bf16[192,448]{1,0:T(8,128)(2,1)} %get-tuple-element.14), channel_id=1, source_target_pairs={{0,2},{1,3},{2,0},{3,1},{4,6},{5,7},{6,4},{7,5},{8,10},{9,11},{10,... | collective-permute-start | bytes 516104 | tf_op jit(solution)/shard_map/ppermute | solution.py:20
  220.6 24.7 %all-reduce.1 = bf16[256,448]{1,0:T(8,128)(2,1)S(1)} all-reduce(f32[256,448]{1,0:T(8,128)} %pad_maximum_fusion.2), channel_id=1, replica_groups=mesh['y'=4,'z'=8,'core'=2,'x'=4] {'x'}, use_global_device_ids=true, to_apply=%region_0.0 | all-reduce | flops 114688 | bytes 688128 | tf_op jit(solution)/shard_map/psum | solution.py:149
  245.8 0.9 constant_dynamic-update-slice_fusion.20
  246.7 0.9 constant_dynamic-update-slice_fusion.19
  247.7 3.6 %collective-permute-done.16 = bf16[192,448]{1,0:T(8,128)(2,1)S(1)} collective-permute-done((bf16[192,448]{1,0:T(8,128)(2,1)}, bf16[192,448]{1,0:T(8,128)(2,1)S(1)}, u32[]{:S(2)}, u32[]{:S(2)}) %collective-permute-start.16) | collective-permute-done | bytes 172064 | tf_op jit(solution)/shard_map/ppermute | solution.py:20
  251.4 9.4 %shard_map.57 = f32[448,2048]{1,0:T(8,128)} custom-call(s32[72]{0:T(128)S(1)} %concatenate.27.table, bf16[1024,448]{1,0:T(8,128)(2,1)S(1)} %convert_dynamic-update-slice_fusion.g_ref, bf16[4,8,128,256]{3,2,1,0:T(8,128)(2,1)S(1)} %bitcast.40, bf16[4,8,128,256]{3,2,1,0:T(8,128)(2,1)} %collective-permute-done.20.other_ref), custom_call_target="tpu_custom_call" | custom-call | flops 1879048192 | bytes 12058624 | tf_op jit(solution)/shard_map/pallas_call | solution.py:89
  (78 shorter events, 8.5 us)
Async XLA Ops:
  6.5 13.6 %copy-start.6 = (bf16[16,7168]{1,0:T(8,128)(2,1)S(1)}, bf16[16,7168]{1,0:T(8,128)(2,1)}, u32[]{:S(2)}) copy-start(bf16[16,7168]{1,0:T(8,128)(2,1)} %param.6) | copy-start | bytes 688132
  6.5 69.1 %all-gather.4.cloned.1.call-start = ((), (), s32[]{:S(2)}) async-start(), calls=%async_computation.2 | async-start | bytes 2359296 | tf_op jit(solution)/shard_map/all_gather | solution.py:121
  6.5 14.3 %collective-permute-start = (bf16[16,7168]{1,0:T(8,128)(2,1)}, bf16[16,7168]{1,0:T(8,128)(2,1)S(1)}, u32[]{:S(2)}, u32[]{:S(2)}) collective-permute-start(bf16[16,7168]{1,0:T(8,128)(2,1)} %param.6), channel_id=1, source_target_pairs={{0,8},{8,16},{16,24},{24,32},{32,40},{40,48},{48,56},{56,0},{1,9},... | collective-permute-start | bytes 688136 | tf_op jit(solution)/shard_map/ppermute | solution.py:20
  8.5 14.5 %collective-permute-start.4 = (bf16[16,7168]{1,0:T(8,128)(2,1)}, bf16[16,7168]{1,0:T(8,128)(2,1)S(1)}, u32[]{:S(2)}, u32[]{:S(2)}) collective-permute-start(bf16[16,7168]{1,0:T(8,128)(2,1)} %param.6), channel_id=1, source_target_pairs={{0,56},{8,0},{16,8},{24,16},{32,24},{40,32},{48,40},{56,48},{1,57}... | collective-permute-start | bytes 688136 | tf_op jit(solution)/shard_map/ppermute | solution.py:20
  12.4 143.4 %collective-permute-start.9 = (bf16[448,7168]{1,0:T(8,128)(2,1)}, bf16[448,7168]{1,0:T(8,128)(2,1)}, u32[]{:S(2)}, u32[]{:S(2)}) collective-permute-start(bf16[448,7168]{1,0:T(8,128)(2,1)} %bitcast.34), channel_id=1, source_target_pairs={{0,4},{4,0},{1,5},{5,1},{2,6},{6,2},{3,7},{7,3},{8,12},{12,8},{9,1... | collective-permute-start | bytes 19267592 | tf_op jit(solution)/shard_map/ppermute | solution.py:20
  14.3 54.5 %all-to-all-start = ((bf16[128,8,256]{2,0,1:T(8,128)(2,1)}), bf16[128,8,256]{2,0,1:T(8,128)(2,1)S(1)}, u32[]{:S(2)}, u32[]{:S(2)}) async-start(bf16[128,8,256]{2,0,1:T(8,128)(2,1)} %bitcast.33), calls=%async_computation | async-start | bytes 1048576 | tf_op jit(solution)/shard_map/all_to_all | solution.py:122
  20.9 25.3 %collective-permute-start.1 = (bf16[16,7168]{1,0:T(8,128)(2,1)S(1)}, bf16[16,7168]{1,0:T(8,128)(2,1)S(1)}, u32[]{:S(2)}, u32[]{:S(2)}) collective-permute-start(bf16[16,7168]{1,0:T(8,128)(2,1)S(1)} %collective-permute-done), channel_id=1, source_target_pairs={{0,8},{8,16},{16,24},{24,32},{32,40},{40,48},{48,56},{56,0},{1,9},... | collective-permute-start | bytes 688136 | tf_op jit(solution)/shard_map/ppermute | solution.py:20
  22.9 23.2 %collective-permute-start.5 = (bf16[16,7168]{1,0:T(8,128)(2,1)S(1)}, bf16[16,7168]{1,0:T(8,128)(2,1)S(1)}, u32[]{:S(2)}, u32[]{:S(2)}) collective-permute-start(bf16[16,7168]{1,0:T(8,128)(2,1)S(1)} %collective-permute-done.4), channel_id=1, source_target_pairs={{0,56},{8,0},{16,8},{24,16},{32,24},{40,32},{48,40},{56,48},{1,57}... | collective-permute-start | bytes 688136 | tf_op jit(solution)/shard_map/ppermute | solution.py:20
  46.2 11.8 %collective-permute-start.2 = (bf16[16,7168]{1,0:T(8,128)(2,1)S(1)}, bf16[16,7168]{1,0:T(8,128)(2,1)S(1)}, u32[]{:S(2)}, u32[]{:S(2)}) collective-permute-start(bf16[16,7168]{1,0:T(8,128)(2,1)S(1)} %collective-permute-done.1), channel_id=1, source_target_pairs={{0,8},{8,16},{16,24},{24,32},{32,40},{40,48},{48,56},{56,0},{1,9},... | collective-permute-start | bytes 688136 | tf_op jit(solution)/shard_map/ppermute | solution.py:20
  46.2 36.8 %copy-start.7 = (bf16[16,7168]{1,0:T(8,128)(2,1)}, bf16[16,7168]{1,0:T(8,128)(2,1)S(1)}, u32[]{:S(2)}) copy-start(bf16[16,7168]{1,0:T(8,128)(2,1)S(1)} %collective-permute-done.5) | copy-start | bytes 688132
  46.2 36.8 %collective-permute-start.6 = (bf16[16,7168]{1,0:T(8,128)(2,1)S(1)}, bf16[16,7168]{1,0:T(8,128)(2,1)S(1)}, u32[]{:S(2)}, u32[]{:S(2)}) collective-permute-start(bf16[16,7168]{1,0:T(8,128)(2,1)S(1)} %collective-permute-done.5), channel_id=1, source_target_pairs={{0,56},{8,0},{16,8},{24,16},{32,24},{40,32},{48,40},{56,48},{1,57}... | collective-permute-start | bytes 688136 | tf_op jit(solution)/shard_map/ppermute | solution.py:20
  58.0 10.0 %collective-permute-start.3 = (bf16[16,7168]{1,0:T(8,128)(2,1)S(1)}, bf16[16,7168]{1,0:T(8,128)(2,1)S(1)}, u32[]{:S(2)}, u32[]{:S(2)}) collective-permute-start(bf16[16,7168]{1,0:T(8,128)(2,1)S(1)} %collective-permute-done.2), channel_id=1, source_target_pairs={{0,8},{8,16},{16,24},{24,32},{32,40},{40,48},{48,56},{56,0},{1,9},... | collective-permute-start | bytes 688136 | tf_op jit(solution)/shard_map/ppermute | solution.py:20
  68.7 10.2 %copy-start.9 = (bf16[128,7168]{1,0:T(8,128)(2,1)}, bf16[128,7168]{1,0:T(8,128)(2,1)S(1)}, u32[]{:S(2)}) copy-start(bf16[128,7168]{1,0:T(8,128)(2,1)S(1)} %get-tuple-element.28) | copy-start | bytes 5505028
  78.9 19.9 %all-to-all-start.1 = ((f32[8,128,256]{2,1,0:T(8,128)}), f32[8,128,256]{2,1,0:T(8,128)S(1)}, u32[]{:S(2)}, u32[]{:S(2)}) async-start(f32[8,128,256]{2,1,0:T(8,128)} %fusion.26), calls=%async_computation.1 | async-start | bytes 2097152 | tf_op jit(solution)/shard_map/all_to_all | solution.py:124
  82.9 20.4 %copy-start.4 = (s32[4]{0:T(128)S(1)}, s32[4]{0:T(128)}, u32[]{:S(2)}) copy-start(s32[4]{0:T(128)} %constant.168.clone) | copy-start | bytes 52
  82.9 92.3 %all-gather.6.cloned.1.call-start = ((), (), s32[]{:S(2)}) async-start(), calls=%async_computation.3 | async-start | bytes 2162688 | tf_op jit(solution)/shard_map/all_gather | solution.py:126
  83.0 0.7 copy-start.8
  83.6 72.2 %slice-start = ((s8[6422528]{0:T(1024)(128)(4,1)}), s8[2228224]{0:T(1024)(128)(4,1)S(1)}, s32[]{:S(2)}) async-start(s8[6422528]{0:T(1024)(128)(4,1)} %bitcast.35), calls=%async_computation.4 | async-start | bytes 4456448
  100.4 42.9 %collective-permute-start.8 = (bf16[128,7168]{1,0:T(8,128)(2,1)}, bf16[128,7168]{1,0:T(8,128)(2,1)}, u32[]{:S(2)}, u32[]{:S(2)}) collective-permute-start(bf16[128,7168]{1,0:T(8,128)(2,1)} %get-tuple-element.22), channel_id=1, source_target_pairs={{0,192},{64,0},{128,64},{192,128},{1,193},{65,1},{129,65},{193,129... | collective-permute-start | bytes 5505032 | tf_op jit(solution)/shard_map/ppermute | solution.py:20
  101.6 46.3 %collective-permute-start.7 = (bf16[128,7168]{1,0:T(8,128)(2,1)}, bf16[128,7168]{1,0:T(8,128)(2,1)}, u32[]{:S(2)}, u32[]{:S(2)}) collective-permute-start(bf16[128,7168]{1,0:T(8,128)(2,1)} %get-tuple-element.22), channel_id=1, source_target_pairs={{0,64},{64,128},{128,192},{192,0},{1,65},{65,129},{129,193},{193,1... | collective-permute-start | bytes 5505032 | tf_op jit(solution)/shard_map/ppermute | solution.py:20
  145.5 10.3 %slice-start.1 = ((s8[6422528]{0:T(1024)(128)(4,1)}), s8[4194304]{0:T(1024)(128)(4,1)S(1)}, s32[]{:S(2)}) async-start(s8[6422528]{0:T(1024)(128)(4,1)} %bitcast.35), calls=%async_computation.5 | async-start | bytes 8388608
  145.5 29.7 %collective-permute-start.18 = (bf16[64,7168]{1,0:T(8,128)(2,1)}, bf16[64,7168]{1,0:T(8,128)(2,1)}, u32[]{:S(2)}, u32[]{:S(2)}) collective-permute-start(bf16[64,7168]{1,0:T(8,128)(2,1)} %slice.18), channel_id=1, source_target_pairs={{0,192},{64,0},{128,64},{192,128},{1,193},{65,1},{129,65},{193,129... | collective-permute-start | bytes 2752520 | tf_op jit(solution)/shard_map/ppermute | solution.py:20
  150.0 27.9 %collective-permute-start.17 = (bf16[64,7168]{1,0:T(8,128)(2,1)}, bf16[64,7168]{1,0:T(8,128)(2,1)}, u32[]{:S(2)}, u32[]{:S(2)}) collective-permute-start(bf16[64,7168]{1,0:T(8,128)(2,1)} %slice.17), channel_id=1, source_target_pairs={{0,64},{64,128},{128,192},{192,0},{1,65},{65,129},{129,193},{193,1... | collective-permute-start | bytes 2752520 | tf_op jit(solution)/shard_map/ppermute | solution.py:20
  167.1 0.9 copy-start.2
  168.2 23.0 %collective-permute-start.10 = (f32[384,448]{0,1:T(8,128)S(1)}, f32[384,448]{0,1:T(8,128)S(1)}, u32[]{:S(2)}, u32[]{:S(2)}) collective-permute-start(f32[384,448]{0,1:T(8,128)S(1)} %copy.8), channel_id=1, source_target_pairs={{0,4},{4,0},{1,5},{5,1},{2,6},{6,2},{3,7},{7,3},{8,12},{12,8},{9,1... | collective-permute-start | bytes 2064392 | tf_op jit(solution)/shard_map/ppermute | solution.py:20
  175.2 76.2 %collective-permute-start.20 = (bf16[4,8,128,256]{3,2,1,0:T(8,128)(2,1)}, bf16[4,8,128,256]{3,2,1,0:T(8,128)(2,1)}, u32[]{:S(2)}, u32[]{:S(2)}) collective-permute-start(bf16[4,8,128,256]{3,2,1,0:T(8,128)(2,1)} %bitcast.39), channel_id=1, source_target_pairs={{0,4},{4,0},{1,5},{5,1},{2,6},{6,2},{3,7},{7,3},{8,12},{12,8},{9,1... | collective-permute-start | bytes 6291464 | tf_op jit(solution)/shard_map/ppermute | solution.py:20
  179.5 2.8 %copy-start = (bf16[7168,448]{0,1:T(8,128)(2,1)S(1)}, bf16[7168,448]{0,1:T(8,128)(2,1)}, u32[]{:S(2)}) copy-start(bf16[7168,448]{0,1:T(8,128)(2,1)} %param.8) | copy-start | bytes 19267588
  182.3 9.2 %copy-start.3 = (f32[384,448]{1,0:T(8,128)S(1)}, f32[384,448]{1,0:T(8,128)}, u32[]{:S(2)}) copy-start(f32[384,448]{1,0:T(8,128)} %copy-done.2) | copy-start | bytes 2064388
  191.1 5.6 %collective-permute-start.19 = (f32[128,448]{1,0:T(8,128)S(1)}, f32[128,448]{1,0:T(8,128)}, u32[]{:S(2)}, u32[]{:S(2)}) collective-permute-start(f32[128,448]{1,0:T(8,128)S(1)} %get-tuple-element.12), channel_id=1, source_target_pairs={{0,4},{4,0},{1,5},{5,1},{2,6},{6,2},{3,7},{7,3},{8,12},{12,8},{9,1... | collective-permute-start | bytes 688136 | tf_op jit(solution)/shard_map/ppermute | solution.py:20
  191.5 5.1 %copy-start.11 = (s32[8]{0:T(128)S(1)}, s32[8]{0:T(128)}, u32[]{:S(2)}) copy-start(s32[8]{0:T(128)} %get-tuple-element.16) | copy-start | bytes 100
  191.5 5.1 %copy-start.10 = (s32[4]{0:T(128)S(1)}, s32[4]{0:T(128)}, u32[]{:S(2)}) copy-start(s32[4]{0:T(128)} %get-tuple-element.39) | copy-start | bytes 52
  191.6 5.0 %copy-start.5 = (f32[768,448]{1,0:T(8,128)}, f32[768,448]{1,0:T(8,128)S(1)}, u32[]{:S(2)}) copy-start(f32[768,448]{1,0:T(8,128)S(1)} %pad_maximum_fusion.1) | copy-start | bytes 4128772
  191.8 11.7 %collective-permute-start.13 = (f32[192,448]{1,0:T(8,128)S(1)}, f32[192,448]{1,0:T(8,128)}, u32[]{:S(2)}, u32[]{:S(2)}) collective-permute-start(f32[192,448]{1,0:T(8,128)S(1)} %get-tuple-element.20), channel_id=1, source_target_pairs={{0,3},{1,0},{2,1},{3,2},{4,7},{5,4},{6,5},{7,6},{8,11},{9,8},{10,9... | collective-permute-start | bytes 1032200 | tf_op jit(solution)/shard_map/ppermute | solution.py:20
  192.6 20.2 %collective-permute-start.12 = (f32[192,448]{1,0:T(8,128)S(1)}, f32[192,448]{1,0:T(8,128)}, u32[]{:S(2)}, u32[]{:S(2)}) collective-permute-start(f32[192,448]{1,0:T(8,128)S(1)} %get-tuple-element.21), channel_id=1, source_target_pairs={{0,2},{1,3},{2,0},{3,1},{4,6},{5,7},{6,4},{7,5},{8,10},{9,11},{10,... | collective-permute-start | bytes 1032200 | tf_op jit(solution)/shard_map/ppermute | solution.py:20
  194.8 18.9 %collective-permute-start.11 = (f32[192,448]{1,0:T(8,128)S(1)}, f32[192,448]{1,0:T(8,128)}, u32[]{:S(2)}, u32[]{:S(2)}) collective-permute-start(f32[192,448]{1,0:T(8,128)S(1)} %get-tuple-element.19), channel_id=1, source_target_pairs={{0,1},{1,2},{2,3},{3,0},{4,5},{5,6},{6,7},{7,4},{8,9},{9,10},{10,1... | collective-permute-start | bytes 1032200 | tf_op jit(solution)/shard_map/ppermute | solution.py:20
  198.5 52.9 %copy-start.1 = (bf16[4096,256]{1,0:T(8,128)(2,1)S(1)}, bf16[4096,256]{1,0:T(8,128)(2,1)}, u32[]{:S(2)}) copy-start(bf16[4096,256]{1,0:T(8,128)(2,1)} %all-gather.6.cloned.1.call-done) | copy-start | bytes 6291460
  215.9 29.9 %collective-permute-start.14 = (bf16[192,448]{1,0:T(8,128)(2,1)}, bf16[192,448]{1,0:T(8,128)(2,1)}, u32[]{:S(2)}, u32[]{:S(2)}) collective-permute-start(bf16[192,448]{1,0:T(8,128)(2,1)} %get-tuple-element.14), channel_id=1, source_target_pairs={{0,1},{1,2},{2,3},{3,0},{4,5},{5,6},{6,7},{7,4},{8,9},{9,10},{10,1... | collective-permute-start | bytes 516104 | tf_op jit(solution)/shard_map/ppermute | solution.py:20
  217.3 29.4 %collective-permute-start.15 = (bf16[192,448]{1,0:T(8,128)(2,1)}, bf16[192,448]{1,0:T(8,128)(2,1)}, u32[]{:S(2)}, u32[]{:S(2)}) collective-permute-start(bf16[192,448]{1,0:T(8,128)(2,1)} %get-tuple-element.14), channel_id=1, source_target_pairs={{0,2},{1,3},{2,0},{3,1},{4,6},{5,7},{6,4},{7,5},{8,10},{9,11},{10,... | collective-permute-start | bytes 516104 | tf_op jit(solution)/shard_map/ppermute | solution.py:20
  245.4 6.0 %collective-permute-start.16 = (bf16[192,448]{1,0:T(8,128)(2,1)}, bf16[192,448]{1,0:T(8,128)(2,1)S(1)}, u32[]{:S(2)}, u32[]{:S(2)}) collective-permute-start(bf16[192,448]{1,0:T(8,128)(2,1)} %get-tuple-element.14), channel_id=1, source_target_pairs={{0,3},{1,0},{2,1},{3,2},{4,7},{5,4},{6,5},{7,6},{8,11},{9,8},{10,9... | collective-permute-start | bytes 516104 | tf_op jit(solution)/shard_map/ppermute | solution.py:20
Sparse Core Ops, SparseCore 0:
  12.5 63.0 all-gather.3
  99.7 75.4 all-gather.5

commit v2 on v0

v2 whole, which is shorter than its diff:
```python
import jax
import jax.numpy as jnp
from jax import lax
from jax.experimental import pallas as pl
from jax.experimental.pallas import tpu as pltpu
from jax.sharding import Mesh, PartitionSpec as P

EXAMPLES = 8
T_EX = 128
NY, NZ, NC, NX = 4, 8, 2, 4
ROWS = 16
STEPS = 4
BF16, F32 = jnp.bfloat16, jnp.float32
SIZES = {"y": NY, "z": NZ, "core": NC, "x": NX}


def shift(v, axis, d):
    n = SIZES[axis]
    return lax.ppermute(v, axis, [(i, (i + d) % n) for i in range(n)])


def ring_z(v):
    up, down = [v], [v]
    for _ in range(4):
        up.append(shift(up[-1], "z", 1))
    for _ in range(3):
        down.append(shift(down[-1], "z", -1))
    return up + down[:0:-1]


def product_kernel(at_ref, *refs):
    parts, (b_ref, b_other_ref, o_ref) = refs[:-3], refs[-3:]
    k, c = pl.program_id(0), at_ref[2]

    @pl.when(k == 0)
    def _():
        o_ref[...] = jnp.zeros_like(o_ref)

    row = 0
    for x_ref in parts:
        n = x_ref.shape[0]
        for b, h in ((b_ref, c), (b_other_ref, 1 - c)):
            o_ref[h, row : row + n, :] += lax.dot_general(
                x_ref[...], b[...], (((1,), (1,)), ((), ())), preferred_element_type=F32
            )
        row += n


def product(at, parts, b, b_other):
    rows, depth = sum(p.shape[0] for p in parts), parts[0].shape[1]
    cols, step = b.shape[0], depth // STEPS
    spec_b = pl.BlockSpec((cols, step), lambda k, t: (0, k))
    return pl.pallas_call(
        product_kernel,
        grid_spec=pltpu.PrefetchScalarGridSpec(
            num_scalar_prefetch=1,
            grid=(STEPS,),
            in_specs=[pl.BlockSpec((p.shape[0], step), lambda k, t: (0, k)) for p in parts] + [spec_b, spec_b],
            out_specs=pl.BlockSpec((NC, rows, cols), lambda k, t: (0, 0, 0)),
        ),
        out_shape=jax.ShapeDtypeStruct((NC, rows, cols), F32),
        compiler_params=pltpu.CompilerParams(vmem_limit_bytes=24 * 2**20),
        cost_estimate=pl.CostEstimate(
            flops=4 * rows * cols * depth, bytes_accessed=2 * depth * (rows + 2 * cols) + 8 * rows * cols, transcendentals=0
        ),
    )(at, *parts, b, b_other)


def sum_over_x(partial):
    cols = partial.shape[2]
    terms = lax.all_to_all(partial.reshape(-1, cols), ("core", "x"), 0, 0, tiled=True)
    total = terms.reshape(NC, NX, -1, cols).sum(1).astype(BF16)
    return total.reshape(-1, cols)


def finish_kernel(at_ref, near_ref, far_ref, own_ref, other_ref, o_ref, rows, turned):
    y, z, c = at_ref[0], at_ref[1], at_ref[2]

    @pl.when(pl.program_id(0) == 0)
    def _():
        chunks = ((near_ref, 0, (0,)), (near_ref, NZ * NC // NX, (-1, 1)), (far_ref, 0, (2,)))
        for ref, skip, y_steps in chunks:
            each = len(y_steps) * NZ // NX
            stride = ref.shape[0] // (NX * ROWS)
            for j in range(NX * NC * each):
                slot, s = j // (NC * each), (j // each) % NC
                i = slot * stride + skip + s * each + j % each
                block = slot * each + j % each
                y_at = lax.rem(y + (y_steps[block // NZ] + NY), NY)
                z_at = lax.rem(z + (NZ - block % NZ), NZ)
                to = pl.multiple_of(((y_at * NZ + z_at) * NC + s) * ROWS, ROWS)
                rows[pl.ds(to, ROWS), :] = ref[i * ROWS : (i + 1) * ROWS, :]
        for e in range(EXAMPLES):
            turned[e] = rows[e * T_EX : (e + 1) * T_EX, :].T

    for i in range(EXAMPLES):
        ref, core = (own_ref, c) if i < NY else (other_ref, 1 - c)
        r = jnp.dot(turned[(i % NY) * NC + core], ref[0, i % NY], preferred_element_type=F32)
        r = r * r
        if i > 0:
            r = r + o_ref[...]
        if i == EXAMPLES - 1:
            r = r * (1.0 / (EXAMPLES * T_EX))
        o_ref[...] = r


def finish(at, g_parts, own, other):
    tokens, cols = sum(g.shape[0] for g in g_parts), g_parts[0].shape[1]
    n_blk = own.shape[3]
    spec_a = pl.BlockSpec((1, NY, T_EX, n_blk), lambda j, t: (j, 0, 0, 0))
    return pl.pallas_call(
        finish_kernel,
        grid_spec=pltpu.PrefetchScalarGridSpec(
            num_scalar_prefetch=1,
            grid=(NZ,),
            in_specs=[pl.BlockSpec(g.shape, lambda j, t: (0, 0)) for g in g_parts] + [spec_a, spec_a],
            out_specs=pl.BlockSpec((cols, n_blk), lambda j, t: (0, j)),
            scratch_shapes=[pltpu.VMEM((tokens, cols), BF16), pltpu.VMEM((EXAMPLES, cols, T_EX), BF16)],
        ),
        out_shape=jax.ShapeDtypeStruct((cols, NZ * n_blk), F32),
        compiler_params=pltpu.CompilerParams(vmem_limit_bytes=24 * 2**20),
        cost_estimate=pl.CostEstimate(
            flops=2 * tokens * cols * NZ * n_blk, bytes_accessed=4 * cols * NZ * n_blk + 4 * tokens * n_blk * NZ, transcendentals=0
        ),
    )(at, *g_parts, own, other)


def exchange_acts(acts, act_basis, x):
    depth, n_blk = act_basis.shape[0], act_basis.shape[1] // NZ
    quarter = acts.shape[0] // NX
    halves = n_blk // depth
    mine = lax.dynamic_slice_in_dim(acts, x * quarter, quarter, 0)
    basis = act_basis.reshape(depth, NZ, halves, depth).transpose(1, 2, 0, 3).reshape(NZ, n_blk, depth)
    sent = jnp.concatenate([basis, jnp.broadcast_to(mine[None], (NZ, quarter, depth))], axis=1)
    got = lax.all_to_all(sent, "z", 0, 0, tiled=True)
    basis = got[:, :n_blk].reshape(NZ, halves, depth, depth).transpose(0, 2, 1, 3).reshape(NZ * depth, n_blk)
    rows = got[:, n_blk:].transpose(1, 0, 2).reshape(quarter, NZ * depth)
    return lax.all_gather(rows, "x", axis=0, tiled=True), basis


def after(values, *others):
    return lax.optimization_barrier((tuple(values), others))[0]


def body(acts, grads, act_basis, grad_basis):
    y, z, c, x = (lax.axis_index(a) for a in ("y", "z", "core", "x"))
    at = jnp.stack([y, z, c]).astype(jnp.int32)
    basis = grad_basis.T
    basis_other = shift(basis, "core", 1)
    rows, basis_acts = exchange_acts(acts, act_basis, x)
    load = jnp.concatenate(ring_z(grads), axis=0)
    h = load.shape[0] // 2

    below, above = shift(load, "y", 1), shift(load, "y", -1)
    product_load = product(at, [load], basis, basis_other)
    (rows,) = after([rows], load, product_load)
    partial = jnp.dot(rows, basis_acts, preferred_element_type=F32)
    terms = lax.all_to_all(partial, ("y", "core"), 0, 0, tiled=True)
    piece = terms.reshape(NY * NC, T_EX, -1).sum(0).astype(BF16)

    far = [shift(below[:h], "y", 1), shift(above[h:], "y", -1)]
    product_near = product(at, [below, above], basis, basis_other)
    along_y = lax.all_to_all(jnp.broadcast_to(piece[None], (NY,) + piece.shape), "y", 0, 0, tiled=True)
    (along_y,) = after([along_y], below, above)
    own = lax.all_gather(along_y, "z", axis=0)
    total_load = sum_over_x(product_load)

    far = after(far, product_near, along_y, total_load)
    product_far = product(at, far, basis, basis_other)
    total_far = sum_over_x(product_far)
    total_near = sum_over_x(product_near)
    g_load = lax.all_gather(jnp.concatenate([total_load, total_near], axis=0), "x", axis=0, tiled=True)
    (total_far,) = after([total_far], g_load)
    g_far = lax.all_gather(total_far, "x", axis=0, tiled=True)
    (own,) = after([own], g_far)
    return finish(at, [g_load, g_far], own, shift(own, "core", 1))


def solution(mesh):
    wide = ("y", "z", "core")
    return jax.shard_map(
        body,
        mesh=Mesh(mesh.devices.reshape(NY, NZ, NC, NX), wide + ("x",)),
        in_specs=(P(None, wide), P(wide, "x"), P(wide, "x"), P("x", wide)),
        out_specs=P(wide, "x"),
        check_vma=False,
    )
```

time: 423 us -> 241 us (0.57)
  blocking collectives: 349 us -> 48.7 us
  waiting for transfers between devices: 0.71 us -> 61.5 us
  matrix products: 53.9 us -> 2.3 us
  starting transfers between devices: 0.01 us -> 43 us
  Pallas kernels: 0 us -> 37.4 us
  local copies, waits for them, and re-layouts: 0.84 us -> 28.1 us
    psum x2 -> x0, blocking collectives: 349 us -> none  [the longest x1 313 us: body(): rot_acts = lax.psum(act_terms, 'wide').astype(jnp.bfloat16)]
    dot_general x10 -> x1, matrix products: 53.9 us -> 2.3 us  [body(): partial = jnp.dot(rows, basis_acts, preferred_element_type=F32)]
    ppermute x0 -> x13, waiting for transfers between devices: none -> 41.7 us  [shift(): return lax.ppermute(v, axis, [(i, (i + d) % n) for i in range(n)])]
    pallas_call x0 -> x4, Pallas kernels: none -> 37.4 us  [the longest x3 30.2 us: product(): pl.pallas_call(product_kernel, grid_spec=pltpu.PrefetchScalarGridSpec(num...]
    all_gather x0 -> x2, blocking collectives: none -> 28.5 us  [the longest x1 16.1 us: body(): lax.all_gather(jnp.concatenate([total_load, total_near], axis=0), 'x', ax...]
    all_to_all x0 -> x5, starting transfers between devices: none -> 24.1 us  [the longest x3 14.8 us: sum_over_x(): lax.all_to_all(partial.reshape(-1, cols), ('core', 'x'), 0, 0, tiled=True)]
    all_to_all x0 -> x1, blocking collectives: none -> 20.2 us  [body(): terms = lax.all_to_all(partial, ('y', 'core'), 0, 0, tiled=True)]
    ppermute x0 -> x13, starting transfers between devices: none -> 18.8 us  [shift(): return lax.ppermute(v, axis, [(i, (i + d) % n) for i in range(n)])]
  transfers between devices with their start and end apart: 1 -> 20, of which waited for: 0 -> 7; matrix products, arithmetic and copies ran while one was open for 1% -> 9% of each run, Pallas kernels for 0% -> 13%
where the time goes in v2:
time: 241 us; the launch traced here: 237 us
  waiting for transfers between devices  61.5 us (26%)
  blocking collectives  48.7 us (20%)
  starting transfers between devices  43 us (18%)
  Pallas kernels  37.4 us (16%)
  local copies, waits for them, and re-layouts  28.1 us (12%)
  between operations  13.6 us (6%)
  other arithmetic  2.62 us (1%)
    ppermute x13, waiting for transfers between devices, shift(): return lax.ppermute(v, axis, [(i, (i + d) % n) for i in range(n)])  41.7 us
    pallas_call x3, Pallas kernels, product(): pl.pallas_call(product_kernel, grid_spec=pltpu.PrefetchScalarGridSpec(num...  30.2 us
    all_to_all x1, blocking collectives, body(): terms = lax.all_to_all(partial, ('y', 'core'), 0, 0, tiled=True)  20.2 us
    ppermute x13, starting transfers between devices, shift(): return lax.ppermute(v, axis, [(i, (i + d) % n) for i in range(n)])  18.8 us
    unnamed x22, local copies, waits for them, and re-layouts  17.2 us
    all_gather x1, blocking collectives, body(): lax.all_gather(jnp.concatenate([total_load, total_near], axis=0), 'x', ax...  16.1 us
    all_to_all x3, starting transfers between devices, sum_over_x(): lax.all_to_all(partial.reshape(-1, cols), ('core', 'x'), 0, 0, tiled=True)  14.8 us
    all_gather x1, waiting for transfers between devices, exchange_acts(): return (lax.all_gather(rows, 'x', axis=0, tiled=True), basis)  13.2 us
  transfers between devices with their start and end apart: 20, of which 7 were waited for; matrix products, arithmetic and copies ran while one was open for 9% of the time, Pallas kernels for 13%

profile of v2, /device:TPU:2, one launch (start us, length us, event | category | flops | bytes accessed | tf_op | source)
XLA Modules:
  0.0 237.2 jit_solution(5913340228469066638)
XLA Ops:
  6.5 1.9 collective-permute-start
  8.5 3.9 %collective-permute-start.4 = (bf16[16,7168]{1,0:T(8,128)(2,1)}, bf16[16,7168]{1,0:T(8,128)(2,1)S(1)}, u32[]{:S(2)}, u32[]{:S(2)}) collective-permute-start(bf16[16,7168]{1,0:T(8,128)(2,1)} %param.5), channel_id=1, source_target_pairs={{0,56},{8,0},{16,8},{24,16},{32,24},{40,32},{48,40},{56,48},{1,57}... | collective-permute-start | bytes 688136 | tf_op jit(solution)/shard_map/ppermute | solution.py:19
  12.4 1.3 copy.11
  14.1 1.0 pad_maximum_fusion
  15.2 5.8 %all-to-all-start.2 = ((bf16[8,512,128]{2,1,0:T(8,128)(2,1)}), bf16[8,512,128]{2,1,0:T(8,128)(2,1)S(1)}, u32[]{:S(2)}, u32[]{:S(2)}) async-start(bf16[8,512,128]{2,1,0:T(8,128)(2,1)} %pad_maximum_fusion), calls=%async_computation.2 | async-start | bytes 2097152 | tf_op jit(solution)/shard_map/all_to_all | solution.py:135
  21.1 0.7 constant_dynamic-update-slice_fusion.7
  21.8 2.0 collective-permute-start.1
  23.8 0.7 constant_dynamic-update-slice_fusion.6
  24.5 1.3 collective-permute-start.5
  25.7 26.9 %collective-permute-done.1 = bf16[16,7168]{1,0:T(8,128)(2,1)S(1)} collective-permute-done((bf16[16,7168]{1,0:T(8,128)(2,1)S(1)}, bf16[16,7168]{1,0:T(8,128)(2,1)S(1)}, u32[]{:S(2)}, u32[]{:S(2)}) %collective-permute-start.1) | collective-permute-done | bytes 229408 | tf_op jit(solution)/shard_map/ppermute | solution.py:19
  52.6 0.7 constant_dynamic-update-slice_fusion.5
  53.4 3.2 %collective-permute-start.6 = (bf16[16,7168]{1,0:T(8,128)(2,1)S(1)}, bf16[16,7168]{1,0:T(8,128)(2,1)S(1)}, u32[]{:S(2)}, u32[]{:S(2)}) collective-permute-start(bf16[16,7168]{1,0:T(8,128)(2,1)S(1)} %collective-permute-done.5), channel_id=1, source_target_pairs={{0,56},{8,0},{16,8},{24,16},{32,24},{40,32},{48,40},{56,48},{1,57}... | collective-permute-start | bytes 688136 | tf_op jit(solution)/shard_map/ppermute | solution.py:19
  56.6 4.2 %collective-permute-done.2 = bf16[16,7168]{1,0:T(8,128)(2,1)S(1)} collective-permute-done((bf16[16,7168]{1,0:T(8,128)(2,1)S(1)}, bf16[16,7168]{1,0:T(8,128)(2,1)S(1)}, u32[]{:S(2)}, u32[]{:S(2)}) %collective-permute-start.2) | collective-permute-done | bytes 229408 | tf_op jit(solution)/shard_map/ppermute | solution.py:19
  60.8 0.7 constant_dynamic-update-slice_fusion.4
  61.6 1.0 copy.13
  62.6 5.4 %collective-permute-done.3 = bf16[16,7168]{1,0:T(8,128)(2,1)S(1)} collective-permute-done((bf16[16,7168]{1,0:T(8,128)(2,1)S(1)}, bf16[16,7168]{1,0:T(8,128)(2,1)S(1)}, u32[]{:S(2)}, u32[]{:S(2)}) %collective-permute-start.3) | collective-permute-done | bytes 229408 | tf_op jit(solution)/shard_map/ppermute | solution.py:19
  68.0 0.7 constant_dynamic-update-slice_fusion.3
  69.4 0.7 constant_dynamic-update-slice_fusion.1
  70.1 0.7 constant_dynamic-update-slice_fusion.refs_0_
  70.8 1.6 collective-permute-start.8
  72.4 1.7 collective-permute-start.9
  75.0 2.9 %copy-done.1 = bf16[7168,448]{0,1:T(8,128)(2,1)S(1)} copy-done((bf16[7168,448]{0,1:T(8,128)(2,1)S(1)}, bf16[7168,448]{0,1:T(8,128)(2,1)}, u32[]{:S(2)}) %copy-start.1) | copy-done | bytes 6422552
  78.0 7.9 %shard_map.46 = f32[2,128,448]{2,1,0:T(8,128)} custom-call(s32[3]{0:T(128)S(1)} %pad_add_fusion.at_ref, bf16[128,7168]{1,0:T(8,128)(2,1)} %constant_dynamic-update-slice_fusion.refs_0_, bf16[448,7168]{1,0:T(8,128)(2,1)S(1)} %bitcast.31, bf16[448,7168]{1,0:T(8,128)(2,1)} %collective-permute-done.7.refs_2_.refs_3_), custom_call_target="tpu_custom_call" | custom-call | flops 1644167168 | bytes 15138816 | tf_op jit(solution)/shard_map/pallas_call | solution.py:53
  85.9 13.2 %all-gather.4.cloned.1.call-done = bf16[1024,1024]{0,1:T(8,128)(2,1)} async-done(((bf16[256,1024]{0,1:T(8,128)(2,1)}), bf16[1024,1024]{0,1:T(8,128)(2,1)}) %all-gather.4.cloned.1.call-update) | async-done | bytes 2097168 | tf_op jit(solution)/shard_map/all_gather | solution.py:138
  99.1 3.9 %copy.16 = bf16[1024,1024]{1,0:T(8,128)(2,1)} copy(bf16[1024,1024]{0,1:T(8,128)(2,1)} %all-gather.4.cloned.1.call-done) | data formatting | bytes 4194304 | tf_op jit(solution)/shard_map/dot_general | solution.py:157
  103.0 2.3 fusion.1
  105.3 20.2 %all_to_all.43 = f32[8,128,256]{2,1,0:T(8,128)S(1)} all-to-all(f32[8,128,256]{2,1,0:T(8,128)S(1)} %fusion.1), channel_id=1, replica_groups=mesh['y'=4,'z'=8,'core'=2,'x'=4] {'y','core'}, dimensions={0} | all-to-all | bytes 2097152 | tf_op jit(solution)/shard_map/all_to_all | solution.py:158
  125.6 0.7 broadcast_in_dim.5
  126.3 3.4 %all-to-all-start.4 = ((bf16[4,128,256]{2,1,0:T(8,128)(2,1)}), bf16[4,128,256]{2,1,0:T(8,128)(2,1)S(1)}, u32[]{:S(2)}, u32[]{:S(2)}) async-start(bf16[4,128,256]{2,1,0:T(8,128)(2,1)} %broadcast_in_dim.5), calls=%async_computation.4 | async-start | bytes 524288 | tf_op jit(solution)/shard_map/all_to_all | solution.py:163
  129.8 6.6 %all-to-all-done.4 = bf16[4,128,256]{2,1,0:T(8,128)(2,1)S(1)} async-done(((bf16[4,128,256]{2,1,0:T(8,128)(2,1)}), bf16[4,128,256]{2,1,0:T(8,128)(2,1)S(1)}, u32[]{:S(2)}, u32[]{:S(2)}) %all-to-all-start.4) | async-done | bytes 262176 | tf_op jit(solution)/shard_map/all_to_all | solution.py:163
  136.3 0.7 copy-done.5
  137.1 5.2 %all-to-all-start = ((f32[8,32,448]{2,1,0:T(8,128)}), f32[8,32,448]{2,1,0:T(8,128)S(1)}, u32[]{:S(2)}, u32[]{:S(2)}) async-start(f32[8,32,448]{2,1,0:T(8,128)} %bitcast.4), calls=%async_computation | async-start | bytes 1048576 | tf_op jit(solution)/shard_map/all_to_all | solution.py:71
  142.3 1.0 slice.16
  143.9 2.2 slice.17
  146.1 2.7 %collective-permute-start.11 = (bf16[64,7168]{1,0:T(8,128)(2,1)}, bf16[64,7168]{1,0:T(8,128)(2,1)}, u32[]{:S(2)}, u32[]{:S(2)}) collective-permute-start(bf16[64,7168]{1,0:T(8,128)(2,1)} %slice.17), channel_id=1, source_target_pairs={{0,192},{64,0},{128,64},{192,128},{1,193},{65,1},{129,65},{193,129... | collective-permute-start | bytes 2752520 | tf_op jit(solution)/shard_map/ppermute | solution.py:19
  148.8 2.8 %copy-done.2 = bf16[7168,448]{0,1:T(8,128)(2,1)S(1)} copy-done((bf16[7168,448]{0,1:T(8,128)(2,1)S(1)}, bf16[7168,448]{0,1:T(8,128)(2,1)}, u32[]{:S(2)}) %copy-start.2) | copy-done | bytes 6422552
  151.6 11.4 %shard_map.47 = f32[2,256,448]{2,1,0:T(8,128)} custom-call(s32[3]{0:T(128)S(1)} %pad_add_fusion.at_ref, bf16[128,7168]{1,0:T(8,128)(2,1)S(1)} %collective-permute-done.8.refs_0_, bf16[128,7168]{1,0:T(8,128)(2,1)} %collective-permute-done.9.refs_1_, bf16[448,7168]{1,0:T(8,128)(2,1)S(1)} %bitcast.32, bf16[448,7168]{1,0:T(8,128)(2,1)} %collective-permute-done.7.refs_2_.refs_3_), custom_call_target="tpu_custom_call" | custom-call | flops 3288334336 | bytes 17432576 | tf_op jit(solution)/shard_map/pallas_call | solution.py:53
  163.0 4.8 %all-to-all-start.1 = ((f32[8,64,448]{2,1,0:T(8,128)}), f32[8,64,448]{2,1,0:T(8,128)}, u32[]{:S(2)}, u32[]{:S(2)}) async-start(f32[8,64,448]{2,1,0:T(8,128)} %bitcast.7), calls=%async_computation.1 | async-start | bytes 2097152 | tf_op jit(solution)/shard_map/all_to_all | solution.py:71
  167.8 0.9 collective-permute-done.11.refs_1_
  168.7 2.9 %copy-done.3 = bf16[7168,448]{0,1:T(8,128)(2,1)S(1)} copy-done((bf16[7168,448]{0,1:T(8,128)(2,1)S(1)}, bf16[7168,448]{0,1:T(8,128)(2,1)}, u32[]{:S(2)}) %copy-start.3) | copy-done | bytes 6422552
  171.6 10.9 %shard_map.48 = f32[2,128,448]{2,1,0:T(8,128)} custom-call(s32[3]{0:T(128)S(1)} %pad_add_fusion.at_ref, bf16[64,7168]{1,0:T(8,128)(2,1)S(1)} %collective-permute-done.10.refs_0_, bf16[64,7168]{1,0:T(8,128)(2,1)} %collective-permute-done.11.refs_1_, bf16[448,7168]{1,0:T(8,128)(2,1)S(1)} %bitcast.33, bf16[448,7168]{1,0:T(8,128)(2,1)} %collective-permute-done.7.refs_2_.refs_3_), custom_call_target="tpu_custom_call" | custom-call | flops 1644167168 | bytes 15138816 | tf_op jit(solution)/shard_map/pallas_call | solution.py:53
  182.5 4.8 %all-to-all-start.5 = ((f32[8,32,448]{2,1,0:T(8,128)}), f32[8,32,448]{2,1,0:T(8,128)S(1)}, u32[]{:S(2)}, u32[]{:S(2)}) async-start(f32[8,32,448]{2,1,0:T(8,128)} %bitcast.18), calls=%async_computation.5 | async-start | bytes 1048576 | tf_op jit(solution)/shard_map/all_to_all | solution.py:71
  187.3 1.3 bitcast_reduce_fusion
  188.6 16.1 %all_gather.15.near_ref = bf16[768,448]{1,0:T(8,128)(2,1)S(1)} all-gather(bf16[192,448]{1,0:T(8,128)(2,1)S(1)} %pad_maximum_fusion.1), channel_id=1, replica_groups=mesh['y'=4,'z'=8,'core'=2,'x'=4] {'x'}, dimensions={0}, use_global_device_ids=true | all-gather | bytes 860160 | tf_op jit(solution)/shard_map/all_gather | solution.py:172
  204.7 12.5 %all_gather.17.far_ref = bf16[256,448]{1,0:T(8,128)(2,1)S(1)} all-gather(bf16[64,448]{1,0:T(8,128)(2,1)S(1)} %bitcast.42), channel_id=1, replica_groups=mesh['y'=4,'z'=8,'core'=2,'x'=4] {'x'}, dimensions={0}, use_global_device_ids=true | all-gather | bytes 286720 | tf_op jit(solution)/shard_map/all_gather | solution.py:174
  217.2 4.4 %collective-permute-done.12.other_ref = bf16[8,4,128,256]{3,2,1,0:T(8,128)(2,1)S(1)} collective-permute-done((bf16[8,4,128,256]{3,2,1,0:T(8,128)(2,1)}, bf16[8,4,128,256]{3,2,1,0:T(8,128)(2,1)S(1)}, u32[]{:S(2)}, u32[]{:S(2)}) %collective-permute-start.12) | collective-permute-done | bytes 2097184 | tf_op jit(solution)/shard_map/ppermute | solution.py:19
  221.6 1.6 copy-done.4
  223.2 7.2 %shard_map.49 = f32[448,2048]{1,0:T(8,128)} custom-call(s32[3]{0:T(128)S(1)} %pad_add_fusion.at_ref, bf16[768,448]{1,0:T(8,128)(2,1)S(1)} %all_gather.15.near_ref, bf16[256,448]{1,0:T(8,128)(2,1)S(1)} %all_gather.17.far_ref, bf16[8,4,128,256]{3,2,1,0:T(8,128)(2,1)S(1)} %bitcast.35, bf16[8,4,128,256]{3,2,1,0:T(8,128)(2,1)S(1)} %collective-permute-done.12.other_ref), custom_call_target="tpu_custom_call" | custom-call | flops 1879048192 | bytes 12058624 | tf_op jit(solution)/shard_map/pallas_call | solution.py:111
  (43 shorter events, 3.0 us)
Async XLA Ops:
  6.5 7.5 %copy-start = (bf16[1024,128]{1,0:T(8,128)(2,1)S(1)}, bf16[1024,128]{1,0:T(8,128)(2,1)}, u32[]{:S(2)}) copy-start(bf16[1024,128]{1,0:T(8,128)(2,1)} %param.4) | copy-start | bytes 786436
  6.5 15.2 %collective-permute-start = (bf16[16,7168]{1,0:T(8,128)(2,1)}, bf16[16,7168]{1,0:T(8,128)(2,1)S(1)}, u32[]{:S(2)}, u32[]{:S(2)}) collective-permute-start(bf16[16,7168]{1,0:T(8,128)(2,1)} %param.5), channel_id=1, source_target_pairs={{0,8},{8,16},{16,24},{24,32},{32,40},{40,48},{48,56},{56,0},{1,9},... | collective-permute-start | bytes 688136 | tf_op jit(solution)/shard_map/ppermute | solution.py:19
  8.5 16.0 %collective-permute-start.4 = (bf16[16,7168]{1,0:T(8,128)(2,1)}, bf16[16,7168]{1,0:T(8,128)(2,1)S(1)}, u32[]{:S(2)}, u32[]{:S(2)}) collective-permute-start(bf16[16,7168]{1,0:T(8,128)(2,1)} %param.5), channel_id=1, source_target_pairs={{0,56},{8,0},{16,8},{24,16},{32,24},{40,32},{48,40},{56,48},{1,57}... | collective-permute-start | bytes 688136 | tf_op jit(solution)/shard_map/ppermute | solution.py:19
  12.4 62.6 %collective-permute-start.7 = (bf16[448,7168]{1,0:T(8,128)(2,1)}, bf16[448,7168]{1,0:T(8,128)(2,1)}, u32[]{:S(2)}, u32[]{:S(2)}) collective-permute-start(bf16[448,7168]{1,0:T(8,128)(2,1)} %bitcast.30), channel_id=1, source_target_pairs={{0,4},{4,0},{1,5},{5,1},{2,6},{6,2},{3,7},{7,3},{8,12},{12,8},{9,1... | collective-permute-start | bytes 19267592 | tf_op jit(solution)/shard_map/ppermute | solution.py:19
  14.1 6.9 %copy-start.6 = (bf16[16,7168]{1,0:T(8,128)(2,1)S(1)}, bf16[16,7168]{1,0:T(8,128)(2,1)}, u32[]{:S(2)}) copy-start(bf16[16,7168]{1,0:T(8,128)(2,1)} %param.5) | copy-start | bytes 688132
  15.2 46.3 %all-to-all-start.2 = ((bf16[8,512,128]{2,1,0:T(8,128)(2,1)}), bf16[8,512,128]{2,1,0:T(8,128)(2,1)S(1)}, u32[]{:S(2)}, u32[]{:S(2)}) async-start(bf16[8,512,128]{2,1,0:T(8,128)(2,1)} %pad_maximum_fusion), calls=%async_computation.2 | async-start | bytes 2097152 | tf_op jit(solution)/shard_map/all_to_all | solution.py:135
  21.0 78.0 %all-gather.4.cloned.1.call-start = ((), (), s32[]{:S(2)}) async-start(), calls=%async_computation.6 | async-start | bytes 2621440 | tf_op jit(solution)/shard_map/all_gather | solution.py:138
  21.8 30.9 %collective-permute-start.1 = (bf16[16,7168]{1,0:T(8,128)(2,1)S(1)}, bf16[16,7168]{1,0:T(8,128)(2,1)S(1)}, u32[]{:S(2)}, u32[]{:S(2)}) collective-permute-start(bf16[16,7168]{1,0:T(8,128)(2,1)S(1)} %collective-permute-done), channel_id=1, source_target_pairs={{0,8},{8,16},{16,24},{24,32},{32,40},{40,48},{48,56},{56,0},{1,9},... | collective-permute-start | bytes 688136 | tf_op jit(solution)/shard_map/ppermute | solution.py:19
  24.5 28.9 %collective-permute-start.5 = (bf16[16,7168]{1,0:T(8,128)(2,1)S(1)}, bf16[16,7168]{1,0:T(8,128)(2,1)S(1)}, u32[]{:S(2)}, u32[]{:S(2)}) collective-permute-start(bf16[16,7168]{1,0:T(8,128)(2,1)S(1)} %collective-permute-done.4), channel_id=1, source_target_pairs={{0,56},{8,0},{16,8},{24,16},{32,24},{40,32},{48,40},{56,48},{1,57}... | collective-permute-start | bytes 688136 | tf_op jit(solution)/shard_map/ppermute | solution.py:19
  52.6 8.1 %collective-permute-start.2 = (bf16[16,7168]{1,0:T(8,128)(2,1)S(1)}, bf16[16,7168]{1,0:T(8,128)(2,1)S(1)}, u32[]{:S(2)}, u32[]{:S(2)}) collective-permute-start(bf16[16,7168]{1,0:T(8,128)(2,1)S(1)} %collective-permute-done.1), channel_id=1, source_target_pairs={{0,8},{8,16},{16,24},{24,32},{32,40},{40,48},{48,56},{56,0},{1,9},... | collective-permute-start | bytes 688136 | tf_op jit(solution)/shard_map/ppermute | solution.py:19
  53.4 15.4 %collective-permute-start.6 = (bf16[16,7168]{1,0:T(8,128)(2,1)S(1)}, bf16[16,7168]{1,0:T(8,128)(2,1)S(1)}, u32[]{:S(2)}, u32[]{:S(2)}) collective-permute-start(bf16[16,7168]{1,0:T(8,128)(2,1)S(1)} %collective-permute-done.5), channel_id=1, source_target_pairs={{0,56},{8,0},{16,8},{24,16},{32,24},{40,32},{48,40},{56,48},{1,57}... | collective-permute-start | bytes 688136 | tf_op jit(solution)/shard_map/ppermute | solution.py:19
  60.8 7.2 %collective-permute-start.3 = (bf16[16,7168]{1,0:T(8,128)(2,1)S(1)}, bf16[16,7168]{1,0:T(8,128)(2,1)S(1)}, u32[]{:S(2)}, u32[]{:S(2)}) collective-permute-start(bf16[16,7168]{1,0:T(8,128)(2,1)S(1)} %collective-permute-done.2), channel_id=1, source_target_pairs={{0,8},{8,16},{16,24},{24,32},{32,40},{40,48},{48,56},{56,0},{1,9},... | collective-permute-start | bytes 688136 | tf_op jit(solution)/shard_map/ppermute | solution.py:19
  70.8 58.9 %collective-permute-start.8 = (bf16[128,7168]{1,0:T(8,128)(2,1)}, bf16[128,7168]{1,0:T(8,128)(2,1)S(1)}, u32[]{:S(2)}, u32[]{:S(2)}) collective-permute-start(bf16[128,7168]{1,0:T(8,128)(2,1)} %constant_dynamic-update-slice_fusion.refs_0_), channel_id=1, source_target_pairs={{0,64},{64,128},{128,192},{192,0},{1,65},{65,129},{129,193},{193,1... | collective-permute-start | bytes 5505032 | tf_op jit(solution)/shard_map/ppermute | solution.py:19
  72.4 57.4 %collective-permute-start.9 = (bf16[128,7168]{1,0:T(8,128)(2,1)}, bf16[128,7168]{1,0:T(8,128)(2,1)}, u32[]{:S(2)}, u32[]{:S(2)}) collective-permute-start(bf16[128,7168]{1,0:T(8,128)(2,1)} %constant_dynamic-update-slice_fusion.refs_0_), channel_id=1, source_target_pairs={{0,192},{64,0},{128,64},{192,128},{1,193},{65,1},{129,65},{193,129... | collective-permute-start | bytes 5505032 | tf_op jit(solution)/shard_map/ppermute | solution.py:19
  75.0 2.9 %copy-start.1 = (bf16[7168,448]{0,1:T(8,128)(2,1)S(1)}, bf16[7168,448]{0,1:T(8,128)(2,1)}, u32[]{:S(2)}) copy-start(bf16[7168,448]{0,1:T(8,128)(2,1)} %param.7) | copy-start | bytes 19267588
  126.3 10.1 %all-to-all-start.4 = ((bf16[4,128,256]{2,1,0:T(8,128)(2,1)}), bf16[4,128,256]{2,1,0:T(8,128)(2,1)S(1)}, u32[]{:S(2)}, u32[]{:S(2)}) async-start(bf16[4,128,256]{2,1,0:T(8,128)(2,1)} %broadcast_in_dim.5), calls=%async_computation.4 | async-start | bytes 524288 | tf_op jit(solution)/shard_map/all_to_all | solution.py:163
  129.7 87.5 %all-gather.6.cloned.1.call-start = ((), (), s32[]{:S(2)}) async-start(), calls=%async_computation.7 | async-start | bytes 2359296 | tf_op jit(solution)/shard_map/all_gather | solution.py:165
  136.3 0.7 copy-start.5
  137.1 25.9 %all-to-all-start = ((f32[8,32,448]{2,1,0:T(8,128)}), f32[8,32,448]{2,1,0:T(8,128)S(1)}, u32[]{:S(2)}, u32[]{:S(2)}) async-start(f32[8,32,448]{2,1,0:T(8,128)} %bitcast.4), calls=%async_computation | async-start | bytes 1048576 | tf_op jit(solution)/shard_map/all_to_all | solution.py:71
  143.3 24.5 %collective-permute-start.10 = (bf16[64,7168]{1,0:T(8,128)(2,1)}, bf16[64,7168]{1,0:T(8,128)(2,1)S(1)}, u32[]{:S(2)}, u32[]{:S(2)}) collective-permute-start(bf16[64,7168]{1,0:T(8,128)(2,1)} %slice.16), channel_id=1, source_target_pairs={{0,64},{64,128},{128,192},{192,0},{1,65},{65,129},{129,193},{193,1... | collective-permute-start | bytes 2752520 | tf_op jit(solution)/shard_map/ppermute | solution.py:19
  146.1 22.6 %collective-permute-start.11 = (bf16[64,7168]{1,0:T(8,128)(2,1)}, bf16[64,7168]{1,0:T(8,128)(2,1)}, u32[]{:S(2)}, u32[]{:S(2)}) collective-permute-start(bf16[64,7168]{1,0:T(8,128)(2,1)} %slice.17), channel_id=1, source_target_pairs={{0,192},{64,0},{128,64},{192,128},{1,193},{65,1},{129,65},{193,129... | collective-permute-start | bytes 2752520 | tf_op jit(solution)/shard_map/ppermute | solution.py:19
  148.8 2.8 %copy-start.2 = (bf16[7168,448]{0,1:T(8,128)(2,1)S(1)}, bf16[7168,448]{0,1:T(8,128)(2,1)}, u32[]{:S(2)}) copy-start(bf16[7168,448]{0,1:T(8,128)(2,1)} %param.7) | copy-start | bytes 19267588
  163.0 19.5 %all-to-all-start.1 = ((f32[8,64,448]{2,1,0:T(8,128)}), f32[8,64,448]{2,1,0:T(8,128)}, u32[]{:S(2)}, u32[]{:S(2)}) async-start(f32[8,64,448]{2,1,0:T(8,128)} %bitcast.7), calls=%async_computation.1 | async-start | bytes 2097152 | tf_op jit(solution)/shard_map/all_to_all | solution.py:71
  168.7 2.9 %copy-start.3 = (bf16[7168,448]{0,1:T(8,128)(2,1)S(1)}, bf16[7168,448]{0,1:T(8,128)(2,1)}, u32[]{:S(2)}) copy-start(bf16[7168,448]{0,1:T(8,128)(2,1)} %param.7) | copy-start | bytes 19267588
  182.5 22.2 %all-to-all-start.5 = ((f32[8,32,448]{2,1,0:T(8,128)}), f32[8,32,448]{2,1,0:T(8,128)S(1)}, u32[]{:S(2)}, u32[]{:S(2)}) async-start(f32[8,32,448]{2,1,0:T(8,128)} %bitcast.18), calls=%async_computation.5 | async-start | bytes 1048576 | tf_op jit(solution)/shard_map/all_to_all | solution.py:71
  217.2 4.4 %collective-permute-start.12 = (bf16[8,4,128,256]{3,2,1,0:T(8,128)(2,1)}, bf16[8,4,128,256]{3,2,1,0:T(8,128)(2,1)S(1)}, u32[]{:S(2)}, u32[]{:S(2)}) collective-permute-start(bf16[8,4,128,256]{3,2,1,0:T(8,128)(2,1)} %bitcast.34), channel_id=1, source_target_pairs={{0,4},{4,0},{1,5},{5,1},{2,6},{6,2},{3,7},{7,3},{8,12},{12,8},{9,1... | collective-permute-start | bytes 6291464 | tf_op jit(solution)/shard_map/ppermute | solution.py:19
  221.6 1.6 copy-start.4
Sparse Core Ops, SparseCore 0:
  62.7 36.2 all-gather.3
  137.2 40.7 all-gather.5

commit v3 on v2

--- a/solution.py
+++ b/solution.py
@@ -36,14 +36,9 @@
     def _():
         o_ref[...] = jnp.zeros_like(o_ref)
 
-    row = 0
-    for x_ref in parts:
-        n = x_ref.shape[0]
-        for b, h in ((b_ref, c), (b_other_ref, 1 - c)):
-            o_ref[h, row : row + n, :] += lax.dot_general(
-                x_ref[...], b[...], (((1,), (1,)), ((), ())), preferred_element_type=F32
-            )
-        row += n
+    x = jnp.concatenate([p[...] for p in parts], axis=0) if len(parts) > 1 else parts[0][...]
+    for b, h in ((b_ref, c), (b_other_ref, 1 - c)):
+        o_ref[h] += lax.dot_general(x, b[...], (((1,), (1,)), ((), ())), preferred_element_type=F32)
 
 
 def product(at, parts, b, b_other):
@@ -59,7 +54,7 @@
             out_specs=pl.BlockSpec((NC, rows, cols), lambda k, t: (0, 0, 0)),
         ),
         out_shape=jax.ShapeDtypeStruct((NC, rows, cols), F32),
-        compiler_params=pltpu.CompilerParams(vmem_limit_bytes=24 * 2**20),
+        compiler_params=pltpu.CompilerParams(vmem_limit_bytes=54 * 2**20),
         cost_estimate=pl.CostEstimate(
             flops=4 * rows * cols * depth, bytes_accessed=2 * depth * (rows + 2 * cols) + 8 * rows * cols, transcendentals=0
         ),
@@ -125,17 +120,9 @@
     )(at, *g_parts, own, other)
 
 
-def exchange_acts(acts, act_basis, x):
-    depth, n_blk = act_basis.shape[0], act_basis.shape[1] // NZ
-    quarter = acts.shape[0] // NX
-    halves = n_blk // depth
-    mine = lax.dynamic_slice_in_dim(acts, x * quarter, quarter, 0)
-    basis = act_basis.reshape(depth, NZ, halves, depth).transpose(1, 2, 0, 3).reshape(NZ, n_blk, depth)
-    sent = jnp.concatenate([basis, jnp.broadcast_to(mine[None], (NZ, quarter, depth))], axis=1)
-    got = lax.all_to_all(sent, "z", 0, 0, tiled=True)
-    basis = got[:, :n_blk].reshape(NZ, halves, depth, depth).transpose(0, 2, 1, 3).reshape(NZ * depth, n_blk)
-    rows = got[:, n_blk:].transpose(1, 0, 2).reshape(quarter, NZ * depth)
-    return lax.all_gather(rows, "x", axis=0, tiled=True), basis
+def gather_x(v):
+    copies = jnp.broadcast_to(v[None], (NX,) + v.shape)
+    return lax.all_to_all(copies, "x", 0, 0, tiled=True).reshape((-1,) + v.shape[1:])
 
 
 def after(values, *others):
@@ -143,12 +130,14 @@
 
 
 def body(acts, grads, act_basis, grad_basis):
-    y, z, c, x = (lax.axis_index(a) for a in ("y", "z", "core", "x"))
+    y, z, c = (lax.axis_index(a) for a in ("y", "z", "core"))
     at = jnp.stack([y, z, c]).astype(jnp.int32)
     basis = grad_basis.T
     basis_other = shift(basis, "core", 1)
-    rows, basis_acts = exchange_acts(acts, act_basis, x)
+    rows = lax.all_gather(acts, "z", axis=1, tiled=True)
     load = jnp.concatenate(ring_z(grads), axis=0)
+    (act_basis,) = after([act_basis], load)
+    basis_acts = lax.all_to_all(act_basis, "z", 1, 0, tiled=True)
     h = load.shape[0] // 2
 
     below, above = shift(load, "y", 1), shift(load, "y", -1)
@@ -171,8 +160,8 @@
     total_near = sum_over_x(product_near)
     g_load = lax.all_gather(jnp.concatenate([total_load, total_near], axis=0), "x", axis=0, tiled=True)
     (total_far,) = after([total_far], g_load)
-    g_far = lax.all_gather(total_far, "x", axis=0, tiled=True)
-    (own,) = after([own], g_far)
+    (own,) = after([own], total_far)
+    g_far = gather_x(total_far)
     return finish(at, [g_load, g_far], own, shift(own, "core", 1))
 
 

time: 241 us -> 208 us (0.86)
  waiting for transfers between devices: 61.5 us -> 39.3 us
  local copies, waits for them, and re-layouts: 28.1 us -> 12.7 us
  blocking collectives: 48.7 us -> 58.4 us
    ppermute x13, waiting for transfers between devices: 41.7 us -> 28.4 us  [shift(): return lax.ppermute(v, axis, [(i, (i + d) % n) for i in range(n)])]
    all_gather x1 -> x0, blocking collectives: 12.5 us -> none  [body(): g_far = lax.all_gather(total_far, 'x', axis=0, tiled=True)]
    all_to_all x0 -> x1, blocking collectives: none -> 11.4 us  [gather_x(): lax.all_to_all(copies, 'x', 0, 0, tiled=True).reshape((-1,) + v.shape[1:])]
    all_to_all x1, blocking collectives: 20.2 us -> 30.5 us  [body(): terms = lax.all_to_all(partial, ('y', 'core'), 0, 0, tiled=True)]
    all_gather x1, waiting for transfers between devices: 13.2 us -> 4.19 us  [body(): rows = lax.all_gather(acts, 'z', axis=1, tiled=True)]
    unnamed x22 -> x17, local copies, waits for them, and re-layouts: 17.2 us -> 8.22 us
    dot_general x1 -> x0, local copies, waits for them, and re-layouts: 3.93 us -> none  [body(): partial = jnp.dot(rows, basis_acts, preferred_element_type=F32)]
  transfers between devices with their start and end apart: 20 -> 20, of which waited for: 7 -> 9; matrix products, arithmetic and copies ran while one was open for 9% -> 7% of each run, Pallas kernels for 13% -> 14%
where the time goes in v3:
time: 208 us; the launch traced here: 206 us
  blocking collectives  58.4 us (28%)
  starting transfers between devices  43.5 us (21%)
  waiting for transfers between devices  39.3 us (19%)
  Pallas kernels  35.5 us (17%)
  between operations  13.5 us (6%)
  local copies, waits for them, and re-layouts  12.7 us (6%)
  matrix products  2.3 us (1%)
    all_to_all x1, blocking collectives, body(): terms = lax.all_to_all(partial, ('y', 'core'), 0, 0, tiled=True)  30.5 us
    ppermute x13, waiting for transfers between devices, shift(): return lax.ppermute(v, axis, [(i, (i + d) % n) for i in range(n)])  28.4 us
    pallas_call x3, Pallas kernels, product(): pl.pallas_call(product_kernel, grid_spec=pltpu.PrefetchScalarGridSpec(num...  28.2 us
    ppermute x13, starting transfers between devices, shift(): return lax.ppermute(v, axis, [(i, (i + d) % n) for i in range(n)])  19.4 us
    all_gather x1, blocking collectives, body(): lax.all_gather(jnp.concatenate([total_load, total_near], axis=0), 'x', ax...  16.6 us
    all_to_all x3, starting transfers between devices, sum_over_x(): lax.all_to_all(partial.reshape(-1, cols), ('core', 'x'), 0, 0, tiled=True)  14.4 us
    all_to_all x1, blocking collectives, gather_x(): lax.all_to_all(copies, 'x', 0, 0, tiled=True).reshape((-1,) + v.shape[1:])  11.4 us
    unnamed x17, local copies, waits for them, and re-layouts  8.22 us
  transfers between devices with their start and end apart: 20, of which 9 were waited for; matrix products, arithmetic and copies ran while one was open for 7% of the time, Pallas kernels for 14%

profile of v3, /device:TPU:2, one launch (start us, length us, event | category | flops | bytes accessed | tf_op | source)
XLA Modules:
  0.0 206.1 jit_solution(4344541081051134914)
XLA Ops:
  6.5 1.9 collective-permute-start
  8.5 3.9 %collective-permute-start.4 = (bf16[16,7168]{1,0:T(8,128)(2,1)}, bf16[16,7168]{1,0:T(8,128)(2,1)S(1)}, u32[]{:S(2)}, u32[]{:S(2)}) collective-permute-start(bf16[16,7168]{1,0:T(8,128)(2,1)} %param.5), channel_id=1, source_target_pairs={{0,56},{8,0},{16,8},{24,16},{32,24},{40,32},{48,40},{56,48},{1,57}... | collective-permute-start | bytes 688136 | tf_op jit(solution)/shard_map/ppermute | solution.py:19
  12.4 1.7 constant_dynamic-update-slice_fusion.7
  14.1 4.1 %collective-permute-done = bf16[16,7168]{1,0:T(8,128)(2,1)S(1)} collective-permute-done((bf16[16,7168]{1,0:T(8,128)(2,1)}, bf16[16,7168]{1,0:T(8,128)(2,1)S(1)}, u32[]{:S(2)}, u32[]{:S(2)}) %collective-permute-start) | collective-permute-done | bytes 229408 | tf_op jit(solution)/shard_map/ppermute | solution.py:19
  18.2 0.7 constant_dynamic-update-slice_fusion.6
  18.9 3.2 %collective-permute-start.5 = (bf16[16,7168]{1,0:T(8,128)(2,1)S(1)}, bf16[16,7168]{1,0:T(8,128)(2,1)S(1)}, u32[]{:S(2)}, u32[]{:S(2)}) collective-permute-start(bf16[16,7168]{1,0:T(8,128)(2,1)S(1)} %collective-permute-done.4), channel_id=1, source_target_pairs={{0,56},{8,0},{16,8},{24,16},{32,24},{40,32},{48,40},{56,48},{1,57}... | collective-permute-start | bytes 688136 | tf_op jit(solution)/shard_map/ppermute | solution.py:19
  22.1 4.1 %collective-permute-done.1 = bf16[16,7168]{1,0:T(8,128)(2,1)S(1)} collective-permute-done((bf16[16,7168]{1,0:T(8,128)(2,1)S(1)}, bf16[16,7168]{1,0:T(8,128)(2,1)S(1)}, u32[]{:S(2)}, u32[]{:S(2)}) %collective-permute-start.1) | collective-permute-done | bytes 229408 | tf_op jit(solution)/shard_map/ppermute | solution.py:19
  26.2 0.7 constant_dynamic-update-slice_fusion.5
  26.9 2.7 %collective-permute-done.5 = bf16[16,7168]{1,0:T(8,128)(2,1)S(1)} collective-permute-done((bf16[16,7168]{1,0:T(8,128)(2,1)S(1)}, bf16[16,7168]{1,0:T(8,128)(2,1)S(1)}, u32[]{:S(2)}, u32[]{:S(2)}) %collective-permute-start.5) | collective-permute-done | bytes 229408 | tf_op jit(solution)/shard_map/ppermute | solution.py:19
  29.6 3.7 %collective-permute-start.6 = (bf16[16,7168]{1,0:T(8,128)(2,1)S(1)}, bf16[16,7168]{1,0:T(8,128)(2,1)S(1)}, u32[]{:S(2)}, u32[]{:S(2)}) collective-permute-start(bf16[16,7168]{1,0:T(8,128)(2,1)S(1)} %collective-permute-done.5), channel_id=1, source_target_pairs={{0,56},{8,0},{16,8},{24,16},{32,24},{40,32},{48,40},{56,48},{1,57}... | collective-permute-start | bytes 688136 | tf_op jit(solution)/shard_map/ppermute | solution.py:19
  33.3 3.4 %collective-permute-done.2 = bf16[16,7168]{1,0:T(8,128)(2,1)S(1)} collective-permute-done((bf16[16,7168]{1,0:T(8,128)(2,1)S(1)}, bf16[16,7168]{1,0:T(8,128)(2,1)S(1)}, u32[]{:S(2)}, u32[]{:S(2)}) %collective-permute-start.2) | collective-permute-done | bytes 229408 | tf_op jit(solution)/shard_map/ppermute | solution.py:19
  36.8 0.7 constant_dynamic-update-slice_fusion.4
  37.5 8.9 %collective-permute-done.3 = bf16[16,7168]{1,0:T(8,128)(2,1)S(1)} collective-permute-done((bf16[16,7168]{1,0:T(8,128)(2,1)S(1)}, bf16[16,7168]{1,0:T(8,128)(2,1)S(1)}, u32[]{:S(2)}, u32[]{:S(2)}) %collective-permute-start.3) | collective-permute-done | bytes 229408 | tf_op jit(solution)/shard_map/ppermute | solution.py:19
  46.4 0.7 constant_dynamic-update-slice_fusion.3
  47.1 0.7 constant_dynamic-update-slice_fusion.2
  47.8 0.7 constant_dynamic-update-slice_fusion.1
  48.5 0.7 constant_dynamic-update-slice_fusion.refs_0_
  49.2 0.8 copy.9
  50.0 5.6 %all-to-all-start.2 = ((bf16[128,8,256]{2,0,1:T(8,128)(2,1)}), bf16[128,8,256]{2,0,1:T(8,128)(2,1)S(1)}, u32[]{:S(2)}, u32[]{:S(2)}) async-start(bf16[128,8,256]{2,0,1:T(8,128)(2,1)} %bitcast.29), calls=%async_computation.2 | async-start | bytes 1048576 | tf_op jit(solution)/shard_map/all_to_all | solution.py:140
  55.6 1.3 collective-permute-start.8
  56.9 1.9 collective-permute-start.9
  58.8 0.6 pad_add_fusion.at_ref
  59.4 9.1 %shard_map.46 = f32[2,128,448]{2,1,0:T(8,128)} custom-call(s32[3]{0:T(128)} %pad_add_fusion.at_ref, bf16[128,7168]{1,0:T(8,128)(2,1)} %constant_dynamic-update-slice_fusion.refs_0_, bf16[448,7168]{1,0:T(8,128)(2,1)} %bitcast.34, bf16[448,7168]{1,0:T(8,128)(2,1)} %collective-permute-done.7.refs_2_.refs_3_), custom_call_target="tpu_custom_call" | custom-call | flops 1644167168 | bytes 15138816 | tf_op jit(solution)/shard_map/pallas_call | solution.py:48
  68.5 4.2 %all-gather.4.cloned.1.call-done = bf16[1024,1024]{1,0:T(8,128)(2,1)} async-done(((bf16[1024,128]{1,0:T(8,128)(2,1)}), bf16[1024,1024]{1,0:T(8,128)(2,1)}) %all-gather.4.cloned.1.call-update) | async-done | bytes 2097168 | tf_op jit(solution)/shard_map/all_gather | solution.py:137
  72.7 2.3 %fusion = f32[8,128,256]{2,1,0:T(8,128)S(1)} fusion(bf16[8,128,1024]{2,1,0:T(8,128)(2,1)} %bitcast.38, bf16[1024,256,1]{1,0,2:T(8,128)(2,1)S(1)} %bitcast.39), kind=kOutput, calls=%fused_computation.14 | convolution fusion | flops 536870912 | bytes 3670016 | tf_op jit(solution)/shard_map/dot_general | solution.py:146
  75.0 30.5 %all_to_all.62 = f32[8,128,256]{2,1,0:T(8,128)S(1)} all-to-all(f32[8,128,256]{2,1,0:T(8,128)S(1)} %fusion), channel_id=1, replica_groups=mesh['y'=4,'z'=8,'core'=2,'x'=4] {'y','core'}, dimensions={0} | all-to-all | bytes 2097152 | tf_op jit(solution)/shard_map/all_to_all | solution.py:147
  105.5 0.1 reduce_sum.38
  105.5 0.7 broadcast_in_dim.4
  106.3 4.1 %all-to-all-start.4 = ((bf16[4,128,256]{2,1,0:T(8,128)(2,1)}), bf16[4,128,256]{2,1,0:T(8,128)(2,1)S(1)}, u32[]{:S(2)}, u32[]{:S(2)}) async-start(bf16[4,128,256]{2,1,0:T(8,128)(2,1)} %broadcast_in_dim.4), calls=%async_computation.4 | async-start | bytes 524288 | tf_op jit(solution)/shard_map/all_to_all | solution.py:152
  110.4 6.7 %all-to-all-done.4 = bf16[4,128,256]{2,1,0:T(8,128)(2,1)S(1)} async-done(((bf16[4,128,256]{2,1,0:T(8,128)(2,1)}), bf16[4,128,256]{2,1,0:T(8,128)(2,1)S(1)}, u32[]{:S(2)}, u32[]{:S(2)}) %all-to-all-start.4) | async-done | bytes 262176 | tf_op jit(solution)/shard_map/all_to_all | solution.py:152
  117.0 0.7 copy-done.3
  117.8 4.8 %all-to-all-start = ((f32[8,32,448]{2,1,0:T(8,128)}), f32[8,32,448]{2,1,0:T(8,128)S(1)}, u32[]{:S(2)}, u32[]{:S(2)}) async-start(f32[8,32,448]{2,1,0:T(8,128)} %bitcast.4), calls=%async_computation | async-start | bytes 1048576 | tf_op jit(solution)/shard_map/all_to_all | solution.py:66
  122.5 0.1 slice.8
  122.6 0.6 collective-permute-start.10
  123.2 2.2 %slice.9 = bf16[64,7168]{1,0:T(8,128)(2,1)} slice(bf16[128,7168]{1,0:T(8,128)(2,1)} %collective-permute-done.9.refs_1_), slice={[64:128], [0:7168]} | slice | bytes 1835008 | tf_op jit(solution)/shard_map/slice | solution.py:150
  125.4 2.7 %collective-permute-start.11 = (bf16[64,7168]{1,0:T(8,128)(2,1)}, bf16[64,7168]{1,0:T(8,128)(2,1)}, u32[]{:S(2)}, u32[]{:S(2)}) collective-permute-start(bf16[64,7168]{1,0:T(8,128)(2,1)} %slice.9), channel_id=1, source_target_pairs={{0,192},{64,0},{128,64},{192,128},{1,193},{65,1},{129,65},{193,129... | collective-permute-start | bytes 2752520 | tf_op jit(solution)/shard_map/ppermute | solution.py:19
  128.1 9.9 %shard_map.47 = f32[2,256,448]{2,1,0:T(8,128)} custom-call(s32[3]{0:T(128)} %pad_add_fusion.at_ref, bf16[128,7168]{1,0:T(8,128)(2,1)} %copy-done.2, bf16[128,7168]{1,0:T(8,128)(2,1)} %collective-permute-done.9.refs_1_, bf16[448,7168]{1,0:T(8,128)(2,1)} %bitcast.35, bf16[448,7168]{1,0:T(8,128)(2,1)} %collective-permute-done.7.refs_2_.refs_3_), custom_call_target="tpu_custom_call" | custom-call | flops 3288334336 | bytes 17432576 | tf_op jit(solution)/shard_map/pallas_call | solution.py:48
  137.9 4.8 %all-to-all-start.1 = ((f32[8,64,448]{2,1,0:T(8,128)}), f32[8,64,448]{2,1,0:T(8,128)S(1)}, u32[]{:S(2)}, u32[]{:S(2)}) async-start(f32[8,64,448]{2,1,0:T(8,128)} %bitcast.37), calls=%async_computation.1 | async-start | bytes 2097152 | tf_op jit(solution)/shard_map/all_to_all | solution.py:66
  142.8 3.6 %collective-permute-done.10.refs_0_ = bf16[64,7168]{1,0:T(8,128)(2,1)} collective-permute-done((bf16[64,7168]{1,0:T(8,128)(2,1)S(1)}, bf16[64,7168]{1,0:T(8,128)(2,1)}, u32[]{:S(2)}, u32[]{:S(2)}) %collective-permute-start.10) | collective-permute-done | bytes 917536 | tf_op jit(solution)/shard_map/ppermute | solution.py:19
  146.4 1.7 collective-permute-done.11.refs_1_
  148.0 9.3 %shard_map.48 = f32[2,128,448]{2,1,0:T(8,128)} custom-call(s32[3]{0:T(128)} %pad_add_fusion.at_ref, bf16[64,7168]{1,0:T(8,128)(2,1)} %collective-permute-done.10.refs_0_, bf16[64,7168]{1,0:T(8,128)(2,1)} %collective-permute-done.11.refs_1_, bf16[448,7168]{1,0:T(8,128)(2,1)} %bitcast.36, bf16[448,7168]{1,0:T(8,128)(2,1)} %collective-permute-done.7.refs_2_.refs_3_), custom_call_target="tpu_custom_call" | custom-call | flops 1644167168 | bytes 15138816 | tf_op jit(solution)/shard_map/pallas_call | solution.py:48
  157.4 4.8 %all-to-all-start.5 = ((f32[8,32,448]{2,1,0:T(8,128)}), f32[8,32,448]{2,1,0:T(8,128)S(1)}, u32[]{:S(2)}, u32[]{:S(2)}) async-start(f32[8,32,448]{2,1,0:T(8,128)} %bitcast.40), calls=%async_computation.5 | async-start | bytes 1048576 | tf_op jit(solution)/shard_map/all_to_all | solution.py:66
  162.2 0.1 bitcast_reduce_fusion
  162.3 16.6 %all_gather.12.near_ref = bf16[768,448]{1,0:T(8,128)(2,1)S(1)} all-gather(bf16[192,448]{1,0:T(8,128)(2,1)S(1)} %pad_maximum_fusion), channel_id=1, replica_groups=mesh['y'=4,'z'=8,'core'=2,'x'=4] {'x'}, dimensions={0}, use_global_device_ids=true | all-gather | bytes 860160 | tf_op jit(solution)/shard_map/all_gather | solution.py:161
  178.9 0.1 collective-permute-start.12
  179.0 11.4 %all_to_all.63 = bf16[4,64,448]{2,1,0:T(8,128)(2,1)S(1)} all-to-all(bf16[4,64,448]{2,1,0:T(8,128)(2,1)S(1)} %broadcast_in_dim.5), channel_id=1, replica_groups=mesh['y'=4,'z'=8,'core'=2,'x'=4] {'x'}, dimensions={0} | all-to-all | bytes 458752 | tf_op jit(solution)/shard_map/all_to_all | solution.py:125
  190.4 1.6 copy-done
  192.0 7.2 %shard_map.49 = f32[448,2048]{1,0:T(8,128)} custom-call(s32[3]{0:T(128)S(1)} %copy-done.1, bf16[768,448]{1,0:T(8,128)(2,1)S(1)} %all_gather.12.near_ref, bf16[256,448]{1,0:T(8,128)(2,1)S(1)} %bitcast.32, bf16[8,4,128,256]{3,2,1,0:T(8,128)(2,1)S(1)} %bitcast.31, bf16[8,4,128,256]{3,2,1,0:T(8,128)(2,1)S(1)} %collective-permute-done.12.other_ref), custom_call_target="tpu_custom_call" | custom-call | flops 1879048192 | bytes 12058624 | tf_op jit(solution)/shard_map/pallas_call | solution.py:106
  (31 shorter events, 0.2 us)
Async XLA Ops:
  6.5 66.2 %all-gather.4.cloned.1.call-start = ((), (), s32[]{:S(2)}) async-start(), calls=%async_computation.7 | async-start | bytes 2359296 | tf_op jit(solution)/shard_map/all_gather | solution.py:137
  6.5 11.7 %collective-permute-start = (bf16[16,7168]{1,0:T(8,128)(2,1)}, bf16[16,7168]{1,0:T(8,128)(2,1)S(1)}, u32[]{:S(2)}, u32[]{:S(2)}) collective-permute-start(bf16[16,7168]{1,0:T(8,128)(2,1)} %param.5), channel_id=1, source_target_pairs={{0,8},{8,16},{16,24},{24,32},{32,40},{40,48},{48,56},{56,0},{1,9},... | collective-permute-start | bytes 688136 | tf_op jit(solution)/shard_map/ppermute | solution.py:19
  8.5 10.5 %collective-permute-start.4 = (bf16[16,7168]{1,0:T(8,128)(2,1)}, bf16[16,7168]{1,0:T(8,128)(2,1)S(1)}, u32[]{:S(2)}, u32[]{:S(2)}) collective-permute-start(bf16[16,7168]{1,0:T(8,128)(2,1)} %param.5), channel_id=1, source_target_pairs={{0,56},{8,0},{16,8},{24,16},{32,24},{40,32},{48,40},{56,48},{1,57}... | collective-permute-start | bytes 688136 | tf_op jit(solution)/shard_map/ppermute | solution.py:19
  12.4 47.0 %collective-permute-start.7 = (bf16[448,7168]{1,0:T(8,128)(2,1)}, bf16[448,7168]{1,0:T(8,128)(2,1)}, u32[]{:S(2)}, u32[]{:S(2)}) collective-permute-start(bf16[448,7168]{1,0:T(8,128)(2,1)} %bitcast.33), channel_id=1, source_target_pairs={{0,4},{4,0},{1,5},{5,1},{2,6},{6,2},{3,7},{7,3},{8,12},{12,8},{9,1... | collective-permute-start | bytes 19267592 | tf_op jit(solution)/shard_map/ppermute | solution.py:19
  12.4 36.7 %copy-start.4 = (bf16[128,2048]{1,0:T(8,128)(2,1)S(1)}, bf16[128,2048]{1,0:T(8,128)(2,1)}, u32[]{:S(2)}) copy-start(bf16[128,2048]{1,0:T(8,128)(2,1)} %param.6) | copy-start | bytes 1572868
  18.2 8.0 %collective-permute-start.1 = (bf16[16,7168]{1,0:T(8,128)(2,1)S(1)}, bf16[16,7168]{1,0:T(8,128)(2,1)S(1)}, u32[]{:S(2)}, u32[]{:S(2)}) collective-permute-start(bf16[16,7168]{1,0:T(8,128)(2,1)S(1)} %collective-permute-done), channel_id=1, source_target_pairs={{0,8},{8,16},{16,24},{24,32},{32,40},{40,48},{48,56},{56,0},{1,9},... | collective-permute-start | bytes 688136 | tf_op jit(solution)/shard_map/ppermute | solution.py:19
  18.9 10.7 %collective-permute-start.5 = (bf16[16,7168]{1,0:T(8,128)(2,1)S(1)}, bf16[16,7168]{1,0:T(8,128)(2,1)S(1)}, u32[]{:S(2)}, u32[]{:S(2)}) collective-permute-start(bf16[16,7168]{1,0:T(8,128)(2,1)S(1)} %collective-permute-done.4), channel_id=1, source_target_pairs={{0,56},{8,0},{16,8},{24,16},{32,24},{40,32},{48,40},{56,48},{1,57}... | collective-permute-start | bytes 688136 | tf_op jit(solution)/shard_map/ppermute | solution.py:19
  26.2 10.5 %collective-permute-start.2 = (bf16[16,7168]{1,0:T(8,128)(2,1)S(1)}, bf16[16,7168]{1,0:T(8,128)(2,1)S(1)}, u32[]{:S(2)}, u32[]{:S(2)}) collective-permute-start(bf16[16,7168]{1,0:T(8,128)(2,1)S(1)} %collective-permute-done.1), channel_id=1, source_target_pairs={{0,8},{8,16},{16,24},{24,32},{32,40},{40,48},{48,56},{56,0},{1,9},... | collective-permute-start | bytes 688136 | tf_op jit(solution)/shard_map/ppermute | solution.py:19
  29.6 17.4 %collective-permute-start.6 = (bf16[16,7168]{1,0:T(8,128)(2,1)S(1)}, bf16[16,7168]{1,0:T(8,128)(2,1)S(1)}, u32[]{:S(2)}, u32[]{:S(2)}) collective-permute-start(bf16[16,7168]{1,0:T(8,128)(2,1)S(1)} %collective-permute-done.5), channel_id=1, source_target_pairs={{0,56},{8,0},{16,8},{24,16},{32,24},{40,32},{48,40},{56,48},{1,57}... | collective-permute-start | bytes 688136 | tf_op jit(solution)/shard_map/ppermute | solution.py:19
  36.7 9.6 %collective-permute-start.3 = (bf16[16,7168]{1,0:T(8,128)(2,1)S(1)}, bf16[16,7168]{1,0:T(8,128)(2,1)S(1)}, u32[]{:S(2)}, u32[]{:S(2)}) collective-permute-start(bf16[16,7168]{1,0:T(8,128)(2,1)S(1)} %collective-permute-done.2), channel_id=1, source_target_pairs={{0,8},{8,16},{16,24},{24,32},{32,40},{40,48},{48,56},{56,0},{1,9},... | collective-permute-start | bytes 688136 | tf_op jit(solution)/shard_map/ppermute | solution.py:19
  50.0 22.7 %all-to-all-start.2 = ((bf16[128,8,256]{2,0,1:T(8,128)(2,1)}), bf16[128,8,256]{2,0,1:T(8,128)(2,1)S(1)}, u32[]{:S(2)}, u32[]{:S(2)}) async-start(bf16[128,8,256]{2,0,1:T(8,128)(2,1)} %bitcast.29), calls=%async_computation.2 | async-start | bytes 1048576 | tf_op jit(solution)/shard_map/all_to_all | solution.py:140
  55.6 54.8 %collective-permute-start.8 = (bf16[128,7168]{1,0:T(8,128)(2,1)}, bf16[128,7168]{1,0:T(8,128)(2,1)S(1)}, u32[]{:S(2)}, u32[]{:S(2)}) collective-permute-start(bf16[128,7168]{1,0:T(8,128)(2,1)} %constant_dynamic-update-slice_fusion.refs_0_), channel_id=1, source_target_pairs={{0,64},{64,128},{128,192},{192,0},{1,65},{65,129},{129,193},{193,1... | collective-permute-start | bytes 5505032 | tf_op jit(solution)/shard_map/ppermute | solution.py:19
  56.9 53.5 %collective-permute-start.9 = (bf16[128,7168]{1,0:T(8,128)(2,1)}, bf16[128,7168]{1,0:T(8,128)(2,1)}, u32[]{:S(2)}, u32[]{:S(2)}) collective-permute-start(bf16[128,7168]{1,0:T(8,128)(2,1)} %constant_dynamic-update-slice_fusion.refs_0_), channel_id=1, source_target_pairs={{0,192},{64,0},{128,64},{192,128},{1,193},{65,1},{129,65},{193,129... | collective-permute-start | bytes 5505032 | tf_op jit(solution)/shard_map/ppermute | solution.py:19
  106.3 10.8 %all-to-all-start.4 = ((bf16[4,128,256]{2,1,0:T(8,128)(2,1)}), bf16[4,128,256]{2,1,0:T(8,128)(2,1)S(1)}, u32[]{:S(2)}, u32[]{:S(2)}) async-start(bf16[4,128,256]{2,1,0:T(8,128)(2,1)} %broadcast_in_dim.4), calls=%async_computation.4 | async-start | bytes 524288 | tf_op jit(solution)/shard_map/all_to_all | solution.py:152
  110.3 68.5 %all-gather.6.cloned.1.call-start = ((), (), s32[]{:S(2)}) async-start(), calls=%async_computation.8 | async-start | bytes 2359296 | tf_op jit(solution)/shard_map/all_gather | solution.py:154
  110.4 15.1 %copy-start.2 = (bf16[128,7168]{1,0:T(8,128)(2,1)}, bf16[128,7168]{1,0:T(8,128)(2,1)S(1)}, u32[]{:S(2)}) copy-start(bf16[128,7168]{1,0:T(8,128)(2,1)S(1)} %collective-permute-done.8.refs_0_) | copy-start | bytes 5505028
  117.0 0.7 copy-start.3
  117.8 20.2 %all-to-all-start = ((f32[8,32,448]{2,1,0:T(8,128)}), f32[8,32,448]{2,1,0:T(8,128)S(1)}, u32[]{:S(2)}, u32[]{:S(2)}) async-start(f32[8,32,448]{2,1,0:T(8,128)} %bitcast.4), calls=%async_computation | async-start | bytes 1048576 | tf_op jit(solution)/shard_map/all_to_all | solution.py:66
  122.6 23.8 %collective-permute-start.10 = (bf16[64,7168]{1,0:T(8,128)(2,1)S(1)}, bf16[64,7168]{1,0:T(8,128)(2,1)}, u32[]{:S(2)}, u32[]{:S(2)}) collective-permute-start(bf16[64,7168]{1,0:T(8,128)(2,1)S(1)} %slice.8), channel_id=1, source_target_pairs={{0,64},{64,128},{128,192},{192,0},{1,65},{65,129},{129,193},{193,1... | collective-permute-start | bytes 2752520 | tf_op jit(solution)/shard_map/ppermute | solution.py:19
  125.4 22.6 %collective-permute-start.11 = (bf16[64,7168]{1,0:T(8,128)(2,1)}, bf16[64,7168]{1,0:T(8,128)(2,1)}, u32[]{:S(2)}, u32[]{:S(2)}) collective-permute-start(bf16[64,7168]{1,0:T(8,128)(2,1)} %slice.9), channel_id=1, source_target_pairs={{0,192},{64,0},{128,64},{192,128},{1,193},{65,1},{129,65},{193,129... | collective-permute-start | bytes 2752520 | tf_op jit(solution)/shard_map/ppermute | solution.py:19
  137.9 19.4 %all-to-all-start.1 = ((f32[8,64,448]{2,1,0:T(8,128)}), f32[8,64,448]{2,1,0:T(8,128)S(1)}, u32[]{:S(2)}, u32[]{:S(2)}) async-start(f32[8,64,448]{2,1,0:T(8,128)} %bitcast.37), calls=%async_computation.1 | async-start | bytes 2097152 | tf_op jit(solution)/shard_map/all_to_all | solution.py:66
  157.4 21.5 %all-to-all-start.5 = ((f32[8,32,448]{2,1,0:T(8,128)}), f32[8,32,448]{2,1,0:T(8,128)S(1)}, u32[]{:S(2)}, u32[]{:S(2)}) async-start(f32[8,32,448]{2,1,0:T(8,128)} %bitcast.40), calls=%async_computation.5 | async-start | bytes 1048576 | tf_op jit(solution)/shard_map/all_to_all | solution.py:66
  162.1 28.3 %copy-start.1 = (s32[3]{0:T(128)S(1)}, s32[3]{0:T(128)}, u32[]{:S(2)}) copy-start(s32[3]{0:T(128)} %pad_add_fusion.at_ref) | copy-start | bytes 40
  178.9 11.5 %collective-permute-start.12 = (bf16[8,4,128,256]{3,2,1,0:T(8,128)(2,1)}, bf16[8,4,128,256]{3,2,1,0:T(8,128)(2,1)S(1)}, u32[]{:S(2)}, u32[]{:S(2)}) collective-permute-start(bf16[8,4,128,256]{3,2,1,0:T(8,128)(2,1)} %bitcast.30), channel_id=1, source_target_pairs={{0,4},{4,0},{1,5},{5,1},{2,6},{6,2},{3,7},{7,3},{8,12},{12,8},{9,1... | collective-permute-start | bytes 6291464 | tf_op jit(solution)/shard_map/ppermute | solution.py:19
  190.4 1.6 copy-start
Sparse Core Ops, SparseCore 0:
  12.5 60.1 all-gather.3
  117.9 40.3 all-gather.5

commit v4 on v3

--- a/solution.py
+++ b/solution.py
@@ -113,7 +113,7 @@
             scratch_shapes=[pltpu.VMEM((tokens, cols), BF16), pltpu.VMEM((EXAMPLES, cols, T_EX), BF16)],
         ),
         out_shape=jax.ShapeDtypeStruct((cols, NZ * n_blk), F32),
-        compiler_params=pltpu.CompilerParams(vmem_limit_bytes=24 * 2**20),
+        compiler_params=pltpu.CompilerParams(vmem_limit_bytes=54 * 2**20),
         cost_estimate=pl.CostEstimate(
             flops=2 * tokens * cols * NZ * n_blk, bytes_accessed=4 * cols * NZ * n_blk + 4 * tokens * n_blk * NZ, transcendentals=0
         ),
@@ -136,12 +136,12 @@
     basis_other = shift(basis, "core", 1)
     rows = lax.all_gather(acts, "z", axis=1, tiled=True)
     load = jnp.concatenate(ring_z(grads), axis=0)
-    (act_basis,) = after([act_basis], load)
-    basis_acts = lax.all_to_all(act_basis, "z", 1, 0, tiled=True)
     h = load.shape[0] // 2
 
     below, above = shift(load, "y", 1), shift(load, "y", -1)
     product_load = product(at, [load], basis, basis_other)
+    (act_basis,) = after([act_basis], product_load)
+    basis_acts = lax.all_to_all(act_basis, "z", 1, 0, tiled=True)
     (rows,) = after([rows], load, product_load)
     partial = jnp.dot(rows, basis_acts, preferred_element_type=F32)
     terms = lax.all_to_all(partial, ("y", "core"), 0, 0, tiled=True)
@@ -150,7 +150,7 @@
     far = [shift(below[:h], "y", 1), shift(above[h:], "y", -1)]
     product_near = product(at, [below, above], basis, basis_other)
     along_y = lax.all_to_all(jnp.broadcast_to(piece[None], (NY,) + piece.shape), "y", 0, 0, tiled=True)
-    (along_y,) = after([along_y], below, above)
+    (along_y,) = after([along_y], product_near, *far)
     own = lax.all_gather(along_y, "z", axis=0)
     total_load = sum_over_x(product_load)
 

time: 208 us -> 215 us (1.034)
  waiting for transfers between devices: 39.3 us -> 58.9 us
  blocking collectives: 58.4 us -> 42.5 us
  Pallas kernels: 35.5 us -> 38.5 us
    all_to_all x1, blocking collectives: 30.5 us -> 13.1 us  [sum_over_x(): lax.all_to_all(partial.reshape(-1, cols), ('core', 'x'), 0, 0, tiled=True)]
    all_to_all x1, waiting for transfers between devices: 0.01 us -> 13.3 us  [body(): basis_acts = lax.all_to_all(act_basis, 'z', 1, 0, tiled=True)]
    all_to_all x0 -> x1, waiting for transfers between devices: none -> 9.71 us  [body(): terms = lax.all_to_all(partial, ('y', 'core'), 0, 0, tiled=True)]
    all_to_all x3 -> x2, starting transfers between devices: 14.4 us -> 9.37 us  [sum_over_x(): lax.all_to_all(partial.reshape(-1, cols), ('core', 'x'), 0, 0, tiled=True)]
    all_to_all x3 -> x2, waiting for transfers between devices: 0.01 us -> 4.76 us  [sum_over_x(): lax.all_to_all(partial.reshape(-1, cols), ('core', 'x'), 0, 0, tiled=True)]
    all_gather x1, waiting for transfers between devices: 4.19 us -> 0.01 us  [body(): rows = lax.all_gather(acts, 'z', axis=1, tiled=True)]
    all_to_all x1, waiting for transfers between devices: 6.65 us -> 2.72 us  [body(): lax.all_to_all(jnp.broadcast_to(piece[None], (NY,) + piece.shape), 'y', 0...]
    all_to_all x0 -> x1, starting transfers between devices: none -> 3.56 us  [body(): terms = lax.all_to_all(partial, ('y', 'core'), 0, 0, tiled=True)]
  transfers between devices with their start and end apart: 20 -> 20, of which waited for: 9 -> 11; matrix products, arithmetic and copies ran while one was open for 7% -> 7% of each run, Pallas kernels for 14% -> 13%
where the time goes in v4:
time: 215 us; the launch traced here: 213 us
  waiting for transfers between devices  58.9 us (27%)
  blocking collectives  42.5 us (20%)
  starting transfers between devices  41.4 us (19%)
  Pallas kernels  38.5 us (18%)
  local copies, waits for them, and re-layouts  13.6 us (6%)
  between operations  13.5 us (6%)
  matrix products  3.3 us (2%)
    ppermute x13, waiting for transfers between devices, shift(): return lax.ppermute(v, axis, [(i, (i + d) % n) for i in range(n)])  28.4 us
    pallas_call x3, Pallas kernels, product(): pl.pallas_call(product_kernel, grid_spec=pltpu.PrefetchScalarGridSpec(num...  28.3 us
    ppermute x13, starting transfers between devices, shift(): return lax.ppermute(v, axis, [(i, (i + d) % n) for i in range(n)])  19.4 us
    all_gather x1, blocking collectives, body(): lax.all_gather(jnp.concatenate([total_load, total_near], axis=0), 'x', ax...  17.3 us
    all_to_all x1, waiting for transfers between devices, body(): basis_acts = lax.all_to_all(act_basis, 'z', 1, 0, tiled=True)  13.3 us
    all_to_all x1, blocking collectives, sum_over_x(): lax.all_to_all(partial.reshape(-1, cols), ('core', 'x'), 0, 0, tiled=True)  13.1 us
    all_to_all x1, blocking collectives, gather_x(): lax.all_to_all(copies, 'x', 0, 0, tiled=True).reshape((-1,) + v.shape[1:])  12 us
    pallas_call x1, Pallas kernels, finish(): pl.pallas_call(finish_kernel, grid_spec=pltpu.PrefetchScalarGridSpec(num_...  10.1 us
  transfers between devices with their start and end apart: 20, of which 11 were waited for; matrix products, arithmetic and copies ran while one was open for 7% of the time, Pallas kernels for 13%

profile of v4, /device:TPU:2, one launch (start us, length us, event | category | flops | bytes accessed | tf_op | source)
XLA Modules:
  0.0 212.6 jit_solution(1351922592121463625)
XLA Ops:
  6.5 1.9 collective-permute-start
  8.5 3.9 %collective-permute-start.4 = (bf16[16,7168]{1,0:T(8,128)(2,1)}, bf16[16,7168]{1,0:T(8,128)(2,1)S(1)}, u32[]{:S(2)}, u32[]{:S(2)}) collective-permute-start(bf16[16,7168]{1,0:T(8,128)(2,1)} %param.5), channel_id=1, source_target_pairs={{0,56},{8,0},{16,8},{24,16},{32,24},{40,32},{48,40},{56,48},{1,57}... | collective-permute-start | bytes 688136 | tf_op jit(solution)/shard_map/ppermute | solution.py:19
  12.4 1.6 constant_dynamic-update-slice_fusion.7
  14.1 4.1 %collective-permute-done = bf16[16,7168]{1,0:T(8,128)(2,1)S(1)} collective-permute-done((bf16[16,7168]{1,0:T(8,128)(2,1)}, bf16[16,7168]{1,0:T(8,128)(2,1)S(1)}, u32[]{:S(2)}, u32[]{:S(2)}) %collective-permute-start) | collective-permute-done | bytes 229408 | tf_op jit(solution)/shard_map/ppermute | solution.py:19
  18.2 0.7 constant_dynamic-update-slice_fusion.6
  18.9 3.2 %collective-permute-start.5 = (bf16[16,7168]{1,0:T(8,128)(2,1)S(1)}, bf16[16,7168]{1,0:T(8,128)(2,1)S(1)}, u32[]{:S(2)}, u32[]{:S(2)}) collective-permute-start(bf16[16,7168]{1,0:T(8,128)(2,1)S(1)} %collective-permute-done.4), channel_id=1, source_target_pairs={{0,56},{8,0},{16,8},{24,16},{32,24},{40,32},{48,40},{56,48},{1,57}... | collective-permute-start | bytes 688136 | tf_op jit(solution)/shard_map/ppermute | solution.py:19
  22.1 4.1 %collective-permute-done.1 = bf16[16,7168]{1,0:T(8,128)(2,1)S(1)} collective-permute-done((bf16[16,7168]{1,0:T(8,128)(2,1)S(1)}, bf16[16,7168]{1,0:T(8,128)(2,1)S(1)}, u32[]{:S(2)}, u32[]{:S(2)}) %collective-permute-start.1) | collective-permute-done | bytes 229408 | tf_op jit(solution)/shard_map/ppermute | solution.py:19
  26.2 0.7 constant_dynamic-update-slice_fusion.5
  26.9 2.7 %collective-permute-done.5 = bf16[16,7168]{1,0:T(8,128)(2,1)S(1)} collective-permute-done((bf16[16,7168]{1,0:T(8,128)(2,1)S(1)}, bf16[16,7168]{1,0:T(8,128)(2,1)S(1)}, u32[]{:S(2)}, u32[]{:S(2)}) %collective-permute-start.5) | collective-permute-done | bytes 229408 | tf_op jit(solution)/shard_map/ppermute | solution.py:19
  29.6 3.7 %collective-permute-start.6 = (bf16[16,7168]{1,0:T(8,128)(2,1)S(1)}, bf16[16,7168]{1,0:T(8,128)(2,1)S(1)}, u32[]{:S(2)}, u32[]{:S(2)}) collective-permute-start(bf16[16,7168]{1,0:T(8,128)(2,1)S(1)} %collective-permute-done.5), channel_id=1, source_target_pairs={{0,56},{8,0},{16,8},{24,16},{32,24},{40,32},{48,40},{56,48},{1,57}... | collective-permute-start | bytes 688136 | tf_op jit(solution)/shard_map/ppermute | solution.py:19
  33.3 3.4 %collective-permute-done.2 = bf16[16,7168]{1,0:T(8,128)(2,1)S(1)} collective-permute-done((bf16[16,7168]{1,0:T(8,128)(2,1)S(1)}, bf16[16,7168]{1,0:T(8,128)(2,1)S(1)}, u32[]{:S(2)}, u32[]{:S(2)}) %collective-permute-start.2) | collective-permute-done | bytes 229408 | tf_op jit(solution)/shard_map/ppermute | solution.py:19
  36.8 0.7 constant_dynamic-update-slice_fusion.4
  37.5 8.9 %collective-permute-done.3 = bf16[16,7168]{1,0:T(8,128)(2,1)S(1)} collective-permute-done((bf16[16,7168]{1,0:T(8,128)(2,1)S(1)}, bf16[16,7168]{1,0:T(8,128)(2,1)S(1)}, u32[]{:S(2)}, u32[]{:S(2)}) %collective-permute-start.3) | collective-permute-done | bytes 229408 | tf_op jit(solution)/shard_map/ppermute | solution.py:19
  46.4 0.7 constant_dynamic-update-slice_fusion.3
  47.1 0.7 constant_dynamic-update-slice_fusion.2
  47.8 0.7 constant_dynamic-update-slice_fusion.1
  48.5 0.7 constant_dynamic-update-slice_fusion.refs_0_
  49.2 1.5 collective-permute-start.8
  50.6 1.8 collective-permute-start.9
  52.4 0.6 pad_add_fusion.at_ref
  53.0 9.3 %shard_map.46 = f32[2,128,448]{2,1,0:T(8,128)} custom-call(s32[3]{0:T(128)} %pad_add_fusion.at_ref, bf16[128,7168]{1,0:T(8,128)(2,1)} %constant_dynamic-update-slice_fusion.refs_0_, bf16[448,7168]{1,0:T(8,128)(2,1)} %bitcast.31, bf16[448,7168]{1,0:T(8,128)(2,1)} %collective-permute-done.7.refs_2_.refs_3_), custom_call_target="tpu_custom_call" | custom-call | flops 1644167168 | bytes 15138816 | tf_op jit(solution)/shard_map/pallas_call | solution.py:48
  62.3 0.8 copy.9
  63.1 5.5 %all-to-all-start.2 = ((bf16[128,8,256]{2,0,1:T(8,128)(2,1)}), bf16[128,8,256]{2,0,1:T(8,128)(2,1)S(1)}, u32[]{:S(2)}, u32[]{:S(2)}) async-start(bf16[128,8,256]{2,0,1:T(8,128)(2,1)} %bitcast.29), calls=%async_computation.2 | async-start | bytes 1048576 | tf_op jit(solution)/shard_map/all_to_all | solution.py:144
  68.7 13.3 %all-to-all-done.2 = bf16[128,8,256]{2,0,1:T(8,128)(2,1)S(1)} async-done(((bf16[128,8,256]{2,0,1:T(8,128)(2,1)}), bf16[128,8,256]{2,0,1:T(8,128)(2,1)S(1)}, u32[]{:S(2)}, u32[]{:S(2)}) %all-to-all-start.2) | async-done | bytes 524320 | tf_op jit(solution)/shard_map/all_to_all | solution.py:144
  81.9 3.3 %fusion = f32[8,128,256]{2,1,0:T(8,128)} fusion(bf16[8,128,1024]{2,1,0:T(8,128)(2,1)} %bitcast.37, bf16[1024,256,1]{1,0,2:T(8,128)(2,1)S(1)} %bitcast.40), kind=kOutput, calls=%fused_computation.14 | convolution fusion | flops 536870912 | bytes 3670016 | tf_op jit(solution)/shard_map/dot_general | solution.py:146
  85.2 3.6 %all-to-all-start.3 = ((f32[8,128,256]{2,1,0:T(8,128)}), f32[8,128,256]{2,1,0:T(8,128)S(1)}, u32[]{:S(2)}, u32[]{:S(2)}) async-start(f32[8,128,256]{2,1,0:T(8,128)} %fusion), calls=%async_computation.3 | async-start | bytes 2097152 | tf_op jit(solution)/shard_map/all_to_all | solution.py:147
  88.8 0.1 collective-permute-done.8.refs_0_
  88.9 1.1 slice.8
  90.1 1.8 collective-permute-start.10
  91.9 2.2 %slice.9 = bf16[64,7168]{1,0:T(8,128)(2,1)} slice(bf16[128,7168]{1,0:T(8,128)(2,1)} %collective-permute-done.9.refs_1_), slice={[64:128], [0:7168]} | slice | bytes 1835008 | tf_op jit(solution)/shard_map/slice | solution.py:150
  94.0 1.5 collective-permute-start.11
  95.5 9.7 %all-to-all-done.3 = f32[8,128,256]{2,1,0:T(8,128)S(1)} async-done(((f32[8,128,256]{2,1,0:T(8,128)}), f32[8,128,256]{2,1,0:T(8,128)S(1)}, u32[]{:S(2)}, u32[]{:S(2)}) %all-to-all-start.3) | async-done | bytes 1048608 | tf_op jit(solution)/shard_map/all_to_all | solution.py:147
  105.3 0.7 broadcast_in_dim.4
  106.0 3.4 %all-to-all-start.4 = ((bf16[4,128,256]{2,1,0:T(8,128)(2,1)}), bf16[4,128,256]{2,1,0:T(8,128)(2,1)S(1)}, u32[]{:S(2)}, u32[]{:S(2)}) async-start(bf16[4,128,256]{2,1,0:T(8,128)(2,1)} %broadcast_in_dim.4), calls=%async_computation.4 | async-start | bytes 524288 | tf_op jit(solution)/shard_map/all_to_all | solution.py:152
  109.4 0.2 all-gather.6.cloned.1.call-start
  109.6 9.8 %shard_map.47 = f32[2,256,448]{2,1,0:T(8,128)} custom-call(s32[3]{0:T(128)} %pad_add_fusion.at_ref, bf16[128,7168]{1,0:T(8,128)(2,1)} %copy-done, bf16[128,7168]{1,0:T(8,128)(2,1)} %collective-permute-done.9.refs_1_, bf16[448,7168]{1,0:T(8,128)(2,1)} %bitcast.32, bf16[448,7168]{1,0:T(8,128)(2,1)} %collective-permute-done.7.refs_2_.refs_3_), custom_call_target="tpu_custom_call" | custom-call | flops 3288334336 | bytes 17432576 | tf_op jit(solution)/shard_map/pallas_call | solution.py:48
  119.5 5.0 %collective-permute-done.10.refs_0_ = bf16[64,7168]{1,0:T(8,128)(2,1)} collective-permute-done((bf16[64,7168]{1,0:T(8,128)(2,1)}, bf16[64,7168]{1,0:T(8,128)(2,1)}, u32[]{:S(2)}, u32[]{:S(2)}) %collective-permute-start.10) | collective-permute-done | bytes 917536 | tf_op jit(solution)/shard_map/ppermute | solution.py:19
  124.5 2.7 %all-to-all-done.4 = bf16[4,128,256]{2,1,0:T(8,128)(2,1)S(1)} async-done(((bf16[4,128,256]{2,1,0:T(8,128)(2,1)}), bf16[4,128,256]{2,1,0:T(8,128)(2,1)S(1)}, u32[]{:S(2)}, u32[]{:S(2)}) %all-to-all-start.4) | async-done | bytes 262176 | tf_op jit(solution)/shard_map/all_to_all | solution.py:152
  127.2 0.7 copy-done.3
  127.9 13.1 %all_to_all.62 = f32[8,32,448]{2,1,0:T(8,128)S(1)} all-to-all(f32[8,32,448]{2,1,0:T(8,128)S(1)} %bitcast.38), channel_id=1, replica_groups=mesh['y'=4,'z'=8,'core'=2,'x'=4] {'core','x'}, dimensions={0} | all-to-all | bytes 917504 | tf_op jit(solution)/shard_map/all_to_all | solution.py:66
  141.1 4.7 %all-to-all-start.1 = ((f32[8,64,448]{2,1,0:T(8,128)}), f32[8,64,448]{2,1,0:T(8,128)S(1)}, u32[]{:S(2)}, u32[]{:S(2)}) async-start(f32[8,64,448]{2,1,0:T(8,128)} %bitcast.34), calls=%async_computation.1 | async-start | bytes 2097152 | tf_op jit(solution)/shard_map/all_to_all | solution.py:66
  145.8 9.3 %shard_map.48 = f32[2,128,448]{2,1,0:T(8,128)} custom-call(s32[3]{0:T(128)} %pad_add_fusion.at_ref, bf16[64,7168]{1,0:T(8,128)(2,1)} %collective-permute-done.10.refs_0_, bf16[64,7168]{1,0:T(8,128)(2,1)} %collective-permute-done.11.refs_1_, bf16[448,7168]{1,0:T(8,128)(2,1)} %bitcast.33, bf16[448,7168]{1,0:T(8,128)(2,1)} %collective-permute-done.7.refs_2_.refs_3_), custom_call_target="tpu_custom_call" | custom-call | flops 1644167168 | bytes 15138816 | tf_op jit(solution)/shard_map/pallas_call | solution.py:48
  155.1 4.8 %all-to-all-done.1 = f32[8,64,448]{2,1,0:T(8,128)S(1)} async-done(((f32[8,64,448]{2,1,0:T(8,128)}), f32[8,64,448]{2,1,0:T(8,128)S(1)}, u32[]{:S(2)}, u32[]{:S(2)}) %all-to-all-start.1) | async-done | bytes 917536 | tf_op jit(solution)/shard_map/all_to_all | solution.py:66
  159.8 4.7 %all-to-all-start.5 = ((f32[8,32,448]{2,1,0:T(8,128)}), f32[8,32,448]{2,1,0:T(8,128)S(1)}, u32[]{:S(2)}, u32[]{:S(2)}) async-start(f32[8,32,448]{2,1,0:T(8,128)} %bitcast.39), calls=%async_computation.5 | async-start | bytes 1048576 | tf_op jit(solution)/shard_map/all_to_all | solution.py:66
  164.6 17.3 %all_gather.12.near_ref = bf16[768,448]{1,0:T(8,128)(2,1)} all-gather(bf16[192,448]{1,0:T(8,128)(2,1)S(1)} %pad_maximum_fusion), channel_id=1, replica_groups=mesh['y'=4,'z'=8,'core'=2,'x'=4] {'x'}, dimensions={0}, use_global_device_ids=true | all-gather | bytes 860160 | tf_op jit(solution)/shard_map/all_gather | solution.py:161
  182.2 12.0 %all_to_all.63 = bf16[4,64,448]{2,1,0:T(8,128)(2,1)} all-to-all(bf16[4,64,448]{2,1,0:T(8,128)(2,1)S(1)} %broadcast_in_dim.5), channel_id=1, replica_groups=mesh['y'=4,'z'=8,'core'=2,'x'=4] {'x'}, dimensions={0} | all-to-all | bytes 458752 | tf_op jit(solution)/shard_map/all_to_all | solution.py:125
  194.2 1.4 copy-done.1
  195.6 10.1 %shard_map.49 = f32[448,2048]{1,0:T(8,128)} custom-call(s32[3]{0:T(128)} %pad_add_fusion.at_ref, bf16[768,448]{1,0:T(8,128)(2,1)} %all_gather.12.near_ref, bf16[256,448]{1,0:T(8,128)(2,1)} %bitcast.41, bf16[8,4,128,256]{3,2,1,0:T(8,128)(2,1)} %bitcast.36, bf16[8,4,128,256]{3,2,1,0:T(8,128)(2,1)} %copy-done.1), custom_call_target="tpu_custom_call" | custom-call | flops 1879048192 | bytes 12058624 | tf_op jit(solution)/shard_map/pallas_call | solution.py:106
  (31 shorter events, 0.5 us)
Async XLA Ops:
  6.5 62.1 %all-gather.4.cloned.1.call-start = ((), (), s32[]{:S(2)}) async-start(), calls=%async_computation.7 | async-start | bytes 2359296 | tf_op jit(solution)/shard_map/all_gather | solution.py:137
  6.5 11.7 %collective-permute-start = (bf16[16,7168]{1,0:T(8,128)(2,1)}, bf16[16,7168]{1,0:T(8,128)(2,1)S(1)}, u32[]{:S(2)}, u32[]{:S(2)}) collective-permute-start(bf16[16,7168]{1,0:T(8,128)(2,1)} %param.5), channel_id=1, source_target_pairs={{0,8},{8,16},{16,24},{24,32},{32,40},{40,48},{48,56},{56,0},{1,9},... | collective-permute-start | bytes 688136 | tf_op jit(solution)/shard_map/ppermute | solution.py:19
  8.5 10.5 %collective-permute-start.4 = (bf16[16,7168]{1,0:T(8,128)(2,1)}, bf16[16,7168]{1,0:T(8,128)(2,1)S(1)}, u32[]{:S(2)}, u32[]{:S(2)}) collective-permute-start(bf16[16,7168]{1,0:T(8,128)(2,1)} %param.5), channel_id=1, source_target_pairs={{0,56},{8,0},{16,8},{24,16},{32,24},{40,32},{48,40},{56,48},{1,57}... | collective-permute-start | bytes 688136 | tf_op jit(solution)/shard_map/ppermute | solution.py:19
  12.4 40.6 %collective-permute-start.7 = (bf16[448,7168]{1,0:T(8,128)(2,1)}, bf16[448,7168]{1,0:T(8,128)(2,1)}, u32[]{:S(2)}, u32[]{:S(2)}) collective-permute-start(bf16[448,7168]{1,0:T(8,128)(2,1)} %bitcast.30), channel_id=1, source_target_pairs={{0,4},{4,0},{1,5},{5,1},{2,6},{6,2},{3,7},{7,3},{8,12},{12,8},{9,1... | collective-permute-start | bytes 19267592 | tf_op jit(solution)/shard_map/ppermute | solution.py:19
  18.2 8.0 %collective-permute-start.1 = (bf16[16,7168]{1,0:T(8,128)(2,1)S(1)}, bf16[16,7168]{1,0:T(8,128)(2,1)S(1)}, u32[]{:S(2)}, u32[]{:S(2)}) collective-permute-start(bf16[16,7168]{1,0:T(8,128)(2,1)S(1)} %collective-permute-done), channel_id=1, source_target_pairs={{0,8},{8,16},{16,24},{24,32},{32,40},{40,48},{48,56},{56,0},{1,9},... | collective-permute-start | bytes 688136 | tf_op jit(solution)/shard_map/ppermute | solution.py:19
  18.9 10.7 %collective-permute-start.5 = (bf16[16,7168]{1,0:T(8,128)(2,1)S(1)}, bf16[16,7168]{1,0:T(8,128)(2,1)S(1)}, u32[]{:S(2)}, u32[]{:S(2)}) collective-permute-start(bf16[16,7168]{1,0:T(8,128)(2,1)S(1)} %collective-permute-done.4), channel_id=1, source_target_pairs={{0,56},{8,0},{16,8},{24,16},{32,24},{40,32},{48,40},{56,48},{1,57}... | collective-permute-start | bytes 688136 | tf_op jit(solution)/shard_map/ppermute | solution.py:19
  26.2 10.5 %collective-permute-start.2 = (bf16[16,7168]{1,0:T(8,128)(2,1)S(1)}, bf16[16,7168]{1,0:T(8,128)(2,1)S(1)}, u32[]{:S(2)}, u32[]{:S(2)}) collective-permute-start(bf16[16,7168]{1,0:T(8,128)(2,1)S(1)} %collective-permute-done.1), channel_id=1, source_target_pairs={{0,8},{8,16},{16,24},{24,32},{32,40},{40,48},{48,56},{56,0},{1,9},... | collective-permute-start | bytes 688136 | tf_op jit(solution)/shard_map/ppermute | solution.py:19
  29.6 17.4 %collective-permute-start.6 = (bf16[16,7168]{1,0:T(8,128)(2,1)S(1)}, bf16[16,7168]{1,0:T(8,128)(2,1)S(1)}, u32[]{:S(2)}, u32[]{:S(2)}) collective-permute-start(bf16[16,7168]{1,0:T(8,128)(2,1)S(1)} %collective-permute-done.5), channel_id=1, source_target_pairs={{0,56},{8,0},{16,8},{24,16},{32,24},{40,32},{48,40},{56,48},{1,57}... | collective-permute-start | bytes 688136 | tf_op jit(solution)/shard_map/ppermute | solution.py:19
  36.7 9.6 %collective-permute-start.3 = (bf16[16,7168]{1,0:T(8,128)(2,1)S(1)}, bf16[16,7168]{1,0:T(8,128)(2,1)S(1)}, u32[]{:S(2)}, u32[]{:S(2)}) collective-permute-start(bf16[16,7168]{1,0:T(8,128)(2,1)S(1)} %collective-permute-done.2), channel_id=1, source_target_pairs={{0,8},{8,16},{16,24},{24,32},{32,40},{40,48},{48,56},{56,0},{1,9},... | collective-permute-start | bytes 688136 | tf_op jit(solution)/shard_map/ppermute | solution.py:19
  49.2 39.8 %collective-permute-start.8 = (bf16[128,7168]{1,0:T(8,128)(2,1)}, bf16[128,7168]{1,0:T(8,128)(2,1)S(1)}, u32[]{:S(2)}, u32[]{:S(2)}) collective-permute-start(bf16[128,7168]{1,0:T(8,128)(2,1)} %constant_dynamic-update-slice_fusion.refs_0_), channel_id=1, source_target_pairs={{0,64},{64,128},{128,192},{192,0},{1,65},{65,129},{129,193},{193,1... | collective-permute-start | bytes 5505032 | tf_op jit(solution)/shard_map/ppermute | solution.py:19
  50.6 41.2 %collective-permute-start.9 = (bf16[128,7168]{1,0:T(8,128)(2,1)}, bf16[128,7168]{1,0:T(8,128)(2,1)}, u32[]{:S(2)}, u32[]{:S(2)}) collective-permute-start(bf16[128,7168]{1,0:T(8,128)(2,1)} %constant_dynamic-update-slice_fusion.refs_0_), channel_id=1, source_target_pairs={{0,192},{64,0},{128,64},{192,128},{1,193},{65,1},{129,65},{193,129... | collective-permute-start | bytes 5505032 | tf_op jit(solution)/shard_map/ppermute | solution.py:19
  53.0 9.3 %copy-start.4 = (bf16[128,2048]{1,0:T(8,128)(2,1)S(1)}, bf16[128,2048]{1,0:T(8,128)(2,1)}, u32[]{:S(2)}) copy-start(bf16[128,2048]{1,0:T(8,128)(2,1)} %param.6) | copy-start | bytes 1572868
  63.1 18.8 %all-to-all-start.2 = ((bf16[128,8,256]{2,0,1:T(8,128)(2,1)}), bf16[128,8,256]{2,0,1:T(8,128)(2,1)S(1)}, u32[]{:S(2)}, u32[]{:S(2)}) async-start(bf16[128,8,256]{2,0,1:T(8,128)(2,1)} %bitcast.29), calls=%async_computation.2 | async-start | bytes 1048576 | tf_op jit(solution)/shard_map/all_to_all | solution.py:144
  85.2 20.0 %all-to-all-start.3 = ((f32[8,128,256]{2,1,0:T(8,128)}), f32[8,128,256]{2,1,0:T(8,128)S(1)}, u32[]{:S(2)}, u32[]{:S(2)}) async-start(f32[8,128,256]{2,1,0:T(8,128)} %fusion), calls=%async_computation.3 | async-start | bytes 2097152 | tf_op jit(solution)/shard_map/all_to_all | solution.py:147
  88.9 5.1 %copy-start = (bf16[128,7168]{1,0:T(8,128)(2,1)}, bf16[128,7168]{1,0:T(8,128)(2,1)S(1)}, u32[]{:S(2)}) copy-start(bf16[128,7168]{1,0:T(8,128)(2,1)S(1)} %collective-permute-done.8.refs_0_) | copy-start | bytes 5505028
  90.1 34.4 %collective-permute-start.10 = (bf16[64,7168]{1,0:T(8,128)(2,1)}, bf16[64,7168]{1,0:T(8,128)(2,1)}, u32[]{:S(2)}, u32[]{:S(2)}) collective-permute-start(bf16[64,7168]{1,0:T(8,128)(2,1)} %slice.8), channel_id=1, source_target_pairs={{0,64},{64,128},{128,192},{192,0},{1,65},{65,129},{129,193},{193,1... | collective-permute-start | bytes 2752520 | tf_op jit(solution)/shard_map/ppermute | solution.py:19
  94.0 30.4 %collective-permute-start.11 = (bf16[64,7168]{1,0:T(8,128)(2,1)}, bf16[64,7168]{1,0:T(8,128)(2,1)}, u32[]{:S(2)}, u32[]{:S(2)}) collective-permute-start(bf16[64,7168]{1,0:T(8,128)(2,1)} %slice.9), channel_id=1, source_target_pairs={{0,192},{64,0},{128,64},{192,128},{1,193},{65,1},{129,65},{193,129... | collective-permute-start | bytes 2752520 | tf_op jit(solution)/shard_map/ppermute | solution.py:19
  106.0 21.2 %all-to-all-start.4 = ((bf16[4,128,256]{2,1,0:T(8,128)(2,1)}), bf16[4,128,256]{2,1,0:T(8,128)(2,1)S(1)}, u32[]{:S(2)}, u32[]{:S(2)}) async-start(bf16[4,128,256]{2,1,0:T(8,128)(2,1)} %broadcast_in_dim.4), calls=%async_computation.4 | async-start | bytes 524288 | tf_op jit(solution)/shard_map/all_to_all | solution.py:152
  109.4 18.5 %copy-start.2 = (f32[2,128,448]{2,1,0:T(8,128)S(1)}, f32[2,128,448]{2,1,0:T(8,128)}, u32[]{:S(2)}) copy-start(f32[2,128,448]{2,1,0:T(8,128)} %shard_map.46) | copy-start | bytes 1376260
  109.4 72.6 %all-gather.6.cloned.1.call-start = ((), (), s32[]{:S(2)}) async-start(), calls=%async_computation.8 | async-start | bytes 2359296 | tf_op jit(solution)/shard_map/all_gather | solution.py:154
  127.2 0.7 copy-start.3
  141.1 18.7 %all-to-all-start.1 = ((f32[8,64,448]{2,1,0:T(8,128)}), f32[8,64,448]{2,1,0:T(8,128)S(1)}, u32[]{:S(2)}, u32[]{:S(2)}) async-start(f32[8,64,448]{2,1,0:T(8,128)} %bitcast.34), calls=%async_computation.1 | async-start | bytes 2097152 | tf_op jit(solution)/shard_map/all_to_all | solution.py:66
  159.8 22.1 %all-to-all-start.5 = ((f32[8,32,448]{2,1,0:T(8,128)}), f32[8,32,448]{2,1,0:T(8,128)S(1)}, u32[]{:S(2)}, u32[]{:S(2)}) async-start(f32[8,32,448]{2,1,0:T(8,128)} %bitcast.39), calls=%async_computation.5 | async-start | bytes 1048576 | tf_op jit(solution)/shard_map/all_to_all | solution.py:66
  182.0 12.2 %collective-permute-start.12 = (bf16[8,4,128,256]{3,2,1,0:T(8,128)(2,1)}, bf16[8,4,128,256]{3,2,1,0:T(8,128)(2,1)S(1)}, u32[]{:S(2)}, u32[]{:S(2)}) collective-permute-start(bf16[8,4,128,256]{3,2,1,0:T(8,128)(2,1)} %bitcast.35), channel_id=1, source_target_pairs={{0,4},{4,0},{1,5},{5,1},{2,6},{6,2},{3,7},{7,3},{8,12},{12,8},{9,1... | collective-permute-start | bytes 6291464 | tf_op jit(solution)/shard_map/ppermute | solution.py:19
  194.2 1.4 copy-start.1
Sparse Core Ops, SparseCore 0:
  12.5 54.2 all-gather.3
  128.1 35.5 all-gather.5

commit v5 on v4

--- a/solution.py
+++ b/solution.py
@@ -68,23 +68,23 @@
     return total.reshape(-1, cols)
 
 
-def finish_kernel(at_ref, near_ref, far_ref, own_ref, other_ref, o_ref, rows, turned):
+def finish_kernel(at_ref, g_ref, own_ref, other_ref, o_ref, rows, turned):
     y, z, c = at_ref[0], at_ref[1], at_ref[2]
 
     @pl.when(pl.program_id(0) == 0)
     def _():
-        chunks = ((near_ref, 0, (0,)), (near_ref, NZ * NC // NX, (-1, 1)), (far_ref, 0, (2,)))
-        for ref, skip, y_steps in chunks:
-            each = len(y_steps) * NZ // NX
-            stride = ref.shape[0] // (NX * ROWS)
+        stride = g_ref.shape[0] // (NX * ROWS)
+        one = NZ // NX
+        for skip, y_steps in ((0, (0,)), (one, (-1, 1)), (3 * one, (2,))):
+            each = len(y_steps) * one
             for j in range(NX * NC * each):
                 slot, s = j // (NC * each), (j // each) % NC
-                i = slot * stride + skip + s * each + j % each
+                i = slot * stride + s * NY * one + skip + j % each
                 block = slot * each + j % each
                 y_at = lax.rem(y + (y_steps[block // NZ] + NY), NY)
                 z_at = lax.rem(z + (NZ - block % NZ), NZ)
                 to = pl.multiple_of(((y_at * NZ + z_at) * NC + s) * ROWS, ROWS)
-                rows[pl.ds(to, ROWS), :] = ref[i * ROWS : (i + 1) * ROWS, :]
+                rows[pl.ds(to, ROWS), :] = g_ref[i * ROWS : (i + 1) * ROWS, :]
         for e in range(EXAMPLES):
             turned[e] = rows[e * T_EX : (e + 1) * T_EX, :].T
 
@@ -99,8 +99,8 @@
         o_ref[...] = r
 
 
-def finish(at, g_parts, own, other):
-    tokens, cols = sum(g.shape[0] for g in g_parts), g_parts[0].shape[1]
+def finish(at, g_all, own, other):
+    tokens, cols = g_all.shape
     n_blk = own.shape[3]
     spec_a = pl.BlockSpec((1, NY, T_EX, n_blk), lambda j, t: (j, 0, 0, 0))
     return pl.pallas_call(
@@ -108,21 +108,16 @@
         grid_spec=pltpu.PrefetchScalarGridSpec(
             num_scalar_prefetch=1,
             grid=(NZ,),
-            in_specs=[pl.BlockSpec(g.shape, lambda j, t: (0, 0)) for g in g_parts] + [spec_a, spec_a],
+            in_specs=[pl.BlockSpec((tokens, cols), lambda j, t: (0, 0)), spec_a, spec_a],
             out_specs=pl.BlockSpec((cols, n_blk), lambda j, t: (0, j)),
             scratch_shapes=[pltpu.VMEM((tokens, cols), BF16), pltpu.VMEM((EXAMPLES, cols, T_EX), BF16)],
         ),
         out_shape=jax.ShapeDtypeStruct((cols, NZ * n_blk), F32),
-        compiler_params=pltpu.CompilerParams(vmem_limit_bytes=54 * 2**20),
+        compiler_params=pltpu.CompilerParams(vmem_limit_bytes=24 * 2**20),
         cost_estimate=pl.CostEstimate(
             flops=2 * tokens * cols * NZ * n_blk, bytes_accessed=4 * cols * NZ * n_blk + 4 * tokens * n_blk * NZ, transcendentals=0
         ),
-    )(at, *g_parts, own, other)
-
-
-def gather_x(v):
-    copies = jnp.broadcast_to(v[None], (NX,) + v.shape)
-    return lax.all_to_all(copies, "x", 0, 0, tiled=True).reshape((-1,) + v.shape[1:])
+    )(at, g_all, own, other)
 
 
 def after(values, *others):
@@ -152,17 +147,14 @@
     along_y = lax.all_to_all(jnp.broadcast_to(piece[None], (NY,) + piece.shape), "y", 0, 0, tiled=True)
     (along_y,) = after([along_y], product_near, *far)
     own = lax.all_gather(along_y, "z", axis=0)
-    total_load = sum_over_x(product_load)
 
-    far = after(far, product_near, along_y, total_load)
-    product_far = product(at, far, basis, basis_other)
-    total_far = sum_over_x(product_far)
-    total_near = sum_over_x(product_near)
-    g_load = lax.all_gather(jnp.concatenate([total_load, total_near], axis=0), "x", axis=0, tiled=True)
-    (total_far,) = after([total_far], g_load)
-    (own,) = after([own], total_far)
-    g_far = gather_x(total_far)
-    return finish(at, [g_load, g_far], own, shift(own, "core", 1))
+    cols = product_near.shape[2]
+    far = after(far, product_near, along_y)
+    chunks = (product_load, product_near, product(at, far, basis, basis_other))
+    total = sum_over_x(jnp.concatenate([p.reshape(NC * NX, -1, cols) for p in chunks], axis=1))
+    (own,) = after([own], total)
+    g_all = lax.all_gather(total, "x", axis=0, tiled=True)
+    return finish(at, g_all, own, shift(own, "core", 1))
 
 
 def solution(mesh):

time: 215 us -> 206 us (0.958)
  starting transfers between devices: 41.4 us -> 32.2 us
  local copies, waits for them, and re-layouts: 13.6 us -> 20.4 us
  waiting for transfers between devices: 58.9 us -> 54.1 us
  other arithmetic: 0.87 us -> 3.9 us
  Pallas kernels: 38.5 us -> 35.6 us
    all_to_all x1, blocking collectives: 13.1 us -> 27.2 us  [sum_over_x(): lax.all_to_all(partial.reshape(-1, cols), ('core', 'x'), 0, 0, tiled=True)]
    all_to_all x1 -> x0, blocking collectives: 12 us -> none  [gather_x(): lax.all_to_all(copies, 'x', 0, 0, tiled=True).reshape((-1,) + v.shape[1:])]
    all_to_all x2 -> x0, starting transfers between devices: 9.37 us -> none  [sum_over_x(): lax.all_to_all(partial.reshape(-1, cols), ('core', 'x'), 0, 0, tiled=True)]
    reshape x0 -> x3, local copies, waits for them, and re-layouts: none -> 6.45 us  [body(): p.reshape(NC * NX, -1, cols)]
    all_to_all x2 -> x0, waiting for transfers between devices: 4.76 us -> none  [sum_over_x(): lax.all_to_all(partial.reshape(-1, cols), ('core', 'x'), 0, 0, tiled=True)]
    concatenate x1, other arithmetic: 0.02 us -> 3.1 us  [body(): jnp.concatenate([p.reshape(NC * NX, -1, cols) for p in chunks], axis=1)]
    pallas_call x1, Pallas kernels: 10.1 us -> 7.24 us  [finish(): pl.pallas_call(finish_kernel, grid_spec=pltpu.PrefetchScalarGridSpec(num_...]
    all_gather x1, blocking collectives: 17.3 us -> 15.1 us  [body(): g_all = lax.all_gather(total, 'x', axis=0, tiled=True)]
  transfers between devices with their start and end apart: 20 -> 18, of which waited for: 11 -> 10; matrix products, arithmetic and copies ran while one was open for 7% -> 12% of each run, Pallas kernels for 13% -> 14%
where the time goes in v5:
time: 206 us; the launch traced here: 205 us
  waiting for transfers between devices  54.1 us (26%)
  blocking collectives  42.3 us (21%)
  Pallas kernels  35.6 us (17%)
  starting transfers between devices  32.2 us (16%)
  local copies, waits for them, and re-layouts  20.4 us (10%)
  between operations  13.5 us (7%)
  other arithmetic  3.9 us (2%)
  matrix products  3.29 us (2%)
    ppermute x13, waiting for transfers between devices, shift(): return lax.ppermute(v, axis, [(i, (i + d) % n) for i in range(n)])  28.4 us
    pallas_call x3, Pallas kernels, product(): pl.pallas_call(product_kernel, grid_spec=pltpu.PrefetchScalarGridSpec(num...  28.4 us
    all_to_all x1, blocking collectives, sum_over_x(): lax.all_to_all(partial.reshape(-1, cols), ('core', 'x'), 0, 0, tiled=True)  27.2 us
    ppermute x13, starting transfers between devices, shift(): return lax.ppermute(v, axis, [(i, (i + d) % n) for i in range(n)])  19.5 us
    all_gather x1, blocking collectives, body(): g_all = lax.all_gather(total, 'x', axis=0, tiled=True)  15.1 us
    all_to_all x1, waiting for transfers between devices, body(): basis_acts = lax.all_to_all(act_basis, 'z', 1, 0, tiled=True)  13.3 us
    all_to_all x1, waiting for transfers between devices, body(): terms = lax.all_to_all(partial, ('y', 'core'), 0, 0, tiled=True)  9.69 us
    unnamed x19, local copies, waits for them, and re-layouts  8.18 us
  transfers between devices with their start and end apart: 18, of which 10 were waited for; matrix products, arithmetic and copies ran while one was open for 12% of the time, Pallas kernels for 14%

profile of v5, /device:TPU:2, one launch (start us, length us, event | category | flops | bytes accessed | tf_op | source)
XLA Modules:
  0.0 205.3 jit_solution(13834471009502874100)
XLA Ops:
  6.5 1.9 collective-permute-start
  8.5 3.9 %collective-permute-start.4 = (bf16[16,7168]{1,0:T(8,128)(2,1)}, bf16[16,7168]{1,0:T(8,128)(2,1)S(1)}, u32[]{:S(2)}, u32[]{:S(2)}) collective-permute-start(bf16[16,7168]{1,0:T(8,128)(2,1)} %param.5), channel_id=1, source_target_pairs={{0,56},{8,0},{16,8},{24,16},{32,24},{40,32},{48,40},{56,48},{1,57}... | collective-permute-start | bytes 688136 | tf_op jit(solution)/shard_map/ppermute | solution.py:19
  12.4 1.6 constant_dynamic-update-slice_fusion.7
  14.1 4.1 %collective-permute-done = bf16[16,7168]{1,0:T(8,128)(2,1)S(1)} collective-permute-done((bf16[16,7168]{1,0:T(8,128)(2,1)}, bf16[16,7168]{1,0:T(8,128)(2,1)S(1)}, u32[]{:S(2)}, u32[]{:S(2)}) %collective-permute-start) | collective-permute-done | bytes 229408 | tf_op jit(solution)/shard_map/ppermute | solution.py:19
  18.2 0.7 constant_dynamic-update-slice_fusion.6
  18.9 3.2 %collective-permute-start.5 = (bf16[16,7168]{1,0:T(8,128)(2,1)S(1)}, bf16[16,7168]{1,0:T(8,128)(2,1)S(1)}, u32[]{:S(2)}, u32[]{:S(2)}) collective-permute-start(bf16[16,7168]{1,0:T(8,128)(2,1)S(1)} %collective-permute-done.4), channel_id=1, source_target_pairs={{0,56},{8,0},{16,8},{24,16},{32,24},{40,32},{48,40},{56,48},{1,57}... | collective-permute-start | bytes 688136 | tf_op jit(solution)/shard_map/ppermute | solution.py:19
  22.1 4.1 %collective-permute-done.1 = bf16[16,7168]{1,0:T(8,128)(2,1)S(1)} collective-permute-done((bf16[16,7168]{1,0:T(8,128)(2,1)S(1)}, bf16[16,7168]{1,0:T(8,128)(2,1)S(1)}, u32[]{:S(2)}, u32[]{:S(2)}) %collective-permute-start.1) | collective-permute-done | bytes 229408 | tf_op jit(solution)/shard_map/ppermute | solution.py:19
  26.2 0.7 constant_dynamic-update-slice_fusion.5
  26.9 2.7 %collective-permute-done.5 = bf16[16,7168]{1,0:T(8,128)(2,1)S(1)} collective-permute-done((bf16[16,7168]{1,0:T(8,128)(2,1)S(1)}, bf16[16,7168]{1,0:T(8,128)(2,1)S(1)}, u32[]{:S(2)}, u32[]{:S(2)}) %collective-permute-start.5) | collective-permute-done | bytes 229408 | tf_op jit(solution)/shard_map/ppermute | solution.py:19
  29.6 3.7 %collective-permute-start.6 = (bf16[16,7168]{1,0:T(8,128)(2,1)S(1)}, bf16[16,7168]{1,0:T(8,128)(2,1)S(1)}, u32[]{:S(2)}, u32[]{:S(2)}) collective-permute-start(bf16[16,7168]{1,0:T(8,128)(2,1)S(1)} %collective-permute-done.5), channel_id=1, source_target_pairs={{0,56},{8,0},{16,8},{24,16},{32,24},{40,32},{48,40},{56,48},{1,57}... | collective-permute-start | bytes 688136 | tf_op jit(solution)/shard_map/ppermute | solution.py:19
  33.3 3.4 %collective-permute-done.2 = bf16[16,7168]{1,0:T(8,128)(2,1)S(1)} collective-permute-done((bf16[16,7168]{1,0:T(8,128)(2,1)S(1)}, bf16[16,7168]{1,0:T(8,128)(2,1)S(1)}, u32[]{:S(2)}, u32[]{:S(2)}) %collective-permute-start.2) | collective-permute-done | bytes 229408 | tf_op jit(solution)/shard_map/ppermute | solution.py:19
  36.8 0.7 constant_dynamic-update-slice_fusion.4
  37.5 8.9 %collective-permute-done.3 = bf16[16,7168]{1,0:T(8,128)(2,1)S(1)} collective-permute-done((bf16[16,7168]{1,0:T(8,128)(2,1)S(1)}, bf16[16,7168]{1,0:T(8,128)(2,1)S(1)}, u32[]{:S(2)}, u32[]{:S(2)}) %collective-permute-start.3) | collective-permute-done | bytes 229408 | tf_op jit(solution)/shard_map/ppermute | solution.py:19
  46.4 0.7 constant_dynamic-update-slice_fusion.3
  47.1 0.7 constant_dynamic-update-slice_fusion.2
  47.8 0.7 constant_dynamic-update-slice_fusion.1
  48.5 0.7 constant_dynamic-update-slice_fusion.refs_0_
  49.2 1.5 collective-permute-start.8
  50.6 1.8 collective-permute-start.9
  52.4 0.6 pad_add_fusion.at_ref
  53.1 9.3 %shard_map.46 = f32[2,128,448]{2,1,0:T(8,128)} custom-call(s32[3]{0:T(128)} %pad_add_fusion.at_ref, bf16[128,7168]{1,0:T(8,128)(2,1)} %constant_dynamic-update-slice_fusion.refs_0_, bf16[448,7168]{1,0:T(8,128)(2,1)} %bitcast.26, bf16[448,7168]{1,0:T(8,128)(2,1)} %collective-permute-done.7.refs_2_.refs_3_), custom_call_target="tpu_custom_call" | custom-call | flops 1644167168 | bytes 15138816 | tf_op jit(solution)/shard_map/pallas_call | solution.py:48
  62.3 0.8 copy.17
  63.2 5.5 %all-to-all-start = ((bf16[128,8,256]{2,0,1:T(8,128)(2,1)}), bf16[128,8,256]{2,0,1:T(8,128)(2,1)S(1)}, u32[]{:S(2)}, u32[]{:S(2)}) async-start(bf16[128,8,256]{2,0,1:T(8,128)(2,1)} %bitcast.22), calls=%async_computation | async-start | bytes 1048576 | tf_op jit(solution)/shard_map/all_to_all | solution.py:139
  68.7 13.3 %all-to-all-done = bf16[128,8,256]{2,0,1:T(8,128)(2,1)S(1)} async-done(((bf16[128,8,256]{2,0,1:T(8,128)(2,1)}), bf16[128,8,256]{2,0,1:T(8,128)(2,1)S(1)}, u32[]{:S(2)}, u32[]{:S(2)}) %all-to-all-start) | async-done | bytes 524320 | tf_op jit(solution)/shard_map/all_to_all | solution.py:139
  82.0 3.3 %fusion = f32[8,128,256]{2,1,0:T(8,128)} fusion(bf16[8,128,1024]{2,1,0:T(8,128)(2,1)} %bitcast.30, bf16[1024,256,1]{1,0,2:T(8,128)(2,1)S(1)} %bitcast.31), kind=kOutput, calls=%fused_computation.12 | convolution fusion | flops 536870912 | bytes 3670016 | tf_op jit(solution)/shard_map/dot_general | solution.py:141
  85.2 3.6 %all-to-all-start.1 = ((f32[8,128,256]{2,1,0:T(8,128)}), f32[8,128,256]{2,1,0:T(8,128)S(1)}, u32[]{:S(2)}, u32[]{:S(2)}) async-start(f32[8,128,256]{2,1,0:T(8,128)} %fusion), calls=%async_computation.1 | async-start | bytes 2097152 | tf_op jit(solution)/shard_map/all_to_all | solution.py:142
  88.9 1.1 slice.8
  90.1 1.8 collective-permute-start.10
  91.9 2.2 %slice.9 = bf16[64,7168]{1,0:T(8,128)(2,1)} slice(bf16[128,7168]{1,0:T(8,128)(2,1)} %collective-permute-done.9.refs_1_), slice={[64:128], [0:7168]} | slice | bytes 1835008 | tf_op jit(solution)/shard_map/slice | solution.py:145
  94.1 1.4 collective-permute-start.11
  95.5 9.7 %all-to-all-done.1 = f32[8,128,256]{2,1,0:T(8,128)S(1)} async-done(((f32[8,128,256]{2,1,0:T(8,128)}), f32[8,128,256]{2,1,0:T(8,128)S(1)}, u32[]{:S(2)}, u32[]{:S(2)}) %all-to-all-start.1) | async-done | bytes 1048608 | tf_op jit(solution)/shard_map/all_to_all | solution.py:142
  105.3 0.7 broadcast_in_dim.2
  106.0 3.4 %all-to-all-start.2 = ((bf16[4,128,256]{2,1,0:T(8,128)(2,1)}), bf16[4,128,256]{2,1,0:T(8,128)(2,1)S(1)}, u32[]{:S(2)}, u32[]{:S(2)}) async-start(bf16[4,128,256]{2,1,0:T(8,128)(2,1)} %broadcast_in_dim.2), calls=%async_computation.2 | async-start | bytes 524288 | tf_op jit(solution)/shard_map/all_to_all | solution.py:147
  109.4 0.2 all-gather.6.cloned.1.call-start
  109.7 9.8 %shard_map.47 = f32[2,256,448]{2,1,0:T(8,128)} custom-call(s32[3]{0:T(128)} %pad_add_fusion.at_ref, bf16[128,7168]{1,0:T(8,128)(2,1)} %copy-done.2, bf16[128,7168]{1,0:T(8,128)(2,1)} %collective-permute-done.9.refs_1_, bf16[448,7168]{1,0:T(8,128)(2,1)} %bitcast.27, bf16[448,7168]{1,0:T(8,128)(2,1)} %collective-permute-done.7.refs_2_.refs_3_), custom_call_target="tpu_custom_call" | custom-call | flops 3288334336 | bytes 17432576 | tf_op jit(solution)/shard_map/pallas_call | solution.py:48
  119.5 5.0 %collective-permute-done.10.refs_0_ = bf16[64,7168]{1,0:T(8,128)(2,1)} collective-permute-done((bf16[64,7168]{1,0:T(8,128)(2,1)}, bf16[64,7168]{1,0:T(8,128)(2,1)}, u32[]{:S(2)}, u32[]{:S(2)}) %collective-permute-start.10) | collective-permute-done | bytes 917536 | tf_op jit(solution)/shard_map/ppermute | solution.py:19
  124.5 2.7 %all-to-all-done.2 = bf16[4,128,256]{2,1,0:T(8,128)(2,1)S(1)} async-done(((bf16[4,128,256]{2,1,0:T(8,128)(2,1)}), bf16[4,128,256]{2,1,0:T(8,128)(2,1)S(1)}, u32[]{:S(2)}, u32[]{:S(2)}) %all-to-all-start.2) | async-done | bytes 262176 | tf_op jit(solution)/shard_map/all_to_all | solution.py:147
  127.2 0.7 copy-done.4
  128.0 1.8 copy.12
  129.7 1.9 copy.11
  131.6 9.3 %shard_map.48 = f32[2,128,448]{2,1,0:T(8,128)} custom-call(s32[3]{0:T(128)} %pad_add_fusion.at_ref, bf16[64,7168]{1,0:T(8,128)(2,1)} %collective-permute-done.10.refs_0_, bf16[64,7168]{1,0:T(8,128)(2,1)} %collective-permute-done.11.refs_1_, bf16[448,7168]{1,0:T(8,128)(2,1)} %bitcast.28, bf16[448,7168]{1,0:T(8,128)(2,1)} %collective-permute-done.7.refs_2_.refs_3_), custom_call_target="tpu_custom_call" | custom-call | flops 1644167168 | bytes 15138816 | tf_op jit(solution)/shard_map/pallas_call | solution.py:48
  140.9 2.8 %copy.13 = f32[8,32,448]{1,2,0:T(8,128)} copy(f32[8,32,448]{2,1,0:T(8,128)} %bitcast.33) | data formatting | bytes 917504 | tf_op jit(solution)/shard_map/reshape | solution.py:154
  143.7 3.1 %pad_maximum_fusion = f32[8,128,448]{1,2,0:T(8,128)S(1)} fusion(f32[8,32,448]{1,2,0:T(8,128)} %copy.13, f32[8,64,448]{1,2,0:T(8,128)S(1)} %copy.12, f32[8,32,448]{1,2,0:T(8,128)} %copy.11), kind=kLoop, calls=%fused_computation | loop fusion | flops 917504 | bytes 3670016 | tf_op jit(solution)/shard_map/concatenate | solution.py:154
  146.8 27.2 %all_to_all.36 = f32[8,128,448]{1,2,0:T(8,128)S(1)} all-to-all(f32[8,128,448]{1,2,0:T(8,128)S(1)} %pad_maximum_fusion), channel_id=1, replica_groups=mesh['y'=4,'z'=8,'core'=2,'x'=4] {'core','x'}, dimensions={0} | all-to-all | bytes 3670016 | tf_op jit(solution)/shard_map/all_to_all | solution.py:66
  174.3 0.3 collective-permute-start.12
  174.5 15.1 %all_gather.13.g_ref = bf16[1024,448]{1,0:T(8,128)(2,1)S(1)} all-gather(bf16[256,448]{1,0:T(8,128)(2,1)S(1)} %bitcast.34), channel_id=1, replica_groups=mesh['y'=4,'z'=8,'core'=2,'x'=4] {'x'}, dimensions={0}, use_global_device_ids=true | all-gather | bytes 1146880 | tf_op jit(solution)/shard_map/all_gather | solution.py:156
  189.6 1.6 copy-done
  191.2 7.2 %shard_map.49 = f32[448,2048]{1,0:T(8,128)} custom-call(s32[3]{0:T(128)S(1)} %copy-done.1, bf16[1024,448]{1,0:T(8,128)(2,1)S(1)} %all_gather.13.g_ref, bf16[8,4,128,256]{3,2,1,0:T(8,128)(2,1)S(1)} %bitcast.24, bf16[8,4,128,256]{3,2,1,0:T(8,128)(2,1)S(1)} %collective-permute-done.12.other_ref), custom_call_target="tpu_custom_call" | custom-call | flops 1879048192 | bytes 12058624 | tf_op jit(solution)/shard_map/pallas_call | solution.py:106
  (29 shorter events, 0.5 us)
Async XLA Ops:
  6.5 62.1 %all-gather.4.cloned.1.call-start = ((), (), s32[]{:S(2)}) async-start(), calls=%async_computation.4 | async-start | bytes 2359296 | tf_op jit(solution)/shard_map/all_gather | solution.py:132
  6.5 11.7 %collective-permute-start = (bf16[16,7168]{1,0:T(8,128)(2,1)}, bf16[16,7168]{1,0:T(8,128)(2,1)S(1)}, u32[]{:S(2)}, u32[]{:S(2)}) collective-permute-start(bf16[16,7168]{1,0:T(8,128)(2,1)} %param.5), channel_id=1, source_target_pairs={{0,8},{8,16},{16,24},{24,32},{32,40},{40,48},{48,56},{56,0},{1,9},... | collective-permute-start | bytes 688136 | tf_op jit(solution)/shard_map/ppermute | solution.py:19
  8.5 10.5 %collective-permute-start.4 = (bf16[16,7168]{1,0:T(8,128)(2,1)}, bf16[16,7168]{1,0:T(8,128)(2,1)S(1)}, u32[]{:S(2)}, u32[]{:S(2)}) collective-permute-start(bf16[16,7168]{1,0:T(8,128)(2,1)} %param.5), channel_id=1, source_target_pairs={{0,56},{8,0},{16,8},{24,16},{32,24},{40,32},{48,40},{56,48},{1,57}... | collective-permute-start | bytes 688136 | tf_op jit(solution)/shard_map/ppermute | solution.py:19
  12.4 40.7 %collective-permute-start.7 = (bf16[448,7168]{1,0:T(8,128)(2,1)}, bf16[448,7168]{1,0:T(8,128)(2,1)}, u32[]{:S(2)}, u32[]{:S(2)}) collective-permute-start(bf16[448,7168]{1,0:T(8,128)(2,1)} %bitcast.25), channel_id=1, source_target_pairs={{0,4},{4,0},{1,5},{5,1},{2,6},{6,2},{3,7},{7,3},{8,12},{12,8},{9,1... | collective-permute-start | bytes 19267592 | tf_op jit(solution)/shard_map/ppermute | solution.py:19
  18.2 8.0 %collective-permute-start.1 = (bf16[16,7168]{1,0:T(8,128)(2,1)S(1)}, bf16[16,7168]{1,0:T(8,128)(2,1)S(1)}, u32[]{:S(2)}, u32[]{:S(2)}) collective-permute-start(bf16[16,7168]{1,0:T(8,128)(2,1)S(1)} %collective-permute-done), channel_id=1, source_target_pairs={{0,8},{8,16},{16,24},{24,32},{32,40},{40,48},{48,56},{56,0},{1,9},... | collective-permute-start | bytes 688136 | tf_op jit(solution)/shard_map/ppermute | solution.py:19
  18.9 10.7 %collective-permute-start.5 = (bf16[16,7168]{1,0:T(8,128)(2,1)S(1)}, bf16[16,7168]{1,0:T(8,128)(2,1)S(1)}, u32[]{:S(2)}, u32[]{:S(2)}) collective-permute-start(bf16[16,7168]{1,0:T(8,128)(2,1)S(1)} %collective-permute-done.4), channel_id=1, source_target_pairs={{0,56},{8,0},{16,8},{24,16},{32,24},{40,32},{48,40},{56,48},{1,57}... | collective-permute-start | bytes 688136 | tf_op jit(solution)/shard_map/ppermute | solution.py:19
  26.2 10.5 %collective-permute-start.2 = (bf16[16,7168]{1,0:T(8,128)(2,1)S(1)}, bf16[16,7168]{1,0:T(8,128)(2,1)S(1)}, u32[]{:S(2)}, u32[]{:S(2)}) collective-permute-start(bf16[16,7168]{1,0:T(8,128)(2,1)S(1)} %collective-permute-done.1), channel_id=1, source_target_pairs={{0,8},{8,16},{16,24},{24,32},{32,40},{40,48},{48,56},{56,0},{1,9},... | collective-permute-start | bytes 688136 | tf_op jit(solution)/shard_map/ppermute | solution.py:19
  29.6 17.4 %collective-permute-start.6 = (bf16[16,7168]{1,0:T(8,128)(2,1)S(1)}, bf16[16,7168]{1,0:T(8,128)(2,1)S(1)}, u32[]{:S(2)}, u32[]{:S(2)}) collective-permute-start(bf16[16,7168]{1,0:T(8,128)(2,1)S(1)} %collective-permute-done.5), channel_id=1, source_target_pairs={{0,56},{8,0},{16,8},{24,16},{32,24},{40,32},{48,40},{56,48},{1,57}... | collective-permute-start | bytes 688136 | tf_op jit(solution)/shard_map/ppermute | solution.py:19
  36.7 9.6 %collective-permute-start.3 = (bf16[16,7168]{1,0:T(8,128)(2,1)S(1)}, bf16[16,7168]{1,0:T(8,128)(2,1)S(1)}, u32[]{:S(2)}, u32[]{:S(2)}) collective-permute-start(bf16[16,7168]{1,0:T(8,128)(2,1)S(1)} %collective-permute-done.2), channel_id=1, source_target_pairs={{0,8},{8,16},{16,24},{24,32},{32,40},{40,48},{48,56},{56,0},{1,9},... | collective-permute-start | bytes 688136 | tf_op jit(solution)/shard_map/ppermute | solution.py:19
  49.2 39.8 %collective-permute-start.8 = (bf16[128,7168]{1,0:T(8,128)(2,1)}, bf16[128,7168]{1,0:T(8,128)(2,1)S(1)}, u32[]{:S(2)}, u32[]{:S(2)}) collective-permute-start(bf16[128,7168]{1,0:T(8,128)(2,1)} %constant_dynamic-update-slice_fusion.refs_0_), channel_id=1, source_target_pairs={{0,64},{64,128},{128,192},{192,0},{1,65},{65,129},{129,193},{193,1... | collective-permute-start | bytes 5505032 | tf_op jit(solution)/shard_map/ppermute | solution.py:19
  50.6 41.3 %collective-permute-start.9 = (bf16[128,7168]{1,0:T(8,128)(2,1)}, bf16[128,7168]{1,0:T(8,128)(2,1)}, u32[]{:S(2)}, u32[]{:S(2)}) collective-permute-start(bf16[128,7168]{1,0:T(8,128)(2,1)} %constant_dynamic-update-slice_fusion.refs_0_), channel_id=1, source_target_pairs={{0,192},{64,0},{128,64},{192,128},{1,193},{65,1},{129,65},{193,129... | collective-permute-start | bytes 5505032 | tf_op jit(solution)/shard_map/ppermute | solution.py:19
  53.1 9.3 %copy-start.5 = (bf16[128,2048]{1,0:T(8,128)(2,1)S(1)}, bf16[128,2048]{1,0:T(8,128)(2,1)}, u32[]{:S(2)}) copy-start(bf16[128,2048]{1,0:T(8,128)(2,1)} %param.6) | copy-start | bytes 1572868
  63.2 18.8 %all-to-all-start = ((bf16[128,8,256]{2,0,1:T(8,128)(2,1)}), bf16[128,8,256]{2,0,1:T(8,128)(2,1)S(1)}, u32[]{:S(2)}, u32[]{:S(2)}) async-start(bf16[128,8,256]{2,0,1:T(8,128)(2,1)} %bitcast.22), calls=%async_computation | async-start | bytes 1048576 | tf_op jit(solution)/shard_map/all_to_all | solution.py:139
  85.2 20.0 %all-to-all-start.1 = ((f32[8,128,256]{2,1,0:T(8,128)}), f32[8,128,256]{2,1,0:T(8,128)S(1)}, u32[]{:S(2)}, u32[]{:S(2)}) async-start(f32[8,128,256]{2,1,0:T(8,128)} %fusion), calls=%async_computation.1 | async-start | bytes 2097152 | tf_op jit(solution)/shard_map/all_to_all | solution.py:142
  88.9 5.1 %copy-start.2 = (bf16[128,7168]{1,0:T(8,128)(2,1)}, bf16[128,7168]{1,0:T(8,128)(2,1)S(1)}, u32[]{:S(2)}) copy-start(bf16[128,7168]{1,0:T(8,128)(2,1)S(1)} %collective-permute-done.8.refs_0_) | copy-start | bytes 5505028
  90.1 34.4 %collective-permute-start.10 = (bf16[64,7168]{1,0:T(8,128)(2,1)}, bf16[64,7168]{1,0:T(8,128)(2,1)}, u32[]{:S(2)}, u32[]{:S(2)}) collective-permute-start(bf16[64,7168]{1,0:T(8,128)(2,1)} %slice.8), channel_id=1, source_target_pairs={{0,64},{64,128},{128,192},{192,0},{1,65},{65,129},{129,193},{193,1... | collective-permute-start | bytes 2752520 | tf_op jit(solution)/shard_map/ppermute | solution.py:19
  94.1 30.4 %collective-permute-start.11 = (bf16[64,7168]{1,0:T(8,128)(2,1)}, bf16[64,7168]{1,0:T(8,128)(2,1)}, u32[]{:S(2)}, u32[]{:S(2)}) collective-permute-start(bf16[64,7168]{1,0:T(8,128)(2,1)} %slice.9), channel_id=1, source_target_pairs={{0,192},{64,0},{128,64},{192,128},{1,193},{65,1},{129,65},{193,129... | collective-permute-start | bytes 2752520 | tf_op jit(solution)/shard_map/ppermute | solution.py:19
  106.0 21.2 %all-to-all-start.2 = ((bf16[4,128,256]{2,1,0:T(8,128)(2,1)}), bf16[4,128,256]{2,1,0:T(8,128)(2,1)S(1)}, u32[]{:S(2)}, u32[]{:S(2)}) async-start(bf16[4,128,256]{2,1,0:T(8,128)(2,1)} %broadcast_in_dim.2), calls=%async_computation.2 | async-start | bytes 524288 | tf_op jit(solution)/shard_map/all_to_all | solution.py:147
  109.4 64.8 %all-gather.6.cloned.1.call-start = ((), (), s32[]{:S(2)}) async-start(), calls=%async_computation.5 | async-start | bytes 2359296 | tf_op jit(solution)/shard_map/all_gather | solution.py:149
  119.5 10.3 %copy-start.3 = (f32[2,128,448]{2,1,0:T(8,128)S(1)}, f32[2,128,448]{2,1,0:T(8,128)}, u32[]{:S(2)}) copy-start(f32[2,128,448]{2,1,0:T(8,128)} %shard_map.46) | copy-start | bytes 1376260
  127.2 0.7 copy-start.4
  174.0 15.6 %copy-start.1 = (s32[3]{0:T(128)S(1)}, s32[3]{0:T(128)}, u32[]{:S(2)}) copy-start(s32[3]{0:T(128)} %pad_add_fusion.at_ref) | copy-start | bytes 40
  174.3 15.3 %collective-permute-start.12 = (bf16[8,4,128,256]{3,2,1,0:T(8,128)(2,1)}, bf16[8,4,128,256]{3,2,1,0:T(8,128)(2,1)S(1)}, u32[]{:S(2)}, u32[]{:S(2)}) collective-permute-start(bf16[8,4,128,256]{3,2,1,0:T(8,128)(2,1)} %bitcast.23), channel_id=1, source_target_pairs={{0,4},{4,0},{1,5},{5,1},{2,6},{6,2},{3,7},{7,3},{8,12},{12,8},{9,1... | collective-permute-start | bytes 6291464 | tf_op jit(solution)/shard_map/ppermute | solution.py:19
  189.6 1.6 copy-start
Sparse Core Ops, SparseCore 0:
  12.5 54.2 all-gather.3
  128.1 35.5 all-gather.5

commit v6 on v5

--- a/solution.py
+++ b/solution.py
@@ -59,6 +59,49 @@
             flops=4 * rows * cols * depth, bytes_accessed=2 * depth * (rows + 2 * cols) + 8 * rows * cols, transcendentals=0
         ),
     )(at, *parts, b, b_other)
+
+
+def last_kernel(at_ref, x0_ref, x1_ref, load_ref, near_ref, b_ref, b_other_ref, o_ref):
+    k, c = pl.program_id(0), at_ref[2]
+    n, m = load_ref.shape[1] // NX, near_ref.shape[1] // NX
+    x = jnp.concatenate([x0_ref[...], x1_ref[...]], axis=0)
+    each = x.shape[0] // NX
+
+    @pl.when(k == 0)
+    def _():
+        for i in range(NC * NX):
+            h, p = i // NX, i % NX
+            o_ref[i, :n, :] = load_ref[h, p * n : (p + 1) * n, :]
+            o_ref[i, n : n + m, :] = near_ref[h, p * m : (p + 1) * m, :]
+            o_ref[i, n + m :, :] = jnp.zeros((each, o_ref.shape[2]), F32)
+
+    for b, h in ((b_ref, c), (b_other_ref, 1 - c)):
+        r = lax.dot_general(x, b[...], (((1,), (1,)), ((), ())), preferred_element_type=F32)
+        for p in range(NX):
+            o_ref[h * NX + p, n + m :, :] += r[p * each : (p + 1) * each, :]
+
+
+def last_product(at, parts, load, near, b, b_other):
+    rows, depth = sum(p.shape[0] for p in parts), parts[0].shape[1]
+    cols, step = b.shape[0], depth // STEPS
+    total = (rows + load.shape[1] + near.shape[1]) // NX
+    spec_b = pl.BlockSpec((cols, step), lambda k, t: (0, k))
+    return pl.pallas_call(
+        last_kernel,
+        grid_spec=pltpu.PrefetchScalarGridSpec(
+            num_scalar_prefetch=1,
+            grid=(STEPS,),
+            in_specs=[pl.BlockSpec((p.shape[0], step), lambda k, t: (0, k)) for p in parts]
+            + [pl.BlockSpec(p.shape, lambda k, t: (0, 0, 0)) for p in (load, near)]
+            + [spec_b, spec_b],
+            out_specs=pl.BlockSpec((NC * NX, total, cols), lambda k, t: (0, 0, 0)),
+        ),
+        out_shape=jax.ShapeDtypeStruct((NC * NX, total, cols), F32),
+        compiler_params=pltpu.CompilerParams(vmem_limit_bytes=54 * 2**20),
+        cost_estimate=pl.CostEstimate(
+            flops=4 * rows * cols * depth, bytes_accessed=2 * depth * (rows + 2 * cols) + 32 * total * cols, transcendentals=0
+        ),
+    )(at, *parts, load, near, b, b_other)
 
 
 def sum_over_x(partial):
@@ -148,10 +191,8 @@
     (along_y,) = after([along_y], product_near, *far)
     own = lax.all_gather(along_y, "z", axis=0)
 
-    cols = product_near.shape[2]
     far = after(far, product_near, along_y)
-    chunks = (product_load, product_near, product(at, far, basis, basis_other))
-    total = sum_over_x(jnp.concatenate([p.reshape(NC * NX, -1, cols) for p in chunks], axis=1))
+    total = sum_over_x(last_product(at, far, product_load, product_near, basis, basis_other))
     (own,) = after([own], total)
     g_all = lax.all_gather(total, "x", axis=0, tiled=True)
     return finish(at, g_all, own, shift(own, "core", 1))

time: 206 us -> 200 us (0.971)
  local copies, waits for them, and re-layouts: 20.4 us -> 15.7 us
  other arithmetic: 3.9 us -> 0.79 us
    pallas_call x0 -> x1, Pallas kernels: none -> 10.5 us  [last_product(): pl.pallas_call(last_kernel, grid_spec=pltpu.PrefetchScalarGridSpec(num_sc...]
    pallas_call x3 -> x2, Pallas kernels: 28.4 us -> 19 us  [product(): pl.pallas_call(product_kernel, grid_spec=pltpu.PrefetchScalarGridSpec(num...]
    reshape x3 -> x0, local copies, waits for them, and re-layouts: 6.45 us -> none  [body(): p.reshape(NC * NX, -1, cols)]
    concatenate x1 -> x0, other arithmetic: 3.1 us -> none  [body(): jnp.concatenate([p.reshape(NC * NX, -1, cols) for p in chunks], axis=1)]
    unnamed x19 -> x17, local copies, waits for them, and re-layouts: 8.18 us -> 8.17 us
  transfers between devices with their start and end apart: 18 -> 18, of which waited for: 10 -> 10; matrix products, arithmetic and copies ran while one was open for 12% -> 9% of each run, Pallas kernels for 14% -> 15%
where the time goes in v6:
time: 200 us; the launch traced here: 199 us
  waiting for transfers between devices  54.3 us (27%)
  blocking collectives  42.2 us (21%)
  Pallas kernels  36.8 us (18%)
  starting transfers between devices  32.7 us (16%)
  local copies, waits for them, and re-layouts  15.7 us (8%)
  between operations  13.5 us (7%)
  matrix products  3.28 us (2%)
    ppermute x13, waiting for transfers between devices, shift(): return lax.ppermute(v, axis, [(i, (i + d) % n) for i in range(n)])  28.3 us
    all_to_all x1, blocking collectives, sum_over_x(): lax.all_to_all(partial.reshape(-1, cols), ('core', 'x'), 0, 0, tiled=True)  27.1 us
    pallas_call x2, Pallas kernels, product(): pl.pallas_call(product_kernel, grid_spec=pltpu.PrefetchScalarGridSpec(num...  19 us
    ppermute x13, starting transfers between devices, shift(): return lax.ppermute(v, axis, [(i, (i + d) % n) for i in range(n)])  19 us
    all_gather x1, blocking collectives, body(): g_all = lax.all_gather(total, 'x', axis=0, tiled=True)  15.1 us
    all_to_all x1, waiting for transfers between devices, body(): basis_acts = lax.all_to_all(act_basis, 'z', 1, 0, tiled=True)  13.3 us
    pallas_call x1, Pallas kernels, last_product(): pl.pallas_call(last_kernel, grid_spec=pltpu.PrefetchScalarGridSpec(num_sc...  10.5 us
    all_to_all x1, waiting for transfers between devices, body(): terms = lax.all_to_all(partial, ('y', 'core'), 0, 0, tiled=True)  10 us
  transfers between devices with their start and end apart: 18, of which 10 were waited for; matrix products, arithmetic and copies ran while one was open for 9% of the time, Pallas kernels for 15%

profile of v6, /device:TPU:2, one launch (start us, length us, event | category | flops | bytes accessed | tf_op | source)
XLA Modules:
  0.0 199.3 jit_solution(17809363350844804320)
XLA Ops:
  6.5 1.9 collective-permute-start
  8.5 3.9 %collective-permute-start.4 = (bf16[16,7168]{1,0:T(8,128)(2,1)}, bf16[16,7168]{1,0:T(8,128)(2,1)S(1)}, u32[]{:S(2)}, u32[]{:S(2)}) collective-permute-start(bf16[16,7168]{1,0:T(8,128)(2,1)} %param.5), channel_id=1, source_target_pairs={{0,56},{8,0},{16,8},{24,16},{32,24},{40,32},{48,40},{56,48},{1,57}... | collective-permute-start | bytes 688136 | tf_op jit(solution)/shard_map/ppermute | solution.py:19
  12.4 1.6 constant_dynamic-update-slice_fusion.7
  14.1 4.1 %collective-permute-done = bf16[16,7168]{1,0:T(8,128)(2,1)S(1)} collective-permute-done((bf16[16,7168]{1,0:T(8,128)(2,1)}, bf16[16,7168]{1,0:T(8,128)(2,1)S(1)}, u32[]{:S(2)}, u32[]{:S(2)}) %collective-permute-start) | collective-permute-done | bytes 229408 | tf_op jit(solution)/shard_map/ppermute | solution.py:19
  18.2 0.7 constant_dynamic-update-slice_fusion.6
  18.9 3.2 %collective-permute-start.5 = (bf16[16,7168]{1,0:T(8,128)(2,1)S(1)}, bf16[16,7168]{1,0:T(8,128)(2,1)S(1)}, u32[]{:S(2)}, u32[]{:S(2)}) collective-permute-start(bf16[16,7168]{1,0:T(8,128)(2,1)S(1)} %collective-permute-done.4), channel_id=1, source_target_pairs={{0,56},{8,0},{16,8},{24,16},{32,24},{40,32},{48,40},{56,48},{1,57}... | collective-permute-start | bytes 688136 | tf_op jit(solution)/shard_map/ppermute | solution.py:19
  22.1 4.1 %collective-permute-done.1 = bf16[16,7168]{1,0:T(8,128)(2,1)S(1)} collective-permute-done((bf16[16,7168]{1,0:T(8,128)(2,1)S(1)}, bf16[16,7168]{1,0:T(8,128)(2,1)S(1)}, u32[]{:S(2)}, u32[]{:S(2)}) %collective-permute-start.1) | collective-permute-done | bytes 229408 | tf_op jit(solution)/shard_map/ppermute | solution.py:19
  26.2 0.7 constant_dynamic-update-slice_fusion.5
  26.9 2.7 %collective-permute-done.5 = bf16[16,7168]{1,0:T(8,128)(2,1)S(1)} collective-permute-done((bf16[16,7168]{1,0:T(8,128)(2,1)S(1)}, bf16[16,7168]{1,0:T(8,128)(2,1)S(1)}, u32[]{:S(2)}, u32[]{:S(2)}) %collective-permute-start.5) | collective-permute-done | bytes 229408 | tf_op jit(solution)/shard_map/ppermute | solution.py:19
  29.6 3.7 %collective-permute-start.6 = (bf16[16,7168]{1,0:T(8,128)(2,1)S(1)}, bf16[16,7168]{1,0:T(8,128)(2,1)S(1)}, u32[]{:S(2)}, u32[]{:S(2)}) collective-permute-start(bf16[16,7168]{1,0:T(8,128)(2,1)S(1)} %collective-permute-done.5), channel_id=1, source_target_pairs={{0,56},{8,0},{16,8},{24,16},{32,24},{40,32},{48,40},{56,48},{1,57}... | collective-permute-start | bytes 688136 | tf_op jit(solution)/shard_map/ppermute | solution.py:19
  33.3 3.4 %collective-permute-done.2 = bf16[16,7168]{1,0:T(8,128)(2,1)S(1)} collective-permute-done((bf16[16,7168]{1,0:T(8,128)(2,1)S(1)}, bf16[16,7168]{1,0:T(8,128)(2,1)S(1)}, u32[]{:S(2)}, u32[]{:S(2)}) %collective-permute-start.2) | collective-permute-done | bytes 229408 | tf_op jit(solution)/shard_map/ppermute | solution.py:19
  36.8 0.7 constant_dynamic-update-slice_fusion.4
  37.5 8.9 %collective-permute-done.3 = bf16[16,7168]{1,0:T(8,128)(2,1)S(1)} collective-permute-done((bf16[16,7168]{1,0:T(8,128)(2,1)S(1)}, bf16[16,7168]{1,0:T(8,128)(2,1)S(1)}, u32[]{:S(2)}, u32[]{:S(2)}) %collective-permute-start.3) | collective-permute-done | bytes 229408 | tf_op jit(solution)/shard_map/ppermute | solution.py:19
  46.4 0.7 constant_dynamic-update-slice_fusion.3
  47.1 0.7 constant_dynamic-update-slice_fusion.2
  47.8 0.7 constant_dynamic-update-slice_fusion.1
  48.5 0.7 constant_dynamic-update-slice_fusion.refs_0_
  49.2 2.7 %collective-permute-start.9 = (bf16[128,7168]{1,0:T(8,128)(2,1)}, bf16[128,7168]{1,0:T(8,128)(2,1)S(1)}, u32[]{:S(2)}, u32[]{:S(2)}) collective-permute-start(bf16[128,7168]{1,0:T(8,128)(2,1)} %constant_dynamic-update-slice_fusion.refs_0_), channel_id=1, source_target_pairs={{0,192},{64,0},{128,64},{192,128},{1,193},{65,1},{129,65},{193,129... | collective-permute-start | bytes 5505032 | tf_op jit(solution)/shard_map/ppermute | solution.py:19
  51.9 0.6 pad_add_fusion.at_ref
  52.5 9.2 %shard_map.47.load_ref = f32[2,128,448]{2,1,0:T(8,128)} custom-call(s32[3]{0:T(128)} %pad_add_fusion.at_ref, bf16[128,7168]{1,0:T(8,128)(2,1)} %constant_dynamic-update-slice_fusion.refs_0_, bf16[448,7168]{1,0:T(8,128)(2,1)} %bitcast.23, bf16[448,7168]{1,0:T(8,128)(2,1)} %collective-permute-done.11.refs_3_.refs_2_.b_other_ref), custom_call_target="tpu_custom_call" | custom-call | flops 1644167168 | bytes 15138816 | tf_op jit(solution)/shard_map/pallas_call | solution.py:48
  61.7 0.8 copy.13
  62.6 5.6 %all-to-all-start = ((bf16[128,8,256]{2,0,1:T(8,128)(2,1)}), bf16[128,8,256]{2,0,1:T(8,128)(2,1)S(1)}, u32[]{:S(2)}, u32[]{:S(2)}) async-start(bf16[128,8,256]{2,0,1:T(8,128)(2,1)} %bitcast.19), calls=%async_computation | async-start | bytes 1048576 | tf_op jit(solution)/shard_map/all_to_all | solution.py:182
  68.1 13.3 %all-to-all-done = bf16[128,8,256]{2,0,1:T(8,128)(2,1)S(1)} async-done(((bf16[128,8,256]{2,0,1:T(8,128)(2,1)}), bf16[128,8,256]{2,0,1:T(8,128)(2,1)S(1)}, u32[]{:S(2)}, u32[]{:S(2)}) %all-to-all-start) | async-done | bytes 524320 | tf_op jit(solution)/shard_map/all_to_all | solution.py:182
  81.4 3.3 %fusion = f32[8,128,256]{2,1,0:T(8,128)} fusion(bf16[8,128,1024]{2,1,0:T(8,128)(2,1)} %bitcast.26, bf16[1024,256,1]{1,0,2:T(8,128)(2,1)S(1)} %bitcast.27), kind=kOutput, calls=%fused_computation.11 | convolution fusion | flops 536870912 | bytes 3670016 | tf_op jit(solution)/shard_map/dot_general | solution.py:184
  84.7 4.5 %all-to-all-start.1 = ((f32[8,128,256]{2,1,0:T(8,128)}), f32[8,128,256]{2,1,0:T(8,128)S(1)}, u32[]{:S(2)}, u32[]{:S(2)}) async-start(f32[8,128,256]{2,1,0:T(8,128)} %fusion), calls=%async_computation.1 | async-start | bytes 2097152 | tf_op jit(solution)/shard_map/all_to_all | solution.py:185
  89.2 1.1 slice.9
  90.3 3.2 %collective-permute-start.10 = (bf16[64,7168]{1,0:T(8,128)(2,1)}, bf16[64,7168]{1,0:T(8,128)(2,1)}, u32[]{:S(2)}, u32[]{:S(2)}) collective-permute-start(bf16[64,7168]{1,0:T(8,128)(2,1)} %slice.9), channel_id=1, source_target_pairs={{0,192},{64,0},{128,64},{192,128},{1,193},{65,1},{129,65},{193,129... | collective-permute-start | bytes 2752520 | tf_op jit(solution)/shard_map/ppermute | solution.py:19
  93.5 2.2 %slice.8 = bf16[64,7168]{1,0:T(8,128)(2,1)} slice(bf16[128,7168]{1,0:T(8,128)(2,1)} %collective-permute-done.7.refs_0_), slice={[0:64], [0:7168]} | slice | bytes 1835008 | tf_op jit(solution)/shard_map/slice | solution.py:188
  95.7 10.0 %all-to-all-done.1 = f32[8,128,256]{2,1,0:T(8,128)S(1)} async-done(((f32[8,128,256]{2,1,0:T(8,128)}), f32[8,128,256]{2,1,0:T(8,128)S(1)}, u32[]{:S(2)}, u32[]{:S(2)}) %all-to-all-start.1) | async-done | bytes 1048608 | tf_op jit(solution)/shard_map/all_to_all | solution.py:185
  105.7 0.1 reduce_sum.18
  105.8 0.7 broadcast_in_dim.2
  106.5 3.4 %all-to-all-start.2 = ((bf16[4,128,256]{2,1,0:T(8,128)(2,1)}), bf16[4,128,256]{2,1,0:T(8,128)(2,1)S(1)}, u32[]{:S(2)}, u32[]{:S(2)}) async-start(bf16[4,128,256]{2,1,0:T(8,128)(2,1)} %broadcast_in_dim.2), calls=%async_computation.2 | async-start | bytes 524288 | tf_op jit(solution)/shard_map/all_to_all | solution.py:190
  109.9 0.2 all-gather.6.cloned.1.call-start
  110.1 9.8 %shard_map.46.near_ref = f32[2,256,448]{2,1,0:T(8,128)} custom-call(s32[3]{0:T(128)} %pad_add_fusion.at_ref, bf16[128,7168]{1,0:T(8,128)(2,1)} %collective-permute-done.7.refs_0_, bf16[128,7168]{1,0:T(8,128)(2,1)} %copy-done.2, bf16[448,7168]{1,0:T(8,128)(2,1)} %bitcast.24, bf16[448,7168]{1,0:T(8,128)(2,1)} %collective-permute-done.11.refs_3_.refs_2_.b_other_ref), custom_call_target="tpu_custom_call" | custom-call | flops 3288334336 | bytes 17432576 | tf_op jit(solution)/shard_map/pallas_call | solution.py:48
  120.0 4.0 %collective-permute-done.10.x1_ref = bf16[64,7168]{1,0:T(8,128)(2,1)} collective-permute-done((bf16[64,7168]{1,0:T(8,128)(2,1)}, bf16[64,7168]{1,0:T(8,128)(2,1)}, u32[]{:S(2)}, u32[]{:S(2)}) %collective-permute-start.10) | collective-permute-done | bytes 917536 | tf_op jit(solution)/shard_map/ppermute | solution.py:19
  123.9 1.0 collective-permute-done.8.x0_ref
  125.0 2.7 %all-to-all-done.2 = bf16[4,128,256]{2,1,0:T(8,128)(2,1)S(1)} async-done(((bf16[4,128,256]{2,1,0:T(8,128)(2,1)}), bf16[4,128,256]{2,1,0:T(8,128)(2,1)S(1)}, u32[]{:S(2)}, u32[]{:S(2)}) %all-to-all-start.2) | async-done | bytes 262176 | tf_op jit(solution)/shard_map/all_to_all | solution.py:190
  127.7 0.7 copy-done.3
  128.4 10.5 %shard_map.48 = f32[8,128,448]{2,1,0:T(8,128)} custom-call(s32[3]{0:T(128)} %pad_add_fusion.at_ref, bf16[64,7168]{1,0:T(8,128)(2,1)} %collective-permute-done.8.x0_ref, bf16[64,7168]{1,0:T(8,128)(2,1)} %collective-permute-done.10.x1_ref, f32[2,128,448]{2,1,0:T(8,128)} %shard_map.47.load_ref, f32[2,256,448]{2,1,0:T(8,128)} %shard_map.46.near_ref, ...), custom_call_target="tpu_custom_call" | custom-call | flops 1644167168 | bytes 16515072 | tf_op jit(solution)/shard_map/pallas_call | solution.py:89
  138.9 1.9 copy.9
  140.8 27.1 %all_to_all.36 = f32[8,128,448]{1,2,0:T(8,128)S(1)} all-to-all(f32[8,128,448]{1,2,0:T(8,128)S(1)} %copy.9), channel_id=1, replica_groups=mesh['y'=4,'z'=8,'core'=2,'x'=4] {'core','x'}, dimensions={0} | all-to-all | bytes 3670016 | tf_op jit(solution)/shard_map/all_to_all | solution.py:109
  168.0 0.1 bitcast_reduce_fusion
  168.1 0.1 copy.10
  168.2 0.0 all-gather.6.cloned.1.call-done
  168.2 0.3 collective-permute-start.12
  168.5 15.1 %all_gather.13.g_ref = bf16[1024,448]{1,0:T(8,128)(2,1)S(1)} all-gather(bf16[256,448]{1,0:T(8,128)(2,1)S(1)} %bitcast.28), channel_id=1, replica_groups=mesh['y'=4,'z'=8,'core'=2,'x'=4] {'x'}, dimensions={0}, use_global_device_ids=true | all-gather | bytes 1146880 | tf_op jit(solution)/shard_map/all_gather | solution.py:197
  183.6 1.6 copy-done
  185.2 7.2 %shard_map.49 = f32[448,2048]{1,0:T(8,128)} custom-call(s32[3]{0:T(128)S(1)} %copy-done.1, bf16[1024,448]{1,0:T(8,128)(2,1)S(1)} %all_gather.13.g_ref, bf16[8,4,128,256]{3,2,1,0:T(8,128)(2,1)S(1)} %bitcast.21, bf16[8,4,128,256]{3,2,1,0:T(8,128)(2,1)S(1)} %collective-permute-done.12.other_ref), custom_call_target="tpu_custom_call" | custom-call | flops 1879048192 | bytes 12058624 | tf_op jit(solution)/shard_map/pallas_call | solution.py:149
  (24 shorter events, 0.1 us)
Async XLA Ops:
  6.5 61.6 %all-gather.4.cloned.1.call-start = ((), (), s32[]{:S(2)}) async-start(), calls=%async_computation.4 | async-start | bytes 2359296 | tf_op jit(solution)/shard_map/all_gather | solution.py:175
  6.5 11.7 %collective-permute-start = (bf16[16,7168]{1,0:T(8,128)(2,1)}, bf16[16,7168]{1,0:T(8,128)(2,1)S(1)}, u32[]{:S(2)}, u32[]{:S(2)}) collective-permute-start(bf16[16,7168]{1,0:T(8,128)(2,1)} %param.5), channel_id=1, source_target_pairs={{0,8},{8,16},{16,24},{24,32},{32,40},{40,48},{48,56},{56,0},{1,9},... | collective-permute-start | bytes 688136 | tf_op jit(solution)/shard_map/ppermute | solution.py:19
  8.5 10.5 %collective-permute-start.4 = (bf16[16,7168]{1,0:T(8,128)(2,1)}, bf16[16,7168]{1,0:T(8,128)(2,1)S(1)}, u32[]{:S(2)}, u32[]{:S(2)}) collective-permute-start(bf16[16,7168]{1,0:T(8,128)(2,1)} %param.5), channel_id=1, source_target_pairs={{0,56},{8,0},{16,8},{24,16},{32,24},{40,32},{48,40},{56,48},{1,57}... | collective-permute-start | bytes 688136 | tf_op jit(solution)/shard_map/ppermute | solution.py:19
  12.4 40.1 %collective-permute-start.11 = (bf16[448,7168]{1,0:T(8,128)(2,1)}, bf16[448,7168]{1,0:T(8,128)(2,1)}, u32[]{:S(2)}, u32[]{:S(2)}) collective-permute-start(bf16[448,7168]{1,0:T(8,128)(2,1)} %bitcast.22), channel_id=1, source_target_pairs={{0,4},{4,0},{1,5},{5,1},{2,6},{6,2},{3,7},{7,3},{8,12},{12,8},{9,1... | collective-permute-start | bytes 19267592 | tf_op jit(solution)/shard_map/ppermute | solution.py:19
  18.2 8.0 %collective-permute-start.1 = (bf16[16,7168]{1,0:T(8,128)(2,1)S(1)}, bf16[16,7168]{1,0:T(8,128)(2,1)S(1)}, u32[]{:S(2)}, u32[]{:S(2)}) collective-permute-start(bf16[16,7168]{1,0:T(8,128)(2,1)S(1)} %collective-permute-done), channel_id=1, source_target_pairs={{0,8},{8,16},{16,24},{24,32},{32,40},{40,48},{48,56},{56,0},{1,9},... | collective-permute-start | bytes 688136 | tf_op jit(solution)/shard_map/ppermute | solution.py:19
  18.9 10.7 %collective-permute-start.5 = (bf16[16,7168]{1,0:T(8,128)(2,1)S(1)}, bf16[16,7168]{1,0:T(8,128)(2,1)S(1)}, u32[]{:S(2)}, u32[]{:S(2)}) collective-permute-start(bf16[16,7168]{1,0:T(8,128)(2,1)S(1)} %collective-permute-done.4), channel_id=1, source_target_pairs={{0,56},{8,0},{16,8},{24,16},{32,24},{40,32},{48,40},{56,48},{1,57}... | collective-permute-start | bytes 688136 | tf_op jit(solution)/shard_map/ppermute | solution.py:19
  26.2 10.5 %collective-permute-start.2 = (bf16[16,7168]{1,0:T(8,128)(2,1)S(1)}, bf16[16,7168]{1,0:T(8,128)(2,1)S(1)}, u32[]{:S(2)}, u32[]{:S(2)}) collective-permute-start(bf16[16,7168]{1,0:T(8,128)(2,1)S(1)} %collective-permute-done.1), channel_id=1, source_target_pairs={{0,8},{8,16},{16,24},{24,32},{32,40},{40,48},{48,56},{56,0},{1,9},... | collective-permute-start | bytes 688136 | tf_op jit(solution)/shard_map/ppermute | solution.py:19
  29.6 17.4 %collective-permute-start.6 = (bf16[16,7168]{1,0:T(8,128)(2,1)S(1)}, bf16[16,7168]{1,0:T(8,128)(2,1)S(1)}, u32[]{:S(2)}, u32[]{:S(2)}) collective-permute-start(bf16[16,7168]{1,0:T(8,128)(2,1)S(1)} %collective-permute-done.5), channel_id=1, source_target_pairs={{0,56},{8,0},{16,8},{24,16},{32,24},{40,32},{48,40},{56,48},{1,57}... | collective-permute-start | bytes 688136 | tf_op jit(solution)/shard_map/ppermute | solution.py:19
  36.7 9.6 %collective-permute-start.3 = (bf16[16,7168]{1,0:T(8,128)(2,1)S(1)}, bf16[16,7168]{1,0:T(8,128)(2,1)S(1)}, u32[]{:S(2)}, u32[]{:S(2)}) collective-permute-start(bf16[16,7168]{1,0:T(8,128)(2,1)S(1)} %collective-permute-done.2), channel_id=1, source_target_pairs={{0,8},{8,16},{16,24},{24,32},{32,40},{40,48},{48,56},{56,0},{1,9},... | collective-permute-start | bytes 688136 | tf_op jit(solution)/shard_map/ppermute | solution.py:19
  49.2 40.0 %collective-permute-start.9 = (bf16[128,7168]{1,0:T(8,128)(2,1)}, bf16[128,7168]{1,0:T(8,128)(2,1)S(1)}, u32[]{:S(2)}, u32[]{:S(2)}) collective-permute-start(bf16[128,7168]{1,0:T(8,128)(2,1)} %constant_dynamic-update-slice_fusion.refs_0_), channel_id=1, source_target_pairs={{0,192},{64,0},{128,64},{192,128},{1,193},{65,1},{129,65},{193,129... | collective-permute-start | bytes 5505032 | tf_op jit(solution)/shard_map/ppermute | solution.py:19
  51.9 41.6 %collective-permute-start.7 = (bf16[128,7168]{1,0:T(8,128)(2,1)}, bf16[128,7168]{1,0:T(8,128)(2,1)}, u32[]{:S(2)}, u32[]{:S(2)}) collective-permute-start(bf16[128,7168]{1,0:T(8,128)(2,1)} %constant_dynamic-update-slice_fusion.refs_0_), channel_id=1, source_target_pairs={{0,64},{64,128},{128,192},{192,0},{1,65},{65,129},{129,193},{193,1... | collective-permute-start | bytes 5505032 | tf_op jit(solution)/shard_map/ppermute | solution.py:19
  52.5 9.2 %copy-start.4 = (bf16[128,2048]{1,0:T(8,128)(2,1)S(1)}, bf16[128,2048]{1,0:T(8,128)(2,1)}, u32[]{:S(2)}) copy-start(bf16[128,2048]{1,0:T(8,128)(2,1)} %param.6) | copy-start | bytes 1572868
  62.6 18.8 %all-to-all-start = ((bf16[128,8,256]{2,0,1:T(8,128)(2,1)}), bf16[128,8,256]{2,0,1:T(8,128)(2,1)S(1)}, u32[]{:S(2)}, u32[]{:S(2)}) async-start(bf16[128,8,256]{2,0,1:T(8,128)(2,1)} %bitcast.19), calls=%async_computation | async-start | bytes 1048576 | tf_op jit(solution)/shard_map/all_to_all | solution.py:182
  84.7 21.0 %all-to-all-start.1 = ((f32[8,128,256]{2,1,0:T(8,128)}), f32[8,128,256]{2,1,0:T(8,128)S(1)}, u32[]{:S(2)}, u32[]{:S(2)}) async-start(f32[8,128,256]{2,1,0:T(8,128)} %fusion), calls=%async_computation.1 | async-start | bytes 2097152 | tf_op jit(solution)/shard_map/all_to_all | solution.py:185
  89.2 6.5 %copy-start.2 = (bf16[128,7168]{1,0:T(8,128)(2,1)}, bf16[128,7168]{1,0:T(8,128)(2,1)S(1)}, u32[]{:S(2)}) copy-start(bf16[128,7168]{1,0:T(8,128)(2,1)S(1)} %collective-permute-done.9.refs_1_) | copy-start | bytes 5505028
  90.3 33.7 %collective-permute-start.10 = (bf16[64,7168]{1,0:T(8,128)(2,1)}, bf16[64,7168]{1,0:T(8,128)(2,1)}, u32[]{:S(2)}, u32[]{:S(2)}) collective-permute-start(bf16[64,7168]{1,0:T(8,128)(2,1)} %slice.9), channel_id=1, source_target_pairs={{0,192},{64,0},{128,64},{192,128},{1,193},{65,1},{129,65},{193,129... | collective-permute-start | bytes 2752520 | tf_op jit(solution)/shard_map/ppermute | solution.py:19
  95.7 29.3 %collective-permute-start.8 = (bf16[64,7168]{1,0:T(8,128)(2,1)}, bf16[64,7168]{1,0:T(8,128)(2,1)}, u32[]{:S(2)}, u32[]{:S(2)}) collective-permute-start(bf16[64,7168]{1,0:T(8,128)(2,1)} %slice.8), channel_id=1, source_target_pairs={{0,64},{64,128},{128,192},{192,0},{1,65},{65,129},{129,193},{193,1... | collective-permute-start | bytes 2752520 | tf_op jit(solution)/shard_map/ppermute | solution.py:19
  106.5 21.2 %all-to-all-start.2 = ((bf16[4,128,256]{2,1,0:T(8,128)(2,1)}), bf16[4,128,256]{2,1,0:T(8,128)(2,1)S(1)}, u32[]{:S(2)}, u32[]{:S(2)}) async-start(bf16[4,128,256]{2,1,0:T(8,128)(2,1)} %broadcast_in_dim.2), calls=%async_computation.2 | async-start | bytes 524288 | tf_op jit(solution)/shard_map/all_to_all | solution.py:190
  109.9 58.3 %all-gather.6.cloned.1.call-start = ((), (), s32[]{:S(2)}) async-start(), calls=%async_computation.5 | async-start | bytes 2359296 | tf_op jit(solution)/shard_map/all_gather | solution.py:192
  127.7 0.7 copy-start.3
  168.0 15.6 %copy-start.1 = (s32[3]{0:T(128)S(1)}, s32[3]{0:T(128)}, u32[]{:S(2)}) copy-start(s32[3]{0:T(128)} %pad_add_fusion.at_ref) | copy-start | bytes 40
  168.2 15.3 %collective-permute-start.12 = (bf16[8,4,128,256]{3,2,1,0:T(8,128)(2,1)}, bf16[8,4,128,256]{3,2,1,0:T(8,128)(2,1)S(1)}, u32[]{:S(2)}, u32[]{:S(2)}) collective-permute-start(bf16[8,4,128,256]{3,2,1,0:T(8,128)(2,1)} %bitcast.20), channel_id=1, source_target_pairs={{0,4},{4,0},{1,5},{5,1},{2,6},{6,2},{3,7},{7,3},{8,12},{12,8},{9,1... | collective-permute-start | bytes 6291464 | tf_op jit(solution)/shard_map/ppermute | solution.py:19
  183.6 1.6 copy-start
Sparse Core Ops, SparseCore 0:
  12.5 55.1 all-gather.3
  128.5 35.3 all-gather.5
